TPU v7x, 256 devices: a whole 4x4x8 slice. The times are simulated.
256 devices in a mesh: lat: 8 (over z_hi, x), lon: 16 (over z_lo, y), grp: 2 (over core).
Axes of the slice: x: 4, y: 4, z: 8 (z_hi: 2, z_lo: 4; z = z_hi * 4 + z_lo), core: 2. Of those that a mesh axis runs over, the one named last changes fastest.
Arguments:
- teacher_in: bfloat16 [2, 192, 192, 512], P('grp', 'lat', 'lon'), may hold values from -6 to 6
- student_in: bfloat16 [2, 192, 192, 256], P('grp', 'lat', 'lon'), may hold values from -6 to 6
- regions: int32 [2, 192, 192], P(None, 'lat', 'lon'), may hold values from 0 to 2
- t_qkv: bfloat16 [2, 512, 1536], replicated, may hold values from -0.25 to 0.25
- t_out: bfloat16 [2, 512, 512], replicated, may hold values from -0.25 to 0.25
- s_qkv: bfloat16 [2, 256, 768], replicated, may hold values from -0.375 to 0.375
- s_out: bfloat16 [2, 256, 256], replicated, may hold values from -0.375 to 0.375
- s_proj: bfloat16 [256, 512], replicated, may hold values from -0.375 to 0.375
Outputs:
- teacher_out: bfloat16 [2, 192, 192, 512], P('grp', 'lat', 'lon')
- student_grad: float32 [2, 192, 192, 256], P('grp', 'lat', 'lon')
All inputs are finite; a program needn't handle non-finite values.
Results may differ from a plain program's by a relative error of at most 0.02.
Values may be sent and summed in bfloat16 or wider, within the bound.
No kernel may reach another device: no remote copies, remote signals or barrier semaphores. Data moves between devices by JAX's collectives and lax.ppermute only.
A program may use at most 128 MiB of HBM per device.

v0:
```python
import functools

import jax
import jax.numpy as jnp
import ml_dtypes
import numpy as np
from jax import lax
from jax.experimental import pallas as pl
from jax.experimental.pallas import tpu as pltpu
from jax.sharding import PartitionSpec as P

HEADS_T = 8
HEADS_S = 4
EPS = 1e-06
LOG2E = 1.4426950408889634
SCALE = 10.0 * LOG2E
BF = jnp.bfloat16
F32 = jnp.float32

ROWS, COLS = 24, 12
WIN = 80
NA = 4 * WIN
NAT = ROWS * 16
QUAD = 256

PARTS = (
    ("nw", (0, 6), (0, 3), 32),
    ("n", (0, 6), (3, 9), 48),
    ("ne", (0, 6), (9, 12), 32),
    ("e", (6, 18), (9, 12), 48),
    ("se", (18, 24), (9, 12), 32),
    ("s", (18, 24), (3, 9), 48),
    ("sw", (18, 24), (0, 3), 32),
    ("w", (6, 18), (0, 3), 48),
    ("c", (6, 18), (3, 9), 80),
)
AT = {}
NG = 0
for _name, _r, _c, _kept in PARTS:
    AT[_name] = (NG, _kept)
    NG += _kept


def _a_slot(r, c):
    return (2 * (r // 12) + c // 6) * WIN + (r % 12) * 6 + c % 6


def _tables():
    to_a = np.zeros((NA, NAT), ml_dtypes.bfloat16)
    a_row = np.zeros((NA, ROWS), ml_dtypes.bfloat16)
    a_col = np.zeros((NA, COLS), ml_dtypes.bfloat16)
    for r in range(ROWS):
        for c in range(COLS):
            slot = _a_slot(r, c)
            to_a[slot, r * 16 + c] = 1
            a_row[slot, r] = 1
            a_col[slot, c] = 1
    a_to_g = np.zeros((NG, NA), ml_dtypes.bfloat16)
    for name, (r0, r1), (c0, c1), _ in PARTS:
        spot = AT[name][0]
        for r in range(r0, r1):
            for c in range(c0, c1):
                a_to_g[spot, _a_slot(r, c)] = 1
                spot += 1
    return to_a, a_row, a_col, a_to_g


TO_A, A_ROW, A_COL, A_TO_G = _tables()
FROM_A = np.ascontiguousarray(TO_A.T)
G_TO_A = np.ascontiguousarray(A_TO_G.T)


def dot(a, b):
    return jnp.dot(a, b, preferred_element_type=F32)


def dot_nt(a, b):
    return lax.dot_general(a, b, (((1,), (1,)), ((), ())), preferred_element_type=F32)


def dot_tn(a, b):
    return lax.dot_general(a, b, (((0,), (0,)), ((), ())), preferred_element_type=F32)


def head_lanes(rows, h):
    lane = lax.broadcasted_iota(jnp.int32, (rows, QUAD), 1)
    return jnp.where((lane >> 6) == h, 1.0, 0.0).astype(BF)


def head_blocks():
    row = lax.broadcasted_iota(jnp.int32, (QUAD, QUAD), 0)
    lane = lax.broadcasted_iota(jnp.int32, (QUAD, QUAD), 1)
    return jnp.where((row >> 6) == (lane >> 6), 1.0, 0.0).astype(BF)


def stack_heads(x):
    return jnp.concatenate([x * head_lanes(1, h) for h in range(4)], axis=0)


def stack_values(v):
    rows = v.shape[0]
    ones = jnp.concatenate([head_lanes(rows, h) for h in range(4)], axis=0)
    return jnp.concatenate([stack_heads(v), ones], axis=1)


def unstack_heads(x):
    n = x.shape[0] // 4
    lane = lax.broadcasted_iota(jnp.int32, (1, QUAD), 1) >> 6
    total = x[:n]
    for h in range(1, 4):
        total = jnp.where(lane == h, x[h * n : (h + 1) * n], total)
    return total


def head_sums(x, blocks):
    groups = [dot(x[:, i : i + QUAD].astype(BF), blocks) for i in range(0, x.shape[1], QUAD)]
    return groups[0] if len(groups) == 1 else jnp.concatenate(groups, axis=1)


def unit(x, blocks):
    scale = lax.rsqrt(head_sums(x * x, blocks) + EPS)
    return x * scale, scale


def id_mask(id_query, id_keys):
    keys = jnp.concatenate([id_keys] * 4, axis=0)
    row = dot_nt(jnp.full((8, 128), 1.0 / 128, BF), keys)[0:1]
    return id_query.astype(F32)[:, 0:1] == row


def attend(q, k, v, mask):
    scores = dot_nt(q, stack_heads(k))
    e = jnp.where(mask, jnp.exp2(scores), 0.0).astype(BF)
    both = dot(e, stack_values(v))
    return both[:, :QUAD], both[:, QUAD:], e


def to_window_order(x_ref, pad_ref, to_a):
    pad_ref[...] = jnp.zeros_like(pad_ref)
    pad_ref[:, 0:COLS, :] = x_ref[0]
    natural = pad_ref[...].reshape(NAT, x_ref.shape[3])
    return dot(to_a, natural).astype(BF)


def window_ids(reg, a_row, a_col):
    table = (reg + 1).astype(F32).astype(BF)
    picked = (dot(a_row, table) * a_col.astype(F32)).astype(BF)
    return dot(picked, jnp.ones((COLS, 128), BF)).astype(BF)


def residual(x, att, w):
    y = dot(att, w)
    r = lax.rsqrt(jnp.mean(y * y, axis=1, keepdims=True) + EPS)
    n = y * r
    return (x.astype(F32) + n).astype(BF), n, r


SAVE = 9 * QUAD + 384


def student_layer(x, w_qkv, w_out, ids, save_ref):
    blocks = head_blocks()
    qkv = dot(x, w_qkv)
    q, sq = unit(qkv[:, :QUAD], blocks)
    k, sk = unit(qkv[:, QUAD : 2 * QUAD], blocks)
    q = (q * SCALE).astype(BF)
    k = k.astype(BF)
    v = qkv[:, 2 * QUAD :].astype(BF)
    atts = []
    for w in range(4):
        rows = slice(w * WIN, (w + 1) * WIN)
        mask = id_mask(ids[rows], ids[rows])
        num, den, e = attend(q[rows], k[rows], v[rows], mask)
        z = 1.0 / den
        att = num * z
        save_ref[rows, 4 * QUAD : 5 * QUAD] = z.astype(BF)
        save_ref[rows, 9 * QUAD : 9 * QUAD + 4 * WIN] = e
        atts.append(att.astype(BF))
    att = jnp.concatenate(atts, axis=0)
    h, n, r = residual(x, att, w_out)
    for i, part in ((0, q), (1, k), (2, v), (3, att), (5, sq), (6, sk), (7, n)):
        save_ref[:, i * QUAD : (i + 1) * QUAD] = part.astype(BF)
    save_ref[:, 8 * QUAD : 9 * QUAD] = jnp.broadcast_to(r, (NA, QUAD)).astype(BF)
    return h


def fetch(*pairs):
    copies = [pltpu.make_async_copy(*pair) for pair in pairs]
    for copy in copies:
        copy.start()
    return copies


def student_first(
    x_ref, reg_ref, to_a, a_row, a_col, s_qkv, s_out, h_ref, id_ref, save_ref,
    pad_ref, wqkv, wout, sems,
):
    weights = fetch((s_qkv.at[0], wqkv, sems.at[0]), (s_out.at[0], wout, sems.at[1]))
    level = lax.axis_index("grp")
    x = to_window_order(x_ref, pad_ref, to_a[...])
    ids = window_ids(reg_ref[level], a_row[...], a_col[...])
    id_ref[...] = ids
    for copy in weights:
        copy.wait()
    h_ref[...] = student_layer(x, wqkv[...], wout[...], ids, save_ref)


def student_second(
    h_ref, id_ref, s_qkv, s_out, proj, after_ref, g_ref, save_ref, wqkv, wout, sems
):
    weights = fetch((s_qkv.at[1], wqkv, sems.at[0]), (s_out.at[1], wout, sems.at[1]))
    for copy in weights:
        copy.wait()
    h = student_layer(h_ref[...], wqkv[...], wout[...], id_ref[...], save_ref)
    predicted = dot(h, proj[...])
    g_ref[...] = dot_nt(predicted.astype(BF), proj[...])


def student_back(g, save_ref, w_qkv, w_out):
    blocks = head_blocks()
    part = lambda i: save_ref[:, i * QUAD : (i + 1) * QUAD]
    n, r = part(7).astype(F32), part(8).astype(F32)
    dy = r * (g - n * jnp.mean(g * n, axis=1, keepdims=True))
    datt = dot_nt(dy.astype(BF), w_out) * part(4).astype(F32)
    drop = (datt * part(3).astype(F32)).astype(BF) * jnp.asarray(-1.0, BF)
    datt = datt.astype(BF)
    q, k, v = part(0), part(1), part(2)
    dqs, dks, dvs = [], [], []
    for w in range(4):
        rows = slice(w * WIN, (w + 1) * WIN)
        e = save_ref[rows, 9 * QUAD : 9 * QUAD + 4 * WIN]
        both = jnp.concatenate([datt[rows], drop[rows]], axis=1)
        ds = (e.astype(F32) * dot_nt(both, stack_values(v[rows]))).astype(BF)
        dqs.append(dot(ds, stack_heads(k[rows])))
        dks.append(unstack_heads(dot_tn(ds, q[rows])))
        dvs.append(unstack_heads(dot_tn(e, datt[rows])))
    dq = 10.0 * jnp.concatenate(dqs, axis=0)
    dk = (1.0 / LOG2E) * jnp.concatenate(dks, axis=0)
    dv = jnp.concatenate(dvs, axis=0)
    q_unit = q.astype(F32) * (1.0 / SCALE)
    k_unit = k.astype(F32)
    dq = part(5).astype(F32) * (dq - q_unit * head_sums(q_unit * dq, blocks))
    dk = part(6).astype(F32) * (dk - k_unit * head_sums(k_unit * dk, blocks))
    dqkv = jnp.concatenate([dq.astype(BF), dk.astype(BF), dv.astype(BF)], axis=1)
    return g + dot_nt(dqkv, w_qkv)


def teacher_first(
    x_ref, far_ref, reg_ref, to_a, a_row, a_col, a_to_g, t_qkv, t_out, *refs
):
    h_ref, g_ref, sends, pad_ref, wqkv, wout, sems = *refs[:2], refs[2:10], *refs[10:]
    weights = fetch((t_qkv.at[0], wqkv, sems.at[0]), (t_out.at[0], wout, sems.at[1]))
    level = lax.axis_index("grp")
    width = x_ref.shape[3]
    blocks = head_blocks()
    x = to_window_order(x_ref, pad_ref, to_a[...])
    far = to_window_order(far_ref, pad_ref, to_a[...])
    ids = window_ids(reg_ref[level], a_row[...], a_col[...])
    ids_far = window_ids(reg_ref[1 - level], a_row[...], a_col[...])
    weights[0].wait()
    q = (unit(dot(x, wqkv[:, :width]), blocks)[0] * SCALE).astype(BF)
    rows = jnp.concatenate([x, far], axis=0)
    k = unit(dot(rows, wqkv[:, width : 2 * width]), blocks)[0].astype(BF)
    v = dot(rows, wqkv[:, 2 * width :]).astype(BF)
    atts = []
    for w in range(4):
        near_rows = slice(w * WIN, (w + 1) * WIN)
        far_rows = slice(NA + w * WIN, NA + (w + 1) * WIN)
        id_keys = jnp.concatenate([ids[near_rows], ids_far[near_rows]], axis=0)
        mask = id_mask(ids[near_rows], id_keys)
        quads = []
        for i in range(0, width, QUAD):
            lanes = slice(i, i + QUAD)
            num, den, _ = attend(
                q[near_rows, lanes],
                jnp.concatenate([k[near_rows, lanes], k[far_rows, lanes]], axis=0),
                jnp.concatenate([v[near_rows, lanes], v[far_rows, lanes]], axis=0),
                mask,
            )
            quads.append((num / den).astype(BF))
        atts.append(jnp.concatenate(quads, axis=1))
    weights[1].wait()
    h = residual(x, jnp.concatenate(atts, axis=0), wout[...])[0]
    h_ref[...] = h
    spread = dot(a_to_g[...], jnp.concatenate([h, ids], axis=1)).astype(BF)
    g_ref[...] = spread
    for ref, names in zip(sends, SENDS):
        spot = 0
        for name in names:
            start, kept = AT[name]
            ref[spot : spot + kept] = spread[start : start + kept]
            spot += kept


SENDS = (
    ("nw", "n", "ne"),
    ("ne", "e", "se"),
    ("sw", "s", "se"),
    ("nw", "w", "sw"),
    ("nw",),
    ("ne",),
    ("se",),
    ("sw",),
)
STEPS = ((-1, 0), (0, 1), (1, 0), (0, -1), (-1, -1), (-1, 1), (1, 1), (1, -1))
SIDES = ("N", "E", "S", "W", "NW", "NE", "SE", "SW")
OPPOSITE = {"N": "S", "S": "N", "E": "W", "W": "E", "NW": "SE", "SE": "NW", "NE": "SW", "SW": "NE"}
EXTRA = {
    "nw": (("N", "sw"), ("W", "ne"), ("NW", "se")),
    "n": (("N", "s"),),
    "ne": (("N", "se"), ("E", "nw"), ("NE", "sw")),
    "e": (("E", "w"),),
    "se": (("S", "ne"), ("E", "sw"), ("SE", "nw")),
    "s": (("S", "n"),),
    "sw": (("S", "nw"), ("W", "se"), ("SW", "ne")),
    "w": (("W", "e"),),
    "c": (),
}


def _arrivals():
    spots, spot = {}, NG
    for side in SIDES:
        for name in SENDS[SIDES.index(OPPOSITE[side])]:
            spots[side, name] = spot
            spot += AT[name][1]
    return spots, spot


ARRIVE, NX = _arrivals()


def teacher_second(
    h_ref, g_ref, r0, r1, r2, r3, r4, r5, r6, r7, from_a, g_to_a, t_qkv, t_out,
    proj, s_qkv, s_out, g0_ref, save0_ref, save1_ref, out_ref, grad_ref,
    wqkv, wout, w_proj, w_sqkv, w_sout, save0, save1, sems,
):
    later = fetch(
        (t_qkv.at[1], wqkv, sems.at[0]),
        (t_out.at[1], wout, sems.at[1]),
        (proj, w_proj, sems.at[2]),
        (save1_ref, save1, sems.at[3]),
        (s_qkv, w_sqkv, sems.at[4]),
        (s_out, w_sout, sems.at[5]),
        (save0_ref, save0, sems.at[6]),
    )
    lat = lax.axis_index("lat")
    last = lax.axis_size("lat") - 1
    width = h_ref.shape[1]
    blocks = head_blocks()
    own = g_ref[...]
    arrived = []
    ids = [own[:, width:]]
    for side, ref in zip(SIDES, (r0, r1, r2, r3, r4, r5, r6, r7)):
        arrived.append(ref[:, :width])
        tag = ref[:, width:]
        if "N" in side:
            tag = tag * jnp.where(lat > 0, 1.0, 0.0).astype(BF)
        if "S" in side:
            tag = tag * jnp.where(lat < last, 1.0, 0.0).astype(BF)
        ids.append(tag)
    ids = jnp.concatenate(ids, axis=0)
    later[0].wait()
    q = (unit(dot(own[:, :width], wqkv[:, :width]), blocks)[0] * SCALE).astype(BF)
    rows = jnp.concatenate([own[:, :width]] + arrived, axis=0)
    k = unit(dot(rows, wqkv[:, width : 2 * width]), blocks)[0].astype(BF)
    v = dot(rows, wqkv[:, 2 * width :]).astype(BF)
    atts = []
    for name, _, _, kept in PARTS:
        start = AT[name][0]
        spans = [slice(start, start + kept)]
        for side, part in EXTRA[name]:
            spot = ARRIVE[side, part]
            spans.append(slice(spot, spot + AT[part][1]))
        gather = lambda x: jnp.concatenate([x[s] for s in spans], axis=0) if len(spans) > 1 else x[spans[0]]
        mask = id_mask(ids[spans[0]], gather(ids))
        k_rows, v_rows = gather(k), gather(v)
        quads = []
        for i in range(0, width, QUAD):
            lanes = slice(i, i + QUAD)
            num, den, _ = attend(q[spans[0], lanes], k_rows[:, lanes], v_rows[:, lanes], mask)
            quads.append((num / den).astype(BF))
        atts.append(jnp.concatenate(quads, axis=1))
    att = dot(g_to_a[...], jnp.concatenate(atts, axis=0)).astype(BF)
    later[1].wait()
    teacher = residual(h_ref[...], att, wout[...])[0]
    natural = dot(from_a[...], teacher).astype(BF)
    out_ref[0] = natural.reshape(ROWS, 16, width)[:, :COLS, :]

    for copy in later[2:]:
        copy.wait()
    g = g0_ref[...] - dot_nt(teacher, w_proj[...])
    g = student_back(g, save1, w_sqkv[1], w_sout[1])
    g = student_back(g, save0, w_sqkv[0], w_sout[0])
    high = g.astype(BF)
    low = (g - high.astype(F32)).astype(BF)
    natural = dot(from_a[...], high) + dot(from_a[...], low)
    grad_ref[0] = natural.reshape(ROWS, 16, g.shape[1])[:, :COLS, :]


VMEM = pl.BlockSpec(memory_space=pltpu.VMEM)
ANY = pl.BlockSpec(memory_space=pl.ANY)


def call(kernel, name, outs, specs, args, scratch=(), flops=0):
    shapes = [jax.ShapeDtypeStruct(s, d) for s, d in outs]
    touched = sum(a.size * a.dtype.itemsize for a in args)
    return pl.pallas_call(
        kernel,
        name=name,
        out_shape=shapes,
        in_specs=specs,
        out_specs=[VMEM] * len(outs),
        scratch_shapes=list(scratch),
        compiler_params=pltpu.CompilerParams(vmem_limit_bytes=40 << 20),
        cost_estimate=pl.CostEstimate(flops=flops, bytes_accessed=touched, transcendentals=0),
    )(*args)


def neighbour_routes(step, lat_size, lon_size):
    di, dj = step
    route = []
    for i in range(lat_size):
        for j in range(lon_size):
            to = ((i + di) % lat_size) * lon_size + (j + dj) % lon_size
            route.append((i * lon_size + j, to))
    return route


def shards(teacher_in, student_in, regions, t_qkv, t_out, s_qkv, s_out, s_proj):
    width, narrow = teacher_in.shape[3], student_in.shape[3]
    lat_size, lon_size = lax.axis_size("lat"), lax.axis_size("lon")
    far = lax.ppermute(teacher_in, "grp", [(0, 1), (1, 0)])

    def buffers(*arrays):
        return [pltpu.VMEM(a, BF) for a in arrays] + [pltpu.SemaphoreType.DMA((len(arrays),))]

    layer_t, layer_s = t_qkv.shape[1:], s_qkv.shape[1:]
    out_t, out_s = t_out.shape[1:], s_out.shape[1:]

    args = [student_in, regions, TO_A, A_ROW, A_COL, s_qkv, s_out]
    h1, ids, save0 = call(
        student_first, "student_first",
        [((NA, narrow), BF), ((NA, 128), BF), ((NA, SAVE), BF)],
        [VMEM] * 5 + [ANY] * 2,
        args, [pltpu.VMEM((ROWS, 16, narrow), BF)] + buffers(layer_s, out_s), 10**9,
    )

    args = [teacher_in, far, regions, TO_A, A_ROW, A_COL, A_TO_G, t_qkv, t_out]
    pieces = [sum(AT[n][1] for n in names) for names in SENDS]
    hidden, spread, *sends = call(
        teacher_first, "teacher_first",
        [((NA, width), BF), ((NG, width + 128), BF)] + [((n, width + 128), BF) for n in pieces],
        [VMEM] * 7 + [ANY] * 2,
        args, [pltpu.VMEM((ROWS, 16, width), BF)] + buffers(layer_t, out_t), 4 * 10**9,
    )
    came = {}
    for side, step, piece in zip(SIDES, STEPS, sends):
        came[OPPOSITE[side]] = lax.ppermute(
            piece, ("lat", "lon"), neighbour_routes(step, lat_size, lon_size)
        )

    args = [h1, ids, s_qkv, s_out, s_proj, spread]
    g0, save1 = call(
        student_second, "student_second",
        [((NA, narrow), F32), ((NA, SAVE), BF)],
        [VMEM] * 2 + [ANY, ANY, VMEM, ANY],
        args, buffers(layer_s, out_s), 10**9,
    )

    args = [hidden, spread] + [came[s] for s in SIDES] + [FROM_A, G_TO_A, t_qkv, t_out]
    args += [s_proj, s_qkv, s_out, g0, save0, save1]
    specs = [VMEM] * 12 + [ANY] * 5 + [VMEM] + [ANY] * 2
    scratch = buffers(
        layer_t, out_t, s_proj.shape, s_qkv.shape, s_out.shape, save0.shape, save1.shape
    )
    return tuple(
        call(
            teacher_second, "teacher_second",
            [(teacher_in.shape, BF), (student_in.shape, F32)],
            specs, args, scratch, 6 * 10**9,
        )
    )


def solution(mesh):
    tiles = P("grp", "lat", "lon", None)
    return jax.shard_map(
        shards,
        mesh=mesh,
        in_specs=(tiles, tiles, P(None, "lat", "lon"), P(), P(), P(), P(), P()),
        out_specs=(tiles, tiles),
        check_vma=False,
    )
```

profile of v0, /device:TPU:6, one launch (start us, length us, event | category | flops | bytes accessed | tf_op | source)
XLA Modules:
  0.0 68.8 jit_solution(6887118810793576324)
XLA Ops:
  0.6 1.1 %copy.17.x_ref = bf16[1,24,12,512]{3,2,1,0:T(8,128)(2,1)S(1)} copy(bf16[1,24,12,512]{3,1,2,0:T(8,128)(2,1)} %param.14) | data formatting | bytes 589824 | tf_op args[0]
  1.7 0.1 collective-permute-start
  1.8 0.8 %copy.18.reg_ref = s32[2,24,12]{2,1,0:T(8,128)S(1)} copy(s32[2,24,12]{1,0,2:T(2,128)} %param.16) | data formatting | bytes 4608 | tf_op args[2]
  2.6 0.9 %collective-permute-done.far_ref = bf16[1,24,12,512]{3,2,1,0:T(8,128)(2,1)S(1)} collective-permute-done((bf16[1,24,12,512]{3,2,1,0:T(8,128)(2,1)S(1)}, bf16[1,24,12,512]{3,2,1,0:T(8,128)(2,1)S(1)}, u32[]{:S(2)}, u32[]{:S(2)}) %collective-permute-start) | collective-permute-done | bytes 294944 | tf_op jit(solution)/shard_map/ppermute | solution.py:433
  3.5 1.9 %copy-done = bf16[2,512,1536]{2,1,0:T(8,128)(2,1)S(1)} copy-done((bf16[2,512,1536]{2,1,0:T(8,128)(2,1)S(1)}, bf16[2,512,1536]{2,1,0:T(8,128)(2,1)}, u32[]{:S(2)}) %copy-start) | copy-done | bytes 3145752
  5.4 1.2 %copy-done.2 = bf16[2,512,512]{2,1,0:T(8,128)(2,1)S(1)} copy-done((bf16[2,512,512]{2,1,0:T(8,128)(2,1)S(1)}, bf16[2,512,512]{2,1,0:T(8,128)(2,1)}, u32[]{:S(2)}) %copy-start.2) | copy-done | bytes 1048600
  6.6 1.0 %copy-done.8 = bf16[400,320]{1,0:T(8,128)(2,1)S(1)} copy-done((bf16[400,320]{1,0:T(8,128)(2,1)S(1)}, bf16[400,320]{1,0:T(8,128)(2,1)}, u32[]{:S(2)}) %copy-start.8) | copy-done | bytes 256024
  7.6 0.9 %copy-done.10 = bf16[320,384]{1,0:T(8,128)(2,1)S(1)} copy-done((bf16[320,384]{1,0:T(8,128)(2,1)S(1)}, bf16[320,384]{1,0:T(8,128)(2,1)}, u32[]{:S(2)}) %copy-start.10) | copy-done | bytes 245784
  8.5 0.9 %copy-done.11 = bf16[320,12]{1,0:T(8,128)(2,1)S(1)} copy-done((bf16[320,12]{1,0:T(8,128)(2,1)S(1)}, bf16[320,12]{1,0:T(8,128)(2,1)}, u32[]{:S(2)}) %copy-start.11) | copy-done | bytes 7704
  9.4 0.9 %copy-done.12 = bf16[320,24]{1,0:T(8,128)(2,1)S(1)} copy-done((bf16[320,24]{1,0:T(8,128)(2,1)S(1)}, bf16[320,24]{1,0:T(8,128)(2,1)}, u32[]{:S(2)}) %copy-start.12) | copy-done | bytes 15384
  10.3 5.7 %teacher_first.1 = (bf16[320,512]{1,0:T(8,128)(2,1)S(1)}, bf16[400,640]{1,0:T(8,128)(2,1)S(1)}, bf16[112,640]{1,0:T(8,128)(2,1)S(1)}, bf16[112,640]{1,0:T(8,128)...) custom-call(bf16[1,24,12,512]{3,2,1,0:T(8,128)(2,1)S(1)} %copy.17.x_, ...), custom_call_target="tpu_custom_call" | custom-call | flops 4000000000 | bytes 5311232 | tf_op jit(solution)/shard_map/teacher_first/pallas_call | solution.py:408
  16.0 8.2 %collective-permute-start.5 = (bf16[32,640]{1,0:T(8,128)(2,1)S(1)}, bf16[32,640]{1,0:T(8,128)(2,1)S(1)}, u32[]{:S(2)}, u32[]{:S(2)}) collective-permute-start(bf16[32,640]{1,0:T(8,128)(2,1)S(1)} %get-tuple-element.23), channel_id=1, source_target_pairs={{0,34},{2,36},{4,38},{6,40},{8,42},{10,44},{12,46},{14,48},{16,50}... | collective-permute-start | bytes 122888 | tf_op jit(solution)/shard_map/ppermute | solution.py:459
  24.2 2.6 %collective-permute-start.6 = (bf16[32,640]{1,0:T(8,128)(2,1)S(1)}, bf16[32,640]{1,0:T(8,128)(2,1)S(1)}, u32[]{:S(2)}, u32[]{:S(2)}) collective-permute-start(bf16[32,640]{1,0:T(8,128)(2,1)S(1)} %get-tuple-element.24), channel_id=1, source_target_pairs={{0,62},{2,32},{4,34},{6,36},{8,38},{10,40},{12,42},{14,44},{16,46}... | collective-permute-start | bytes 122888 | tf_op jit(solution)/shard_map/ppermute | solution.py:459
  26.9 3.2 %collective-permute-start.7 = (bf16[32,640]{1,0:T(8,128)(2,1)S(1)}, bf16[32,640]{1,0:T(8,128)(2,1)S(1)}, u32[]{:S(2)}, u32[]{:S(2)}) collective-permute-start(bf16[32,640]{1,0:T(8,128)(2,1)S(1)} %get-tuple-element.25), channel_id=1, source_target_pairs={{0,254},{2,224},{4,226},{6,228},{8,230},{10,232},{12,234},{14,236}... | collective-permute-start | bytes 122888 | tf_op jit(solution)/shard_map/ppermute | solution.py:459
  30.1 4.8 %collective-permute-start.1 = (bf16[112,640]{1,0:T(8,128)(2,1)S(1)}, bf16[112,640]{1,0:T(8,128)(2,1)S(1)}, u32[]{:S(2)}, u32[]{:S(2)}) collective-permute-start(bf16[112,640]{1,0:T(8,128)(2,1)S(1)} %get-tuple-element.19), channel_id=1, source_target_pairs={{0,32},{2,34},{4,36},{6,38},{8,40},{10,42},{12,44},{14,46},{16,48}... | collective-permute-start | bytes 430088 | tf_op jit(solution)/shard_map/ppermute | solution.py:459
  34.9 3.4 %collective-permute-start.2 = (bf16[112,640]{1,0:T(8,128)(2,1)S(1)}, bf16[112,640]{1,0:T(8,128)(2,1)S(1)}, u32[]{:S(2)}, u32[]{:S(2)}) collective-permute-start(bf16[112,640]{1,0:T(8,128)(2,1)S(1)} %get-tuple-element.20), channel_id=1, source_target_pairs={{0,30},{2,0},{4,2},{6,4},{8,6},{10,8},{12,10},{14,12},{16,14},{18,... | collective-permute-start | bytes 430088 | tf_op jit(solution)/shard_map/ppermute | solution.py:459
  38.3 0.1 collective-permute-start.4
  38.5 2.4 %student_first.1 = (bf16[320,256]{1,0:T(8,128)(2,1)S(1)}, bf16[320,128]{1,0:T(8,128)(2,1)S(1)}, bf16[320,2688]{1,0:T(8,128)(2,1)S(1)}) custom-call(bf16[1,24,12,256]{3,2,1,0:T(8,128)(2,1)S(1)} %copy.19.x_ref, s32[2,24,12]{2,1,0:T(8,128)S(1)} %copy.18.reg_ref, bf16[320,384]{1,0:T(8,128)(2,1)S(1)} %copy-done.10, bf16[320,24]{1,0:T(8,128)(2,1)S(1)} %copy-done.12, ...), custom_call_target="tpu_custom_call" | custom-call | flops 1000000000 | bytes 1467136 | tf_op jit(solution)/shard_map/student_first/pallas_call | solution.py:408
  40.9 0.3 collective-permute-start.8
  41.2 2.3 %student_second.1 = (f32[320,256]{1,0:T(8,128)S(1)}, bf16[320,2688]{1,0:T(8,128)(2,1)S(1)}) custom-call(bf16[320,256]{1,0:T(8,128)(2,1)S(1)} %get-tuple-element.27.h_ref, bf16[320,128]{1,0:T(8,128)(2,1)S(1)} %get-tuple-element.28.id_ref, bf16[2,256,768]{2,1,0:T(8,128)(2,1)S(1)} %copy-done.4, bf16[2,256,256]{2,1,0:T(8,128)(2,1)S(1)} %copy-done.6, ...), custom_call_target="tpu_custom_call" | custom-call | flops 1000000000 | bytes 2068480 | tf_op jit(solution)/shard_map/student_second/pallas_call | solution.py:408
  43.6 10.2 %collective-permute-done.8.r7 = bf16[32,640]{1,0:T(8,128)(2,1)S(1)} collective-permute-done((bf16[32,640]{1,0:T(8,128)(2,1)S(1)}, bf16[32,640]{1,0:T(8,128)(2,1)S(1)}, u32[]{:S(2)}, u32[]{:S(2)}) %collective-permute-start.8) | collective-permute-done | bytes 40992 | tf_op jit(solution)/shard_map/ppermute | solution.py:459
  53.8 13.2 %teacher_second.1 = (bf16[1,24,12,512]{3,2,1,0:T(8,128)(2,1)S(1)}, f32[1,24,12,256]{3,2,1,0:T(8,128)S(1)}) custom-call(bf16[320,512]{1,0:T(8,128)(2,1)S(1)} %get-tuple-element.17.h_ref, bf16[400,640]{1,0:T(8,128)(2,1)S(1)} %get-tuple-element.18.after_ref.g_ref, bf16[112,640]{1,0:T(8,128)(2,1)S(1)} %collective-permute-done.1.r0, ...), custom_call_target="tpu_custom_call" | custom-call | flops 6000000000 | bytes 11352064 | tf_op jit(solution)/shard_map/teacher_second/pallas_call | solution.py:408
  67.0 0.9 %copy.21 = bf16[1,24,12,512]{3,1,2,0:T(8,128)(2,1)} copy(bf16[1,24,12,512]{3,2,1,0:T(8,128)(2,1)S(1)} %get-tuple-element.32) | data formatting | bytes 589824 | tf_op jit(solution)/shard_map/teacher_second/pallas_call | solution.py:408
  67.9 0.9 %copy.22 = f32[1,24,12,256]{3,1,2,0:T(8,128)} copy(f32[1,24,12,256]{3,2,1,0:T(8,128)S(1)} %get-tuple-element.33) | data formatting | bytes 589824 | tf_op jit(solution)/shard_map/teacher_second/pallas_call | solution.py:408
  (31 shorter events, 0.1 us)
Async XLA Ops:
  1.7 1.8 %collective-permute-start = (bf16[1,24,12,512]{3,2,1,0:T(8,128)(2,1)S(1)}, bf16[1,24,12,512]{3,2,1,0:T(8,128)(2,1)S(1)}, u32[]{:S(2)}, u32[]{:S(2)}) collective-permute-start(bf16[1,24,12,512]{3,2,1,0:T(8,128)(2,1)S(1)} %copy.17.x_ref), channel_id=1, source_target_pairs={{0,1},{1,0},{2,3},{3,2},{4,5},{5,4},{6,7},{7,6},{8,9},{9,8},{10,11... | collective-permute-start | bytes 884744 | tf_op jit(solution)/shard_map/ppermute | solution.py:433
  3.5 1.9 %copy-start = (bf16[2,512,1536]{2,1,0:T(8,128)(2,1)S(1)}, bf16[2,512,1536]{2,1,0:T(8,128)(2,1)}, u32[]{:S(2)}) copy-start(bf16[2,512,1536]{2,1,0:T(8,128)(2,1)} %t_qkv.3) | copy-start | bytes 9437188
  5.4 1.2 %copy-start.2 = (bf16[2,512,512]{2,1,0:T(8,128)(2,1)S(1)}, bf16[2,512,512]{2,1,0:T(8,128)(2,1)}, u32[]{:S(2)}) copy-start(bf16[2,512,512]{2,1,0:T(8,128)(2,1)} %t_out.3) | copy-start | bytes 3145732
  6.6 1.0 %copy-start.8 = (bf16[400,320]{1,0:T(8,128)(2,1)S(1)}, bf16[400,320]{1,0:T(8,128)(2,1)}, u32[]{:S(2)}) copy-start(bf16[400,320]{1,0:T(8,128)(2,1)} %constant.15.clone.a_to_g) | copy-start | bytes 768004
  7.6 0.9 %copy-start.10 = (bf16[320,384]{1,0:T(8,128)(2,1)S(1)}, bf16[320,384]{1,0:T(8,128)(2,1)}, u32[]{:S(2)}) copy-start(bf16[320,384]{1,0:T(8,128)(2,1)} %constant.12.clone.to_a) | copy-start | bytes 737284
  8.5 0.9 %copy-start.11 = (bf16[320,12]{1,0:T(8,128)(2,1)S(1)}, bf16[320,12]{1,0:T(8,128)(2,1)}, u32[]{:S(2)}) copy-start(bf16[320,12]{1,0:T(8,128)(2,1)} %constant.14.clone.a_col) | copy-start | bytes 23044
  9.4 0.9 %copy-start.12 = (bf16[320,24]{1,0:T(8,128)(2,1)S(1)}, bf16[320,24]{1,0:T(8,128)(2,1)}, u32[]{:S(2)}) copy-start(bf16[320,24]{1,0:T(8,128)(2,1)} %constant.13.clone.a_row) | copy-start | bytes 46084
  10.3 16.5 %copy-start.13 = (bf16[1,24,12,256]{3,1,2,0:T(8,128)(2,1)S(1)}, bf16[1,24,12,256]{3,1,2,0:T(8,128)(2,1)}, u32[]{:S(2)}) copy-start(bf16[1,24,12,256]{3,1,2,0:T(8,128)(2,1)} %param.15) | copy-start | bytes 442372
  10.3 28.1 %copy-start.4 = (bf16[2,256,768]{2,1,0:T(8,128)(2,1)S(1)}, bf16[2,256,768]{2,1,0:T(8,128)(2,1)}, u32[]{:S(2)}) copy-start(bf16[2,256,768]{2,1,0:T(8,128)(2,1)} %s_qkv.5) | copy-start | bytes 2359300
  10.3 28.1 %copy-start.6 = (bf16[2,256,256]{2,1,0:T(8,128)(2,1)S(1)}, bf16[2,256,256]{2,1,0:T(8,128)(2,1)}, u32[]{:S(2)}) copy-start(bf16[2,256,256]{2,1,0:T(8,128)(2,1)} %s_out.5) | copy-start | bytes 786436
  16.0 22.3 %collective-permute-start.5 = (bf16[32,640]{1,0:T(8,128)(2,1)S(1)}, bf16[32,640]{1,0:T(8,128)(2,1)S(1)}, u32[]{:S(2)}, u32[]{:S(2)}) collective-permute-start(bf16[32,640]{1,0:T(8,128)(2,1)S(1)} %get-tuple-element.23), channel_id=1, source_target_pairs={{0,34},{2,36},{4,38},{6,40},{8,42},{10,44},{12,46},{14,48},{16,50}... | collective-permute-start | bytes 122888 | tf_op jit(solution)/shard_map/ppermute | solution.py:459
  24.2 14.1 %collective-permute-start.6 = (bf16[32,640]{1,0:T(8,128)(2,1)S(1)}, bf16[32,640]{1,0:T(8,128)(2,1)S(1)}, u32[]{:S(2)}, u32[]{:S(2)}) collective-permute-start(bf16[32,640]{1,0:T(8,128)(2,1)S(1)} %get-tuple-element.24), channel_id=1, source_target_pairs={{0,62},{2,32},{4,34},{6,36},{8,38},{10,40},{12,42},{14,44},{16,46}... | collective-permute-start | bytes 122888 | tf_op jit(solution)/shard_map/ppermute | solution.py:459
  26.9 14.1 %collective-permute-start.7 = (bf16[32,640]{1,0:T(8,128)(2,1)S(1)}, bf16[32,640]{1,0:T(8,128)(2,1)S(1)}, u32[]{:S(2)}, u32[]{:S(2)}) collective-permute-start(bf16[32,640]{1,0:T(8,128)(2,1)S(1)} %get-tuple-element.25), channel_id=1, source_target_pairs={{0,254},{2,224},{4,226},{6,228},{8,230},{10,232},{12,234},{14,236}... | collective-permute-start | bytes 122888 | tf_op jit(solution)/shard_map/ppermute | solution.py:459
  30.1 23.7 %collective-permute-start.1 = (bf16[112,640]{1,0:T(8,128)(2,1)S(1)}, bf16[112,640]{1,0:T(8,128)(2,1)S(1)}, u32[]{:S(2)}, u32[]{:S(2)}) collective-permute-start(bf16[112,640]{1,0:T(8,128)(2,1)S(1)} %get-tuple-element.19), channel_id=1, source_target_pairs={{0,32},{2,34},{4,36},{6,38},{8,40},{10,42},{12,44},{14,46},{16,48}... | collective-permute-start | bytes 430088 | tf_op jit(solution)/shard_map/ppermute | solution.py:459
  34.9 18.9 %collective-permute-start.2 = (bf16[112,640]{1,0:T(8,128)(2,1)S(1)}, bf16[112,640]{1,0:T(8,128)(2,1)S(1)}, u32[]{:S(2)}, u32[]{:S(2)}) collective-permute-start(bf16[112,640]{1,0:T(8,128)(2,1)S(1)} %get-tuple-element.20), channel_id=1, source_target_pairs={{0,30},{2,0},{4,2},{6,4},{8,6},{10,8},{12,10},{14,12},{16,14},{18,... | collective-permute-start | bytes 430088 | tf_op jit(solution)/shard_map/ppermute | solution.py:459
  38.3 15.5 %collective-permute-start.3 = (bf16[112,640]{1,0:T(8,128)(2,1)S(1)}, bf16[112,640]{1,0:T(8,128)(2,1)S(1)}, u32[]{:S(2)}, u32[]{:S(2)}) collective-permute-start(bf16[112,640]{1,0:T(8,128)(2,1)S(1)} %get-tuple-element.21), channel_id=1, source_target_pairs={{0,224},{2,226},{4,228},{6,230},{8,232},{10,234},{12,236},{14,238}... | collective-permute-start | bytes 430088 | tf_op jit(solution)/shard_map/ppermute | solution.py:459
  38.3 2.9 %copy-start.5 = (bf16[256,512]{1,0:T(8,128)(2,1)S(1)}, bf16[256,512]{1,0:T(8,128)(2,1)}, u32[]{:S(2)}) copy-start(bf16[256,512]{1,0:T(8,128)(2,1)} %proj.3) | copy-start | bytes 786436
  38.3 15.4 %collective-permute-start.4 = (bf16[112,640]{1,0:T(8,128)(2,1)S(1)}, bf16[112,640]{1,0:T(8,128)(2,1)S(1)}, u32[]{:S(2)}, u32[]{:S(2)}) collective-permute-start(bf16[112,640]{1,0:T(8,128)(2,1)S(1)} %get-tuple-element.22), channel_id=1, source_target_pairs={{0,2},{2,4},{4,6},{6,8},{8,10},{10,12},{12,14},{14,16},{16,18},{18... | collective-permute-start | bytes 430088 | tf_op jit(solution)/shard_map/ppermute | solution.py:459
  38.5 15.3 %copy-start.3 = (bf16[2,512,512]{2,1,0:T(8,128)(2,1)S(1)}, bf16[2,512,512]{2,1,0:T(8,128)(2,1)}, u32[]{:S(2)}) copy-start(bf16[2,512,512]{2,1,0:T(8,128)(2,1)} %t_out.3) | copy-start | bytes 3145732
  38.5 15.3 %copy-start.9 = (bf16[384,320]{1,0:T(8,128)(2,1)S(1)}, bf16[384,320]{1,0:T(8,128)(2,1)}, u32[]{:S(2)}) copy-start(bf16[384,320]{1,0:T(8,128)(2,1)} %constant.16.clone.from_a) | copy-start | bytes 737284
  40.9 12.8 %collective-permute-start.8 = (bf16[32,640]{1,0:T(8,128)(2,1)S(1)}, bf16[32,640]{1,0:T(8,128)(2,1)S(1)}, u32[]{:S(2)}, u32[]{:S(2)}) collective-permute-start(bf16[32,640]{1,0:T(8,128)(2,1)S(1)} %get-tuple-element.26), channel_id=1, source_target_pairs={{0,226},{2,228},{4,230},{6,232},{8,234},{10,236},{12,238},{14,240}... | collective-permute-start | bytes 122888 | tf_op jit(solution)/shard_map/ppermute | solution.py:459
  41.2 12.6 %copy-start.1 = (bf16[2,512,1536]{2,1,0:T(8,128)(2,1)S(1)}, bf16[2,512,1536]{2,1,0:T(8,128)(2,1)}, u32[]{:S(2)}) copy-start(bf16[2,512,1536]{2,1,0:T(8,128)(2,1)} %t_qkv.3) | copy-start | bytes 9437188
  41.2 12.6 %copy-start.7 = (bf16[320,400]{1,0:T(8,128)(2,1)S(1)}, bf16[320,400]{1,0:T(8,128)(2,1)}, u32[]{:S(2)}) copy-start(bf16[320,400]{1,0:T(8,128)(2,1)} %constant.17.clone.g_to_a) | copy-start | bytes 768004
where the time goes:
time: 69.1 us; the launch traced here: 68.8 us
  Pallas kernels  23.6 us (34%)
  starting transfers between devices  22.7 us (33%)
  waiting for transfers between devices  11.1 us (16%)
  local copies, waits for them, and re-layouts  10.5 us (15%)
  between operations  0.83 us (1%)
    pallas_call x4, Pallas kernels, call(): pl.pallas_call(kernel, name=name, out_shape=shapes, in_specs=specs, out_s...  23.6 us
    ppermute x8, starting transfers between devices, shards(): lax.ppermute(piece, ('lat', 'lon'), neighbour_routes(step, lat_size, lon_...  22.6 us
    ppermute x8, waiting for transfers between devices, shards(): lax.ppermute(piece, ('lat', 'lon'), neighbour_routes(step, lat_size, lon_...  10.2 us
    unnamed x31, local copies, waits for them, and re-layouts  8.72 us
    pallas_call x2, local copies, waits for them, and re-layouts, call(): pl.pallas_call(kernel, name=name, out_shape=shapes, in_specs=specs, out_s...  1.77 us
  transfers between devices with their start and end apart: 9, of which 2 were waited for; matrix products, arithmetic and copies ran while one was open for 1% of the time, Pallas kernels for 7%

commit v1 on v0

v1 whole, which is shorter than its diff:
```python
import functools

import jax
import jax.numpy as jnp
import ml_dtypes
import numpy as np
from jax import lax
from jax.experimental import pallas as pl
from jax.experimental.pallas import tpu as pltpu
from jax.sharding import PartitionSpec as P

HEADS_T = 8
HEADS_S = 4
EPS = 1e-06
LOG2E = 1.4426950408889634
SCALE = 10.0 * LOG2E
BF = jnp.bfloat16
F32 = jnp.float32

ROWS, COLS = 24, 12
WIN = 80
NA = 4 * WIN
TALL = 32
NAT = COLS * TALL
QUAD = 256

PARTS = (
    ("nw", (0, 6), (0, 3), 32),
    ("n", (0, 6), (3, 9), 48),
    ("ne", (0, 6), (9, 12), 32),
    ("e", (6, 18), (9, 12), 48),
    ("se", (18, 24), (9, 12), 32),
    ("s", (18, 24), (3, 9), 48),
    ("sw", (18, 24), (0, 3), 32),
    ("w", (6, 18), (0, 3), 48),
    ("c", (6, 18), (3, 9), 80),
)
AT = {}
NG = 0
for _name, _r, _c, _kept in PARTS:
    AT[_name] = (NG, _kept)
    NG += _kept


def _a_slot(r, c):
    return (2 * (r // 12) + c // 6) * WIN + (r % 12) * 6 + c % 6


def _tables():
    to_a = np.zeros((NA, NAT), ml_dtypes.bfloat16)
    a_row = np.zeros((NA, ROWS), ml_dtypes.bfloat16)
    a_col = np.zeros((NA, COLS), ml_dtypes.bfloat16)
    for r in range(ROWS):
        for c in range(COLS):
            slot = _a_slot(r, c)
            to_a[slot, c * TALL + r] = 1
            a_row[slot, r] = 1
            a_col[slot, c] = 1
    a_to_g = np.zeros((NG, NA), ml_dtypes.bfloat16)
    for name, (r0, r1), (c0, c1), _ in PARTS:
        spot = AT[name][0]
        for r in range(r0, r1):
            for c in range(c0, c1):
                a_to_g[spot, _a_slot(r, c)] = 1
                spot += 1
    return to_a, a_row, a_col, a_to_g


TO_A, A_ROW, A_COL, A_TO_G = _tables()
FROM_A = np.ascontiguousarray(TO_A.T)
G_TO_A = np.ascontiguousarray(A_TO_G.T)


def dot(a, b):
    return jnp.dot(a, b, preferred_element_type=F32)


def dot_nt(a, b):
    return lax.dot_general(a, b, (((1,), (1,)), ((), ())), preferred_element_type=F32)


def dot_tn(a, b):
    return lax.dot_general(a, b, (((0,), (0,)), ((), ())), preferred_element_type=F32)


def head_lanes(rows, h):
    lane = lax.broadcasted_iota(jnp.int32, (rows, QUAD), 1)
    return jnp.where((lane >> 6) == h, 1.0, 0.0).astype(BF)


def head_blocks():
    row = lax.broadcasted_iota(jnp.int32, (QUAD, QUAD), 0)
    lane = lax.broadcasted_iota(jnp.int32, (QUAD, QUAD), 1)
    return jnp.where((row >> 6) == (lane >> 6), 1.0, 0.0).astype(BF)


def stack_heads(x):
    return jnp.concatenate([x * head_lanes(1, h) for h in range(4)], axis=0)


def stack_values(v):
    rows = v.shape[0]
    ones = jnp.concatenate([head_lanes(rows, h) for h in range(4)], axis=0)
    return jnp.concatenate([stack_heads(v), ones], axis=1)


def unstack_heads(x):
    n = x.shape[0] // 4
    lane = lax.broadcasted_iota(jnp.int32, (1, QUAD), 1) >> 6
    total = x[:n]
    for h in range(1, 4):
        total = jnp.where(lane == h, x[h * n : (h + 1) * n], total)
    return total


def head_sums(x, blocks):
    groups = [dot(x[:, i : i + QUAD].astype(BF), blocks) for i in range(0, x.shape[1], QUAD)]
    return groups[0] if len(groups) == 1 else jnp.concatenate(groups, axis=1)


def unit(x, blocks):
    scale = lax.rsqrt(head_sums(x * x, blocks) + EPS)
    return x * scale, scale


def id_mask(id_query, id_keys):
    keys = jnp.concatenate([id_keys] * 4, axis=0)
    row = dot_nt(jnp.full((8, 128), 1.0 / 128, BF), keys)[0:1]
    return id_query.astype(F32)[:, 0:1] == row


def attend(q, k, v, mask):
    scores = dot_nt(q, stack_heads(k))
    e = jnp.where(mask, jnp.exp2(scores), 0.0).astype(BF)
    both = dot(e, stack_values(v))
    return both[:, :QUAD], both[:, QUAD:], e


def to_window_order(x_ref, pad_ref, to_a):
    pad_ref[...] = jnp.zeros_like(pad_ref)
    pad_ref[:, 0:ROWS, :] = x_ref[0]
    natural = pad_ref[...].reshape(NAT, x_ref.shape[3])
    return dot(to_a, natural).astype(BF)


def window_ids(reg, a_row, a_col):
    table = (reg + 1).astype(F32).astype(BF)
    picked = (dot(a_col, table) * a_row.astype(F32)).astype(BF)
    return dot(picked, jnp.ones((ROWS, 128), BF)).astype(BF)


def by_level(reg_ref):
    level = lax.axis_index("grp")
    low, high = reg_ref[:, 0, :], reg_ref[:, 1, :]
    own = jnp.where(level == 0, low, high)
    return own, low + high - own


def residual(x, att, w):
    y = dot(att, w)
    r = lax.rsqrt(jnp.mean(y * y, axis=1, keepdims=True) + EPS)
    n = y * r
    return (x.astype(F32) + n).astype(BF), n, r


SAVE = 9 * QUAD + 384


def student_layer(x, w_qkv, w_out, ids, save_ref):
    blocks = head_blocks()
    qkv = dot(x, w_qkv)
    q, sq = unit(qkv[:, :QUAD], blocks)
    k, sk = unit(qkv[:, QUAD : 2 * QUAD], blocks)
    q = (q * SCALE).astype(BF)
    k = k.astype(BF)
    v = qkv[:, 2 * QUAD :].astype(BF)
    atts = []
    for w in range(4):
        rows = slice(w * WIN, (w + 1) * WIN)
        mask = id_mask(ids[rows], ids[rows])
        num, den, e = attend(q[rows], k[rows], v[rows], mask)
        z = 1.0 / den
        att = num * z
        save_ref[rows, 4 * QUAD : 5 * QUAD] = z.astype(BF)
        save_ref[rows, 9 * QUAD : 9 * QUAD + 4 * WIN] = e
        atts.append(att.astype(BF))
    att = jnp.concatenate(atts, axis=0)
    h, n, r = residual(x, att, w_out)
    for i, part in ((0, q), (1, k), (2, v), (3, att), (5, sq), (6, sk), (7, n)):
        save_ref[:, i * QUAD : (i + 1) * QUAD] = part.astype(BF)
    save_ref[:, 8 * QUAD : 9 * QUAD] = jnp.broadcast_to(r, (NA, QUAD)).astype(BF)
    return h


def fetch(*pairs):
    copies = [pltpu.make_async_copy(*pair) for pair in pairs]
    for copy in copies:
        copy.start()
    return copies


def student_first(x_ref, id_ref, to_a, s_qkv, s_out, after_ref, h_ref, save_ref, pad_ref):
    x = to_window_order(x_ref, pad_ref, to_a[...])
    h_ref[...] = student_layer(x, s_qkv[0], s_out[0], id_ref[...], save_ref)


def student_back(g, save_ref, w_qkv, w_out):
    blocks = head_blocks()
    part = lambda i: save_ref[:, i * QUAD : (i + 1) * QUAD]
    n, r = part(7).astype(F32), part(8).astype(F32)
    dy = r * (g - n * jnp.mean(g * n, axis=1, keepdims=True))
    datt = dot_nt(dy.astype(BF), w_out) * part(4).astype(F32)
    drop = (datt * part(3).astype(F32)).astype(BF) * jnp.asarray(-1.0, BF)
    datt = datt.astype(BF)
    q, k, v = part(0), part(1), part(2)
    dqs, dks, dvs = [], [], []
    for w in range(4):
        rows = slice(w * WIN, (w + 1) * WIN)
        e = save_ref[rows, 9 * QUAD : 9 * QUAD + 4 * WIN]
        both = jnp.concatenate([datt[rows], drop[rows]], axis=1)
        ds = (e.astype(F32) * dot_nt(both, stack_values(v[rows]))).astype(BF)
        dqs.append(dot(ds, stack_heads(k[rows])))
        dks.append(unstack_heads(dot_tn(ds, q[rows])))
        dvs.append(unstack_heads(dot_tn(e, datt[rows])))
    dq = 10.0 * jnp.concatenate(dqs, axis=0)
    dk = (1.0 / LOG2E) * jnp.concatenate(dks, axis=0)
    dv = jnp.concatenate(dvs, axis=0)
    q_unit = q.astype(F32) * (1.0 / SCALE)
    k_unit = k.astype(F32)
    dq = part(5).astype(F32) * (dq - q_unit * head_sums(q_unit * dq, blocks))
    dk = part(6).astype(F32) * (dk - k_unit * head_sums(k_unit * dk, blocks))
    dqkv = jnp.concatenate([dq.astype(BF), dk.astype(BF), dv.astype(BF)], axis=1)
    return g + dot_nt(dqkv, w_qkv)


def teacher_first(
    x_hbm, far_ref, reg_ref, to_a_hbm, a_row_hbm, a_col_hbm, a_to_g_hbm, t_qkv, t_out,
    h_ref, id_ref, g_ref, north_ref, south_ref,
    pad_ref, x_ref, to_a, a_row, a_col, a_to_g, wqkv, wout, sems,
):
    copies = fetch(
        (x_hbm, x_ref, sems.at[0]),
        (to_a_hbm, to_a, sems.at[1]),
        (t_qkv.at[0], wqkv, sems.at[2]),
        (a_row_hbm, a_row, sems.at[3]),
        (a_col_hbm, a_col, sems.at[4]),
        (t_out.at[0], wout, sems.at[5]),
        (a_to_g_hbm, a_to_g, sems.at[6]),
    )
    width = x_ref.shape[3]
    blocks = head_blocks()
    copies[0].wait()
    copies[1].wait()
    x = to_window_order(x_ref, pad_ref, to_a[...])
    far = to_window_order(far_ref, pad_ref, to_a[...])
    copies[3].wait()
    copies[4].wait()
    reg, reg_far = by_level(reg_ref)
    ids = window_ids(reg, a_row[...], a_col[...])
    ids_far = window_ids(reg_far, a_row[...], a_col[...])
    id_ref[...] = ids
    copies[2].wait()
    q = (unit(dot(x, wqkv[:, :width]), blocks)[0] * SCALE).astype(BF)
    rows = jnp.concatenate([x, far], axis=0)
    k = unit(dot(rows, wqkv[:, width : 2 * width]), blocks)[0].astype(BF)
    v = dot(rows, wqkv[:, 2 * width :]).astype(BF)
    atts = []
    for w in range(4):
        near_rows = slice(w * WIN, (w + 1) * WIN)
        far_rows = slice(NA + w * WIN, NA + (w + 1) * WIN)
        id_keys = jnp.concatenate([ids[near_rows], ids_far[near_rows]], axis=0)
        mask = id_mask(ids[near_rows], id_keys)
        quads = []
        for i in range(0, width, QUAD):
            lanes = slice(i, i + QUAD)
            num, den, _ = attend(
                q[near_rows, lanes],
                jnp.concatenate([k[near_rows, lanes], k[far_rows, lanes]], axis=0),
                jnp.concatenate([v[near_rows, lanes], v[far_rows, lanes]], axis=0),
                mask,
            )
            quads.append((num / den).astype(BF))
        atts.append(jnp.concatenate(quads, axis=1))
    copies[5].wait()
    h = residual(x, jnp.concatenate(atts, axis=0), wout[...])[0]
    h_ref[...] = h
    copies[6].wait()
    spread = dot(a_to_g[...], jnp.concatenate([h, ids], axis=1)).astype(BF)
    g_ref[...] = spread
    put(north_ref, [part(spread, n) for n in TO_NORTH])
    put(south_ref, [part(spread, n) for n in TO_SOUTH])


def part(x, name):
    start, kept = AT[name]
    return x[start : start + kept]


def put(ref, blocks):
    spot = 0
    for block in blocks:
        ref[spot : spot + block.shape[0]] = block
        spot += block.shape[0]


TO_NORTH = ("nw", "n", "ne")
TO_SOUTH = ("sw", "s", "se")
TO_WEST = (("N", "sw"), ("", "nw"), ("", "w"), ("", "sw"), ("S", "nw"))
TO_EAST = (("N", "se"), ("", "ne"), ("", "e"), ("", "se"), ("S", "ne"))
EXTRA = {
    "nw": (("N", "sw"), ("W", "ne"), ("NW", "se")),
    "n": (("N", "s"),),
    "ne": (("N", "se"), ("E", "nw"), ("NE", "sw")),
    "e": (("E", "w"),),
    "se": (("S", "ne"), ("E", "sw"), ("SE", "nw")),
    "s": (("S", "n"),),
    "sw": (("S", "nw"), ("W", "se"), ("SW", "ne")),
    "w": (("W", "e"),),
    "c": (),
}
EARLY = ("n", "c", "s")
LATE = ("nw", "ne", "e", "se", "sw", "w")
ORDER = [name for name, *_ in PARTS]


def _spots(items, start):
    spots = {}
    for side, name in items:
        spots[side, name] = start
        start += AT[name][1]
    return spots, start


KNOWN, NK = _spots([("N", n) for n in TO_SOUTH] + [("S", n) for n in TO_NORTH], NG)
KNOWN.update({("", n): AT[n][0] for n in ORDER})
_come = [((s + "E"), n) for s, n in TO_WEST] + [((s + "W"), n) for s, n in TO_EAST]
COME, NC = _spots(_come, 0)


def send_columns(g_ref, north_ref, south_ref, after_ref, west_ref, east_ref):
    def block(side, name):
        spot = KNOWN[side, name]
        kept = AT[name][1]
        if side == "N":
            return north_ref[spot - NG : spot - NG + kept]
        if side == "S":
            spot = spot - NG - north_ref.shape[0]
            return south_ref[spot : spot + kept]
        return g_ref[spot : spot + kept]

    put(west_ref, [block(*item) for item in TO_WEST])
    put(east_ref, [block(*item) for item in TO_EAST])


def window_attention(name, q, keys, mask_ids):
    k, v = keys
    mask = id_mask(*mask_ids)
    quads = []
    for i in range(0, q.shape[1], QUAD):
        lanes = slice(i, i + QUAD)
        num, den, _ = attend(q[:, lanes], k[:, lanes], v[:, lanes], mask)
        quads.append((num / den).astype(BF))
    return jnp.concatenate(quads, axis=1)


def gather(sources, items):
    blocks = []
    for side, name in items:
        for array, spots in sources:
            if (side, name) in spots:
                spot = spots[side, name]
                blocks.append(array[spot : spot + AT[name][1]])
                break
    return blocks[0] if len(blocks) == 1 else jnp.concatenate(blocks, axis=0)


def middle(
    h_ref, id_ref, s_qkv, s_out, proj, g_ref, north_ref, south_ref, t_qkv, after_ref,
    g0_ref, save_ref, q_ref, k_ref, v_ref, att_ref,
):
    width = g_ref.shape[1] - 128
    blocks = head_blocks()
    known = jnp.concatenate([g_ref[...], north_ref[...], south_ref[...]], axis=0)
    rows, ids = known[:, :width], known[:, width:]
    q = (unit(dot(rows[:NG], t_qkv[1, :, :width]), blocks)[0] * SCALE).astype(BF)
    k = unit(dot(rows, t_qkv[1, :, width : 2 * width]), blocks)[0].astype(BF)
    v = dot(rows, t_qkv[1, :, 2 * width :]).astype(BF)
    q_ref[...] = q
    k_ref[...] = k
    v_ref[...] = v
    for name in EARLY:
        items = (("", name),) + EXTRA[name]
        keys = [gather([(x, KNOWN)], items) for x in (k, v)]
        start, kept = AT[name]
        att_ref[start : start + kept] = window_attention(
            name, part(q, name), keys, (part(ids, name), gather([(ids, KNOWN)], items))
        )
    for name in LATE:
        start, kept = AT[name]
        att_ref[start : start + kept] = jnp.zeros((kept, width), BF)

    h = student_layer(h_ref[...], s_qkv[1], s_out[1], id_ref[...], save_ref)
    predicted = dot(h, proj[...])
    g0_ref[...] = dot_nt(predicted.astype(BF), proj[...])


def teacher_second(
    h_ref, g_ref, north_ref, south_ref, east_ref, west_ref, q_ref, k_ref, v_ref, att_ref,
    from_a, g_to_a, t_qkv, t_out, proj, s_qkv, s_out, g0_ref, save0, save1, out_ref, grad_ref,
):
    width = h_ref.shape[1]
    blocks = head_blocks()
    came = jnp.concatenate([east_ref[...], west_ref[...]], axis=0)
    rows = came[:, :width]
    k = unit(dot(rows, t_qkv[1, :, width : 2 * width]), blocks)[0].astype(BF)
    v = dot(rows, t_qkv[1, :, 2 * width :]).astype(BF)
    known_ids = jnp.concatenate(
        [g_ref[:, width:], north_ref[:, width:], south_ref[:, width:]], axis=0
    )
    atts = {name: part(att_ref, name) for name in EARLY}
    for name in LATE:
        items = (("", name),) + EXTRA[name]
        keys = [gather([(x, COME), (y, KNOWN)], items) for x, y in ((k, k_ref), (v, v_ref))]
        id_keys = gather([(came[:, width:], COME), (known_ids, KNOWN)], items)
        atts[name] = window_attention(
            name, part(q_ref, name), keys, (part(known_ids, name), id_keys)
        )
    att = jnp.concatenate([atts[name] for name in ORDER], axis=0)
    att = dot(g_to_a[...], att).astype(BF)
    teacher = residual(h_ref[...], att, t_out[1])[0]
    natural = dot(from_a[...], teacher).astype(BF)
    out_ref[0] = natural.reshape(COLS, TALL, width)[:, :ROWS, :]

    g = g0_ref[...] - dot_nt(teacher, proj[...])
    g = student_back(g, save1, s_qkv[1], s_out[1])
    g = student_back(g, save0, s_qkv[0], s_out[0])
    high = g.astype(BF)
    low = (g - high.astype(F32)).astype(BF)
    natural = dot(from_a[...], high) + dot(from_a[...], low)
    grad_ref[0] = natural.reshape(COLS, TALL, g.shape[1])[:, :ROWS, :]


VMEM = pl.BlockSpec(memory_space=pltpu.VMEM)
ANY = pl.BlockSpec(memory_space=pl.ANY)
HBM = pl.BlockSpec(memory_space=pltpu.HBM)


def call(kernel, name, outs, specs, args, scratch=(), flops=0):
    shapes = [jax.ShapeDtypeStruct(s, d) for s, d in outs]
    touched = sum(a.size * a.dtype.itemsize for a in args)
    return pl.pallas_call(
        kernel,
        name=name,
        out_shape=shapes,
        in_specs=specs,
        out_specs=[VMEM] * len(outs),
        scratch_shapes=list(scratch),
        compiler_params=pltpu.CompilerParams(vmem_limit_bytes=28 << 20),
        cost_estimate=pl.CostEstimate(flops=flops, bytes_accessed=touched, transcendentals=0),
    )(*args)


def buffers(*arrays):
    return [pltpu.VMEM(a.shape, a.dtype) for a in arrays] + [
        pltpu.SemaphoreType.DMA((len(arrays),))
    ]


def shards(teacher_in, student_in, regions, t_qkv, t_out, s_qkv, s_out, s_proj):
    width, narrow = teacher_in.shape[3], student_in.shape[3]
    lat_size, lon_size = lax.axis_size("lat"), lax.axis_size("lon")
    wide = width + 128
    teacher_in = teacher_in.transpose(0, 2, 1, 3)
    student_in = student_in.transpose(0, 2, 1, 3)
    regions = regions.transpose(2, 0, 1)
    far = lax.ppermute(teacher_in, "grp", [(0, 1), (1, 0)])

    args = [teacher_in, far, regions, TO_A, A_ROW, A_COL, A_TO_G, t_qkv, t_out]
    row_count = sum(AT[n][1] for n in TO_NORTH)
    hidden, ids, spread, to_north, to_south = call(
        teacher_first, "teacher_first",
        [((NA, width), BF), ((NA, 128), BF), ((NG, wide), BF)] + [((row_count, wide), BF)] * 2,
        [HBM, VMEM, VMEM] + [HBM] * 6,
        args,
        [pltpu.VMEM((COLS, TALL, width), BF)]
        + buffers(teacher_in, TO_A, A_ROW, A_COL, A_TO_G, t_qkv[0], t_out[0]),
        4 * 10**9,
    )
    north = lax.ppermute(to_south, "lat", [(i, i + 1) for i in range(lat_size - 1)])
    south = lax.ppermute(to_north, "lat", [(i + 1, i) for i in range(lat_size - 1)])

    h1, save0 = call(
        student_first, "student_first",
        [((NA, narrow), BF), ((NA, SAVE), BF)],
        [VMEM] * 5 + [ANY],
        [student_in, ids, TO_A, s_qkv, s_out, to_north],
        [pltpu.VMEM((COLS, TALL, narrow), BF)], 10**9,
    )

    to_west, to_east = call(
        send_columns, "send_columns",
        [((NC // 2, wide), BF)] * 2,
        [VMEM] * 3 + [ANY],
        [spread, north, south, h1], (), 10**6,
    )
    east = lax.ppermute(to_west, "lon", [((j + 1) % lon_size, j) for j in range(lon_size)])
    west = lax.ppermute(to_east, "lon", [(j, (j + 1) % lon_size) for j in range(lon_size)])

    g0, save1, q, k, v, att = call(
        middle, "middle",
        [((NA, narrow), F32), ((NA, SAVE), BF)]
        + [((NG, width), BF), ((NK, width), BF), ((NK, width), BF), ((NG, width), BF)],
        [VMEM] * 9 + [ANY],
        [h1, ids, s_qkv, s_out, s_proj, spread, north, south, t_qkv, to_west],
        (), 4 * 10**9,
    )

    args = [hidden, spread, north, south, east, west, q, k, v, att, FROM_A, G_TO_A]
    args += [t_qkv, t_out, s_proj, s_qkv, s_out, g0, save0, save1]
    out, grad = call(
        teacher_second, "teacher_second",
        [(teacher_in.shape, BF), (student_in.shape, F32)],
        [VMEM] * len(args), args, (), 6 * 10**9,
    )
    return out.transpose(0, 2, 1, 3), grad.transpose(0, 2, 1, 3)


def solution(mesh):
    tiles = P("grp", "lat", "lon", None)
    return jax.shard_map(
        shards,
        mesh=mesh,
        in_specs=(tiles, tiles, P(None, "lat", "lon"), P(), P(), P(), P(), P()),
        out_specs=(tiles, tiles),
        check_vma=False,
    )
```

time: 69.1 us -> 66.5 us (0.962)
  the two profiles are of different devices: /device:TPU:6 before, /device:TPU:62 now
where the time goes in v1:
time: 66.5 us; the launch traced here: 66.1 us
  Pallas kernels  23.3 us (35%)
  waiting for transfers between devices  21.4 us (32%)
  starting transfers between devices  12.2 us (18%)
  local copies, waits for them, and re-layouts  8.51 us (13%)
  between operations  0.78 us (1%)
    pallas_call x5, Pallas kernels, call(): pl.pallas_call(kernel, name=name, out_shape=shapes, in_specs=specs, out_s...  23.3 us
    ppermute x1, waiting for transfers between devices, shards(): lax.ppermute(to_north, 'lat', [(i + 1, i) for i in range(lat_size - 1)])  15 us
    unnamed x32, local copies, waits for them, and re-layouts  8.51 us
    ppermute x1, starting transfers between devices, shards(): lax.ppermute(to_south, 'lat', [(i, i + 1) for i in range(lat_size - 1)])  8.11 us
    ppermute x1, waiting for transfers between devices, shards(): lax.ppermute(to_south, 'lat', [(i, i + 1) for i in range(lat_size - 1)])  2.48 us
    ppermute x1, waiting for transfers between devices, shards(): lax.ppermute(to_west, 'lon', [((j + 1) % lon_size, j) for j in range(lon_...  2.15 us
    ppermute x1, starting transfers between devices, shards(): lax.ppermute(to_west, 'lon', [((j + 1) % lon_size, j) for j in range(lon_...  1.98 us
    ppermute x1, starting transfers between devices, shards(): lax.ppermute(to_north, 'lat', [(i + 1, i) for i in range(lat_size - 1)])  1.92 us
  transfers between devices with their start and end apart: 5, of which 4 were waited for; matrix products, arithmetic and copies ran while one was open for 0% of the time, Pallas kernels for 10%

profile of v1, /device:TPU:62, one launch (start us, length us, event | category | flops | bytes accessed | tf_op | source)
XLA Modules:
  0.0 66.1 jit_solution(8113557739433129700)
XLA Ops:
  0.6 0.1 collective-permute-start
  0.7 1.8 %collective-permute-done.far_ref = bf16[1,12,24,512]{3,2,1,0:T(8,128)(2,1)S(1)} collective-permute-done((bf16[1,12,24,512]{3,2,1,0:T(8,128)(2,1)}, bf16[1,12,24,512]{3,2,1,0:T(8,128)(2,1)S(1)}, u32[]{:S(2)}, u32[]{:S(2)}) %collective-permute-start) | collective-permute-done | bytes 294944 | tf_op jit(solution)/shard_map/ppermute | solution.py:476
  2.5 1.9 %copy-done = bf16[2,512,1536]{2,1,0:T(8,128)(2,1)S(1)} copy-done((bf16[2,512,1536]{2,1,0:T(8,128)(2,1)S(1)}, bf16[2,512,1536]{2,1,0:T(8,128)(2,1)}, u32[]{:S(2)}) %copy-start) | copy-done | bytes 3145752
  4.4 1.2 %copy-done.2 = bf16[2,512,512]{2,1,0:T(8,128)(2,1)S(1)} copy-done((bf16[2,512,512]{2,1,0:T(8,128)(2,1)S(1)}, bf16[2,512,512]{2,1,0:T(8,128)(2,1)}, u32[]{:S(2)}) %copy-start.2) | copy-done | bytes 1048600
  5.6 1.0 %copy-done.5 = bf16[1,24,12,512]{3,1,2,0:T(8,128)(2,1)S(1)} copy-done((bf16[1,24,12,512]{3,1,2,0:T(8,128)(2,1)S(1)}, bf16[1,24,12,512]{3,1,2,0:T(8,128)(2,1)}, u32[]{:S(2)}) %copy-start.5) | copy-done | bytes 294936
  6.6 0.7 %copy-done.9 = s32[2,24,12]{1,0,2:T(2,128)S(1)} copy-done((s32[2,24,12]{1,0,2:T(2,128)S(1)}, s32[2,24,12]{1,0,2:T(2,128)}, u32[]{:S(2)}) %copy-start.9) | copy-done | bytes 2328
  7.3 1.0 %copy-done.11 = bf16[400,320]{1,0:T(8,128)(2,1)S(1)} copy-done((bf16[400,320]{1,0:T(8,128)(2,1)S(1)}, bf16[400,320]{1,0:T(8,128)(2,1)}, u32[]{:S(2)}) %copy-start.11) | copy-done | bytes 256024
  8.3 0.9 %copy-done.13 = bf16[320,384]{1,0:T(8,128)(2,1)S(1)} copy-done((bf16[320,384]{1,0:T(8,128)(2,1)S(1)}, bf16[320,384]{1,0:T(8,128)(2,1)}, u32[]{:S(2)}) %copy-start.13) | copy-done | bytes 245784
  9.2 0.9 %copy-done.14 = bf16[320,12]{1,0:T(8,128)(2,1)S(1)} copy-done((bf16[320,12]{1,0:T(8,128)(2,1)S(1)}, bf16[320,12]{1,0:T(8,128)(2,1)}, u32[]{:S(2)}) %copy-start.14) | copy-done | bytes 7704
  10.1 0.9 %copy-done.15 = bf16[320,24]{1,0:T(8,128)(2,1)S(1)} copy-done((bf16[320,24]{1,0:T(8,128)(2,1)S(1)}, bf16[320,24]{1,0:T(8,128)(2,1)}, u32[]{:S(2)}) %copy-start.15) | copy-done | bytes 15384
  11.0 6.6 %teacher_first.1 = (bf16[320,512]{1,0:T(8,128)(2,1)S(1)}, bf16[320,128]{1,0:T(8,128)(2,1)S(1)}, bf16[400,640]{1,0:T(8,128)(2,1)S(1)}, bf16[112,640]{1,0:T(8,128)(2,1)S(1)}, bf16[112,640]{1,0:T(8,128)(2,1)S(1)}) custom-call(bf16[1,12,24,512]{3,2,1,0:T(8,128)(2,1)S(1)} %bitcast.6, bf16[1,12,24,512]{3,2,1,0:T(8,128)(2,1)S(1)} %collective-permute-done.far_ref, ...), custom_call_target="tpu_custom_call" | custom-call | flops 4000000000 | bytes 5311232 | tf_op jit(solution)/shard_map/teacher_first/pallas_call | solution.py:451
  17.6 8.1 %collective-permute-start.1 = (bf16[112,640]{1,0:T(8,128)(2,1)S(1)}, bf16[112,640]{1,0:T(8,128)(2,1)S(1)}, u32[]{:S(2)}, u32[]{:S(2)}) collective-permute-start(bf16[112,640]{1,0:T(8,128)(2,1)S(1)} %get-tuple-element.21), channel_id=1, source_target_pairs={{0,32},{32,64},{64,96},{96,128},{128,160},{160,192},{192,224},{1,3... | collective-permute-start | bytes 430088 | tf_op jit(solution)/shard_map/ppermute | solution.py:489
  25.7 1.9 %collective-permute-start.2 = (bf16[112,640]{1,0:T(8,128)(2,1)S(1)}, bf16[112,640]{1,0:T(8,128)(2,1)S(1)}, u32[]{:S(2)}, u32[]{:S(2)}) collective-permute-start(bf16[112,640]{1,0:T(8,128)(2,1)S(1)} %get-tuple-element.22.after_ref), channel_id=1, source_target_pairs={{32,0},{64,32},{96,64},{128,96},{160,128},{192,160},{224,192},{33,... | collective-permute-start | bytes 430088 | tf_op jit(solution)/shard_map/ppermute | solution.py:490
  27.6 0.0 copy-start.1
  27.7 1.9 %student_first.1 = (bf16[320,256]{1,0:T(8,128)(2,1)S(1)}, bf16[320,2688]{1,0:T(8,128)(2,1)S(1)}) custom-call(bf16[1,12,24,256]{3,2,1,0:T(8,128)(2,1)S(1)} %bitcast.7, bf16[320,128]{1,0:T(8,128)(2,1)S(1)} %get-tuple-element.23.id_ref, bf16[320,384]{1,0:T(8,128)(2,1)S(1)} %copy-done.13, bf16[2,256,768]{2,1,0:T(8,128)(2,1)S(1)} %copy-done.4, ...), custom_call_target="tpu_custom_call" | custom-call | flops 1000000000 | bytes 1667072 | tf_op jit(solution)/shard_map/student_first/pallas_call | solution.py:451
  29.6 2.5 %collective-permute-done.1.north_ref = bf16[112,640]{1,0:T(8,128)(2,1)S(1)} collective-permute-done((bf16[112,640]{1,0:T(8,128)(2,1)S(1)}, bf16[112,640]{1,0:T(8,128)(2,1)S(1)}, u32[]{:S(2)}, u32[]{:S(2)}) %collective-permute-start.1) | collective-permute-done | bytes 143392 | tf_op jit(solution)/shard_map/ppermute | solution.py:489
  32.1 15.0 %collective-permute-done.2.south_ref = bf16[112,640]{1,0:T(8,128)(2,1)S(1)} collective-permute-done((bf16[112,640]{1,0:T(8,128)(2,1)S(1)}, bf16[112,640]{1,0:T(8,128)(2,1)S(1)}, u32[]{:S(2)}, u32[]{:S(2)}) %collective-permute-start.2) | collective-permute-done | bytes 143392 | tf_op jit(solution)/shard_map/ppermute | solution.py:490
  47.1 0.1 collective-permute-start.4
  47.2 0.0 copy-start.10
  47.2 0.0 copy-start.12
  47.2 2.0 %collective-permute-start.3 = (bf16[176,640]{1,0:T(8,128)(2,1)S(1)}, bf16[176,640]{1,0:T(8,128)(2,1)S(1)}, u32[]{:S(2)}, u32[]{:S(2)}) collective-permute-start(bf16[176,640]{1,0:T(8,128)(2,1)S(1)} %get-tuple-element.25.after_ref), channel_id=1, source_target_pairs={{2,0},{4,2},{6,4},{8,6},{10,8},{12,10},{14,12},{16,14},{18,16},{20... | collective-permute-start | bytes 675848 | tf_op jit(solution)/shard_map/ppermute | solution.py:506
  49.2 4.7 %middle.1 = (f32[320,256]{1,0:T(8,128)S(1)}, bf16[320,2688]{1,0:T(8,128)(2,1)S(1)}, bf16[400,512]{1,0:T(8,128)(2,1)S(1)}, bf16[624,512]{1,0:T(8,128)(2,1)S(1)}, ...) custom-call(bf16[320,256]{1,0:T(8,128)(2,1)S(1)} %get-tuple-element.24.after_ref.h_ref, ...), custom_call_target="tpu_custom_call" | custom-call | flops 4000000000 | bytes 5726208 | tf_op jit(solution)/shard_map/middle/pallas_call | solution.py:451
  53.9 2.1 %collective-permute-done.3.east_ref = bf16[176,640]{1,0:T(8,128)(2,1)S(1)} collective-permute-done((bf16[176,640]{1,0:T(8,128)(2,1)S(1)}, bf16[176,640]{1,0:T(8,128)(2,1)S(1)}, u32[]{:S(2)}, u32[]{:S(2)}) %collective-permute-start.3) | collective-permute-done | bytes 225312 | tf_op jit(solution)/shard_map/ppermute | solution.py:506
  56.1 10.0 %teacher_second.1 = (bf16[1,12,24,512]{3,2,1,0:T(8,128)(2,1)}, f32[1,12,24,256]{3,2,1,0:T(8,128)}) custom-call(bf16[320,512]{1,0:T(8,128)(2,1)S(1)} %get-tuple-element.19.h_ref, bf16[400,640]{1,0:T(8,128)(2,1)S(1)} %get-tuple-element.20.g_ref, bf16[112,640]{1,0:T(8,128)(2,1)S(1)} %collective-permute-done.1.north_ref, ...), custom_call_target="tpu_custom_call" | custom-call | flops 6000000000 | bytes 13449216 | tf_op jit(solution)/shard_map/teacher_second/pallas_call | solution.py:451
  (23 shorter events, 0.1 us)
Async XLA Ops:
  0.6 1.9 %collective-permute-start = (bf16[1,12,24,512]{3,2,1,0:T(8,128)(2,1)}, bf16[1,12,24,512]{3,2,1,0:T(8,128)(2,1)S(1)}, u32[]{:S(2)}, u32[]{:S(2)}) collective-permute-start(bf16[1,12,24,512]{3,2,1,0:T(8,128)(2,1)} %bitcast.5), channel_id=1, source_target_pairs={{0,1},{1,0},{2,3},{3,2},{4,5},{5,4},{6,7},{7,6},{8,9},{9,8},{10,11... | collective-permute-start | bytes 884744 | tf_op jit(solution)/shard_map/ppermute | solution.py:476
  2.5 1.9 %copy-start = (bf16[2,512,1536]{2,1,0:T(8,128)(2,1)S(1)}, bf16[2,512,1536]{2,1,0:T(8,128)(2,1)}, u32[]{:S(2)}) copy-start(bf16[2,512,1536]{2,1,0:T(8,128)(2,1)} %t_qkv.5) | copy-start | bytes 9437188
  4.4 1.2 %copy-start.2 = (bf16[2,512,512]{2,1,0:T(8,128)(2,1)S(1)}, bf16[2,512,512]{2,1,0:T(8,128)(2,1)}, u32[]{:S(2)}) copy-start(bf16[2,512,512]{2,1,0:T(8,128)(2,1)} %t_out.3) | copy-start | bytes 3145732
  5.6 1.0 %copy-start.5 = (bf16[1,24,12,512]{3,1,2,0:T(8,128)(2,1)S(1)}, bf16[1,24,12,512]{3,1,2,0:T(8,128)(2,1)}, u32[]{:S(2)}) copy-start(bf16[1,24,12,512]{3,1,2,0:T(8,128)(2,1)} %param.14) | copy-start | bytes 884740
  6.6 0.7 %copy-start.9 = (s32[2,24,12]{1,0,2:T(2,128)S(1)}, s32[2,24,12]{1,0,2:T(2,128)}, u32[]{:S(2)}) copy-start(s32[2,24,12]{1,0,2:T(2,128)} %param.16) | copy-start | bytes 6916
  7.3 1.0 %copy-start.11 = (bf16[400,320]{1,0:T(8,128)(2,1)S(1)}, bf16[400,320]{1,0:T(8,128)(2,1)}, u32[]{:S(2)}) copy-start(bf16[400,320]{1,0:T(8,128)(2,1)} %constant.15.clone.a_to_g_hbm) | copy-start | bytes 768004
  8.3 0.9 %copy-start.13 = (bf16[320,384]{1,0:T(8,128)(2,1)S(1)}, bf16[320,384]{1,0:T(8,128)(2,1)}, u32[]{:S(2)}) copy-start(bf16[320,384]{1,0:T(8,128)(2,1)} %constant.12.clone.to_a_hbm.to_a) | copy-start | bytes 737284
  9.2 0.9 %copy-start.14 = (bf16[320,12]{1,0:T(8,128)(2,1)S(1)}, bf16[320,12]{1,0:T(8,128)(2,1)}, u32[]{:S(2)}) copy-start(bf16[320,12]{1,0:T(8,128)(2,1)} %constant.14.clone.a_col_hbm) | copy-start | bytes 23044
  10.1 0.9 %copy-start.15 = (bf16[320,24]{1,0:T(8,128)(2,1)S(1)}, bf16[320,24]{1,0:T(8,128)(2,1)}, u32[]{:S(2)}) copy-start(bf16[320,24]{1,0:T(8,128)(2,1)} %constant.13.clone.a_row_hbm) | copy-start | bytes 46084
  11.0 16.6 %copy-start.4 = (bf16[2,256,768]{2,1,0:T(8,128)(2,1)S(1)}, bf16[2,256,768]{2,1,0:T(8,128)(2,1)}, u32[]{:S(2)}) copy-start(bf16[2,256,768]{2,1,0:T(8,128)(2,1)} %s_qkv.5) | copy-start | bytes 2359300
  11.0 16.6 %copy-start.6 = (bf16[2,256,256]{2,1,0:T(8,128)(2,1)S(1)}, bf16[2,256,256]{2,1,0:T(8,128)(2,1)}, u32[]{:S(2)}) copy-start(bf16[2,256,256]{2,1,0:T(8,128)(2,1)} %s_out.5) | copy-start | bytes 786436
  11.0 16.6 %copy-start.8 = (bf16[1,24,12,256]{3,1,2,0:T(8,128)(2,1)S(1)}, bf16[1,24,12,256]{3,1,2,0:T(8,128)(2,1)}, u32[]{:S(2)}) copy-start(bf16[1,24,12,256]{3,1,2,0:T(8,128)(2,1)} %param.15) | copy-start | bytes 442372
  17.6 14.5 %collective-permute-start.1 = (bf16[112,640]{1,0:T(8,128)(2,1)S(1)}, bf16[112,640]{1,0:T(8,128)(2,1)S(1)}, u32[]{:S(2)}, u32[]{:S(2)}) collective-permute-start(bf16[112,640]{1,0:T(8,128)(2,1)S(1)} %get-tuple-element.21), channel_id=1, source_target_pairs={{0,32},{32,64},{64,96},{96,128},{128,160},{160,192},{192,224},{1,3... | collective-permute-start | bytes 430088 | tf_op jit(solution)/shard_map/ppermute | solution.py:489
  25.7 21.3 %collective-permute-start.2 = (bf16[112,640]{1,0:T(8,128)(2,1)S(1)}, bf16[112,640]{1,0:T(8,128)(2,1)S(1)}, u32[]{:S(2)}, u32[]{:S(2)}) collective-permute-start(bf16[112,640]{1,0:T(8,128)(2,1)S(1)} %get-tuple-element.22.after_ref), channel_id=1, source_target_pairs={{32,0},{64,32},{96,64},{128,96},{160,128},{192,160},{224,192},{33,... | collective-permute-start | bytes 430088 | tf_op jit(solution)/shard_map/ppermute | solution.py:490
  27.6 21.5 %copy-start.1 = (bf16[2,512,1536]{2,1,0:T(8,128)(2,1)S(1)}, bf16[2,512,1536]{2,1,0:T(8,128)(2,1)}, u32[]{:S(2)}) copy-start(bf16[2,512,1536]{2,1,0:T(8,128)(2,1)} %t_qkv.5) | copy-start | bytes 9437188
  27.6 21.5 %copy-start.7 = (bf16[256,512]{1,0:T(8,128)(2,1)S(1)}, bf16[256,512]{1,0:T(8,128)(2,1)}, u32[]{:S(2)}) copy-start(bf16[256,512]{1,0:T(8,128)(2,1)} %proj.3) | copy-start | bytes 786436
  47.1 6.9 %collective-permute-start.4 = (bf16[176,640]{1,0:T(8,128)(2,1)S(1)}, bf16[176,640]{1,0:T(8,128)(2,1)S(1)}, u32[]{:S(2)}, u32[]{:S(2)}) collective-permute-start(bf16[176,640]{1,0:T(8,128)(2,1)S(1)} %get-tuple-element.26), channel_id=1, source_target_pairs={{0,2},{2,4},{4,6},{6,8},{8,10},{10,12},{12,14},{14,16},{16,18},{18... | collective-permute-start | bytes 675848 | tf_op jit(solution)/shard_map/ppermute | solution.py:507
  47.1 8.9 %copy-start.3 = (bf16[2,512,512]{2,1,0:T(8,128)(2,1)S(1)}, bf16[2,512,512]{2,1,0:T(8,128)(2,1)}, u32[]{:S(2)}) copy-start(bf16[2,512,512]{2,1,0:T(8,128)(2,1)} %t_out.3) | copy-start | bytes 3145732
  47.2 8.9 %copy-start.10 = (bf16[320,400]{1,0:T(8,128)(2,1)S(1)}, bf16[320,400]{1,0:T(8,128)(2,1)}, u32[]{:S(2)}) copy-start(bf16[320,400]{1,0:T(8,128)(2,1)} %constant.17.clone.g_to_a) | copy-start | bytes 768004
  47.2 8.9 %copy-start.12 = (bf16[384,320]{1,0:T(8,128)(2,1)S(1)}, bf16[384,320]{1,0:T(8,128)(2,1)}, u32[]{:S(2)}) copy-start(bf16[384,320]{1,0:T(8,128)(2,1)} %constant.16.clone.from_a) | copy-start | bytes 737284
  47.2 8.9 %collective-permute-start.3 = (bf16[176,640]{1,0:T(8,128)(2,1)S(1)}, bf16[176,640]{1,0:T(8,128)(2,1)S(1)}, u32[]{:S(2)}, u32[]{:S(2)}) collective-permute-start(bf16[176,640]{1,0:T(8,128)(2,1)S(1)} %get-tuple-element.25.after_ref), channel_id=1, source_target_pairs={{2,0},{4,2},{6,4},{8,6},{10,8},{12,10},{14,12},{16,14},{18,16},{20... | collective-permute-start | bytes 675848 | tf_op jit(solution)/shard_map/ppermute | solution.py:506

commit v2 on v1

--- a/solution.py
+++ b/solution.py
@@ -69,6 +69,25 @@
 TO_A, A_ROW, A_COL, A_TO_G = _tables()
 FROM_A = np.ascontiguousarray(TO_A.T)
 G_TO_A = np.ascontiguousarray(A_TO_G.T)
+
+
+def _packing(kept):
+    table = np.zeros((128, sum(kept)), ml_dtypes.bfloat16)
+    token, start = 0, 0
+    for rows in kept:
+        count = {32: 18, 48: 36}[rows]
+        for i in range(count):
+            table[token + i, start + i] = 1
+        token, start = token + count, start + rows
+    return table
+
+
+PACK_ROWS = _packing((32, 48, 32))
+PACK_COLS = _packing((32, 32, 48, 32, 32))
+ROW_TOKENS, ROW_SENT = 72, 80
+COL_TOKENS, COL_SENT = 108, 112
+OPEN_ROWS = np.ascontiguousarray(PACK_ROWS.T[:, :ROW_SENT])
+OPEN_COLS = np.ascontiguousarray(PACK_COLS.T[:, :COL_SENT])
 
 
 def dot(a, b):
@@ -197,11 +216,6 @@
     for copy in copies:
         copy.start()
     return copies
-
-
-def student_first(x_ref, id_ref, to_a, s_qkv, s_out, after_ref, h_ref, save_ref, pad_ref):
-    x = to_window_order(x_ref, pad_ref, to_a[...])
-    h_ref[...] = student_layer(x, s_qkv[0], s_out[0], id_ref[...], save_ref)
 
 
 def student_back(g, save_ref, w_qkv, w_out):
@@ -233,74 +247,85 @@
     return g + dot_nt(dqkv, w_qkv)
 
 
-def teacher_first(
-    x_hbm, far_ref, reg_ref, to_a_hbm, a_row_hbm, a_col_hbm, a_to_g_hbm, t_qkv, t_out,
-    h_ref, id_ref, g_ref, north_ref, south_ref,
-    pad_ref, x_ref, to_a, a_row, a_col, a_to_g, wqkv, wout, sems,
+def teacher_own(
+    x_hbm, reg_hbm, to_a_hbm, a_row_hbm, a_col_hbm, t_qkv,
+    x_out, id_ref, far_id_ref, q_ref, k_ref, v_ref,
+    pad_ref, x_ref, reg_ref, to_a, a_row, a_col, wqkv, sems,
 ):
     copies = fetch(
         (x_hbm, x_ref, sems.at[0]),
-        (to_a_hbm, to_a, sems.at[1]),
-        (t_qkv.at[0], wqkv, sems.at[2]),
+        (to_a_hbm, to_a, sems.at[2]),
+        (reg_hbm, reg_ref, sems.at[1]),
         (a_row_hbm, a_row, sems.at[3]),
         (a_col_hbm, a_col, sems.at[4]),
-        (t_out.at[0], wout, sems.at[5]),
-        (a_to_g_hbm, a_to_g, sems.at[6]),
+        (t_qkv.at[0], wqkv, sems.at[5]),
     )
     width = x_ref.shape[3]
     blocks = head_blocks()
     copies[0].wait()
     copies[1].wait()
     x = to_window_order(x_ref, pad_ref, to_a[...])
+    x_out[...] = x
+    for copy in copies[2:5]:
+        copy.wait()
+    reg, reg_far = by_level(reg_ref)
+    id_ref[...] = window_ids(reg, a_row[...], a_col[...])
+    far_id_ref[...] = window_ids(reg_far, a_row[...], a_col[...])
+    copies[5].wait()
+    q_ref[...] = (unit(dot(x, wqkv[:, :width]), blocks)[0] * SCALE).astype(BF)
+    k_ref[...] = unit(dot(x, wqkv[:, width : 2 * width]), blocks)[0].astype(BF)
+    v_ref[...] = dot(x, wqkv[:, 2 * width :]).astype(BF)
+
+
+def teacher_first(
+    far_ref, x_ref, id_ref, far_id_ref, q_ref, k_ref, v_ref, to_a, a_to_g, pack, t_qkv, t_out,
+    h_ref, g_ref, north_ref, south_ref, pad_ref, wout, sems,
+):
+    copies = fetch((t_out.at[0], wout, sems.at[0]))
+    width = x_ref.shape[1]
+    blocks = head_blocks()
     far = to_window_order(far_ref, pad_ref, to_a[...])
-    copies[3].wait()
-    copies[4].wait()
-    reg, reg_far = by_level(reg_ref)
-    ids = window_ids(reg, a_row[...], a_col[...])
-    ids_far = window_ids(reg_far, a_row[...], a_col[...])
-    id_ref[...] = ids
-    copies[2].wait()
-    q = (unit(dot(x, wqkv[:, :width]), blocks)[0] * SCALE).astype(BF)
-    rows = jnp.concatenate([x, far], axis=0)
-    k = unit(dot(rows, wqkv[:, width : 2 * width]), blocks)[0].astype(BF)
-    v = dot(rows, wqkv[:, 2 * width :]).astype(BF)
+    k_far = unit(dot(far, t_qkv[0, :, width : 2 * width]), blocks)[0].astype(BF)
+    v_far = dot(far, t_qkv[0, :, 2 * width :]).astype(BF)
     atts = []
     for w in range(4):
-        near_rows = slice(w * WIN, (w + 1) * WIN)
-        far_rows = slice(NA + w * WIN, NA + (w + 1) * WIN)
-        id_keys = jnp.concatenate([ids[near_rows], ids_far[near_rows]], axis=0)
-        mask = id_mask(ids[near_rows], id_keys)
-        quads = []
-        for i in range(0, width, QUAD):
-            lanes = slice(i, i + QUAD)
-            num, den, _ = attend(
-                q[near_rows, lanes],
-                jnp.concatenate([k[near_rows, lanes], k[far_rows, lanes]], axis=0),
-                jnp.concatenate([v[near_rows, lanes], v[far_rows, lanes]], axis=0),
-                mask,
-            )
-            quads.append((num / den).astype(BF))
-        atts.append(jnp.concatenate(quads, axis=1))
-    copies[5].wait()
-    h = residual(x, jnp.concatenate(atts, axis=0), wout[...])[0]
+        rows = slice(w * WIN, (w + 1) * WIN)
+        id_keys = jnp.concatenate([id_ref[rows], far_id_ref[rows]], axis=0)
+        keys = [
+            jnp.concatenate([near[rows], away[rows]], axis=0)
+            for near, away in ((k_ref, k_far), (v_ref, v_far))
+        ]
+        atts.append(window_attention(q_ref[rows], keys, (id_ref[rows], id_keys)))
+    copies[0].wait()
+    h = residual(x_ref[...], jnp.concatenate(atts, axis=0), wout[...])[0]
     h_ref[...] = h
-    copies[6].wait()
-    spread = dot(a_to_g[...], jnp.concatenate([h, ids], axis=1)).astype(BF)
+    spread = dot(a_to_g[...], jnp.concatenate([h, id_ref[...]], axis=1)).astype(BF)
     g_ref[...] = spread
-    put(north_ref, [part(spread, n) for n in TO_NORTH])
-    put(south_ref, [part(spread, n) for n in TO_SOUTH])
+    for ref, names in ((north_ref, TO_NORTH), (south_ref, TO_SOUTH)):
+        rows = jnp.concatenate([part(spread, n) for n in names], axis=0)
+        ref[...] = packed(rows, pack[...], ROW_TOKENS, ROW_SENT)
+
+
+def packed(rows, table, tokens, sent):
+    width = rows.shape[1] - 128
+    values = dot(table[:sent], rows[:, :width])
+    ids = dot(table, rows[:, width:]).astype(BF)
+    row = dot_nt(jnp.full((8, 128), 1.0 / 128, BF), ids)[0:1]
+    row = jnp.concatenate([row, jnp.zeros((1, width - 128), F32)], axis=1)
+    at = lax.broadcasted_iota(jnp.int32, (sent, 1), 0)
+    return jnp.where(at == tokens, row, values).astype(BF)
+
+
+def opened(sent, table, tokens):
+    values = dot(table, sent).astype(BF)
+    row = sent.astype(F32)[tokens : tokens + 1, : table.shape[1]]
+    ids = dot((table.astype(F32) * row).astype(BF), jnp.ones((table.shape[1], 128), BF))
+    return jnp.concatenate([values, ids.astype(BF)], axis=1)
 
 
 def part(x, name):
     start, kept = AT[name]
     return x[start : start + kept]
-
-
-def put(ref, blocks):
-    spot = 0
-    for block in blocks:
-        ref[spot : spot + block.shape[0]] = block
-        spot += block.shape[0]
 
 
 TO_NORTH = ("nw", "n", "ne")
@@ -318,43 +343,38 @@
     "w": (("W", "e"),),
     "c": (),
 }
-EARLY = ("n", "c", "s")
 LATE = ("nw", "ne", "e", "se", "sw", "w")
 ORDER = [name for name, *_ in PARTS]
 
 
-def _spots(items, start):
-    spots = {}
+def _spots(items):
+    spots, start = {}, 0
     for side, name in items:
         spots[side, name] = start
         start += AT[name][1]
-    return spots, start
-
-
-KNOWN, NK = _spots([("N", n) for n in TO_SOUTH] + [("S", n) for n in TO_NORTH], NG)
-KNOWN.update({("", n): AT[n][0] for n in ORDER})
-_come = [((s + "E"), n) for s, n in TO_WEST] + [((s + "W"), n) for s, n in TO_EAST]
-COME, NC = _spots(_come, 0)
-
-
-def send_columns(g_ref, north_ref, south_ref, after_ref, west_ref, east_ref):
-    def block(side, name):
-        spot = KNOWN[side, name]
-        kept = AT[name][1]
-        if side == "N":
-            return north_ref[spot - NG : spot - NG + kept]
-        if side == "S":
-            spot = spot - NG - north_ref.shape[0]
-            return south_ref[spot : spot + kept]
-        return g_ref[spot : spot + kept]
-
-    put(west_ref, [block(*item) for item in TO_WEST])
-    put(east_ref, [block(*item) for item in TO_EAST])
-
-
-def window_attention(name, q, keys, mask_ids):
+    return spots
+
+
+OWN = {("", name): AT[name][0] for name in ORDER}
+EDGE = _spots([("N", n) for n in TO_SOUTH] + [("S", n) for n in TO_NORTH])
+COME = _spots([(s + "E", n) for s, n in TO_WEST] + [(s + "W", n) for s, n in TO_EAST])
+NE_ROWS = 2 * sum(AT[n][1] for n in TO_NORTH)
+
+
+def gather(sources, items):
+    blocks = []
+    for item in items:
+        for array, spots in sources:
+            if item in spots:
+                spot = spots[item]
+                blocks.append(array[spot : spot + AT[item[1]][1]])
+                break
+    return blocks[0] if len(blocks) == 1 else jnp.concatenate(blocks, axis=0)
+
+
+def window_attention(q, keys, ids):
     k, v = keys
-    mask = id_mask(*mask_ids)
+    mask = id_mask(*ids)
     quads = []
     for i in range(0, q.shape[1], QUAD):
         lanes = slice(i, i + QUAD)
@@ -363,68 +383,88 @@
     return jnp.concatenate(quads, axis=1)
 
 
-def gather(sources, items):
-    blocks = []
-    for side, name in items:
-        for array, spots in sources:
-            if (side, name) in spots:
-                spot = spots[side, name]
-                blocks.append(array[spot : spot + AT[name][1]])
-                break
-    return blocks[0] if len(blocks) == 1 else jnp.concatenate(blocks, axis=0)
-
-
-def middle(
-    h_ref, id_ref, s_qkv, s_out, proj, g_ref, north_ref, south_ref, t_qkv, after_ref,
-    g0_ref, save_ref, q_ref, k_ref, v_ref, att_ref,
+def beside_rows(
+    x_ref, id_ref, to_a, s_qkv, s_out, proj, g_ref, t_qkv, after_ref,
+    g0_ref, save0, save1, q_ref, k_ref, v_ref, att_ref, pad_ref,
 ):
     width = g_ref.shape[1] - 128
     blocks = head_blocks()
-    known = jnp.concatenate([g_ref[...], north_ref[...], south_ref[...]], axis=0)
-    rows, ids = known[:, :width], known[:, width:]
-    q = (unit(dot(rows[:NG], t_qkv[1, :, :width]), blocks)[0] * SCALE).astype(BF)
+    x = to_window_order(x_ref, pad_ref, to_a[...])
+    h = student_layer(x, s_qkv[0], s_out[0], id_ref[...], save0)
+    h = student_layer(h, s_qkv[1], s_out[1], id_ref[...], save1)
+    predicted = dot(h, proj[...])
+    g0_ref[...] = dot_nt(predicted.astype(BF), proj[...])
+
+    rows = g_ref[:, :width]
+    q = (unit(dot(rows, t_qkv[1, :, :width]), blocks)[0] * SCALE).astype(BF)
     k = unit(dot(rows, t_qkv[1, :, width : 2 * width]), blocks)[0].astype(BF)
     v = dot(rows, t_qkv[1, :, 2 * width :]).astype(BF)
     q_ref[...] = q
     k_ref[...] = k
     v_ref[...] = v
-    for name in EARLY:
+    ids = part(g_ref, "c")[:, width:]
+    att_ref[...] = window_attention(part(q, "c"), [part(k, "c"), part(v, "c")], (ids, ids))
+
+
+def send_columns(
+    g_ref, north_ref, south_ref, open_rows, pack, after_ref, edge_ref, west_ref, east_ref
+):
+    width = north_ref.shape[1]
+    lat = lax.axis_index("lat")
+    blocks = []
+    inside = (lat > 0, lat < lax.axis_size("lat") - 1)
+    for ref, there in zip((north_ref, south_ref), inside):
+        rows = opened(ref[...], open_rows[...], ROW_TOKENS)
+        ids = rows[:, width:] * jnp.where(there, 1.0, 0.0).astype(BF)
+        blocks.append(jnp.concatenate([rows[:, :width], ids], axis=1))
+    edge = jnp.concatenate(blocks, axis=0)
+    edge_ref[...] = edge
+    for ref, items in ((west_ref, TO_WEST), (east_ref, TO_EAST)):
+        rows = gather([(g_ref, OWN), (edge, EDGE)], items)
+        ref[...] = packed(rows, pack[...], COL_TOKENS, COL_SENT)
+
+
+def beside_columns(
+    g_ref, edge_ref, t_qkv, q_ref, k_ref, v_ref, after_ref, k_out, v_out, n_ref, s_ref
+):
+    width = g_ref.shape[1] - 128
+    blocks = head_blocks()
+    rows = edge_ref[:, :width]
+    k = unit(dot(rows, t_qkv[1, :, width : 2 * width]), blocks)[0].astype(BF)
+    v = dot(rows, t_qkv[1, :, 2 * width :]).astype(BF)
+    k_out[...] = k
+    v_out[...] = v
+    for name, ref in (("n", n_ref), ("s", s_ref)):
         items = (("", name),) + EXTRA[name]
-        keys = [gather([(x, KNOWN)], items) for x in (k, v)]
-        start, kept = AT[name]
-        att_ref[start : start + kept] = window_attention(
-            name, part(q, name), keys, (part(ids, name), gather([(ids, KNOWN)], items))
-        )
-    for name in LATE:
-        start, kept = AT[name]
-        att_ref[start : start + kept] = jnp.zeros((kept, width), BF)
-
-    h = student_layer(h_ref[...], s_qkv[1], s_out[1], id_ref[...], save_ref)
-    predicted = dot(h, proj[...])
-    g0_ref[...] = dot_nt(predicted.astype(BF), proj[...])
+        keys = [gather([(own, OWN), (edge, EDGE)], items) for own, edge in ((k_ref, k), (v_ref, v))]
+        ids = [gather([(g_ref, OWN), (edge_ref, EDGE)], some)[:, width:] for some in (items[:1], items)]
+        ref[...] = window_attention(part(q_ref, name), keys, ids)
 
 
 def teacher_second(
-    h_ref, g_ref, north_ref, south_ref, east_ref, west_ref, q_ref, k_ref, v_ref, att_ref,
-    from_a, g_to_a, t_qkv, t_out, proj, s_qkv, s_out, g0_ref, save0, save1, out_ref, grad_ref,
+    h_ref, g_ref, edge_ref, east_ref, west_ref, q_ref, k_ref, v_ref, k_edge, v_edge,
+    c_ref, n_ref, s_ref, open_cols, from_a, g_to_a, t_qkv, t_out, proj, s_qkv, s_out,
+    g0_ref, save0, save1, out_ref, grad_ref,
 ):
     width = h_ref.shape[1]
     blocks = head_blocks()
-    came = jnp.concatenate([east_ref[...], west_ref[...]], axis=0)
+    came = [opened(ref[...], open_cols[...], COL_TOKENS) for ref in (east_ref, west_ref)]
+    came = jnp.concatenate(came, axis=0)
     rows = came[:, :width]
     k = unit(dot(rows, t_qkv[1, :, width : 2 * width]), blocks)[0].astype(BF)
     v = dot(rows, t_qkv[1, :, 2 * width :]).astype(BF)
-    known_ids = jnp.concatenate(
-        [g_ref[:, width:], north_ref[:, width:], south_ref[:, width:]], axis=0
-    )
-    atts = {name: part(att_ref, name) for name in EARLY}
+    atts = {"c": c_ref[...], "n": n_ref[...], "s": s_ref[...]}
     for name in LATE:
         items = (("", name),) + EXTRA[name]
-        keys = [gather([(x, COME), (y, KNOWN)], items) for x, y in ((k, k_ref), (v, v_ref))]
-        id_keys = gather([(came[:, width:], COME), (known_ids, KNOWN)], items)
-        atts[name] = window_attention(
-            name, part(q_ref, name), keys, (part(known_ids, name), id_keys)
-        )
+        keys = [
+            gather([(own, OWN), (edge, EDGE), (new, COME)], items)
+            for own, edge, new in ((k_ref, k_edge, k), (v_ref, v_edge, v))
+        ]
+        ids = [
+            gather([(g_ref, OWN), (edge_ref, EDGE), (came, COME)], some)[:, width:]
+            for some in (items[:1], items)
+        ]
+        atts[name] = window_attention(part(q_ref, name), keys, ids)
     att = jnp.concatenate([atts[name] for name in ORDER], axis=0)
     att = dot(g_to_a[...], att).astype(BF)
     teacher = residual(h_ref[...], att, t_out[1])[0]
@@ -475,48 +515,54 @@
     regions = regions.transpose(2, 0, 1)
     far = lax.ppermute(teacher_in, "grp", [(0, 1), (1, 0)])
 
-    args = [teacher_in, far, regions, TO_A, A_ROW, A_COL, A_TO_G, t_qkv, t_out]
-    row_count = sum(AT[n][1] for n in TO_NORTH)
-    hidden, ids, spread, to_north, to_south = call(
+    pinned = [
+        pltpu.with_memory_space_constraint(jnp.asarray(a), pltpu.HBM)
+        for a in (teacher_in, regions, TO_A, A_ROW, A_COL, t_qkv)
+    ]
+    x, ids, far_ids, q, k, v = call(
+        teacher_own, "teacher_own",
+        [((NA, width), BF), ((NA, 128), BF), ((NA, 128), BF)] + [((NA, width), BF)] * 3,
+        [HBM] * 6, pinned,
+        [pltpu.VMEM((COLS, TALL, width), BF)]
+        + buffers(teacher_in, regions, TO_A, A_ROW, A_COL, t_qkv[0]),
+        10**9,
+    )
+    hidden, spread, to_north, to_south = call(
         teacher_first, "teacher_first",
-        [((NA, width), BF), ((NA, 128), BF), ((NG, wide), BF)] + [((row_count, wide), BF)] * 2,
-        [HBM, VMEM, VMEM] + [HBM] * 6,
-        args,
-        [pltpu.VMEM((COLS, TALL, width), BF)]
-        + buffers(teacher_in, TO_A, A_ROW, A_COL, A_TO_G, t_qkv[0], t_out[0]),
-        4 * 10**9,
-    )
-    north = lax.ppermute(to_south, "lat", [(i, i + 1) for i in range(lat_size - 1)])
-    south = lax.ppermute(to_north, "lat", [(i + 1, i) for i in range(lat_size - 1)])
-
-    h1, save0 = call(
-        student_first, "student_first",
-        [((NA, narrow), BF), ((NA, SAVE), BF)],
+        [((NA, width), BF), ((NG, wide), BF)] + [((ROW_SENT, width), BF)] * 2,
+        [VMEM] * 11 + [HBM],
+        [far, x, ids, far_ids, q, k, v, TO_A, A_TO_G, PACK_ROWS, t_qkv]
+        + [pltpu.with_memory_space_constraint(t_out, pltpu.HBM)],
+        [pltpu.VMEM((COLS, TALL, width), BF)] + buffers(t_out[0]), 3 * 10**9,
+    )
+    north = lax.ppermute(to_south, "lat", [(i, (i + 1) % lat_size) for i in range(lat_size)])
+    south = lax.ppermute(to_north, "lat", [((i + 1) % lat_size, i) for i in range(lat_size)])
+
+    g0, save0, save1, q, k, v, c_att = call(
+        beside_rows, "beside_rows",
+        [((NA, narrow), F32), ((NA, SAVE), BF), ((NA, SAVE), BF)]
+        + [((NG, width), BF)] * 3 + [((AT["c"][1], width), BF)],
+        [VMEM] * 8 + [ANY],
+        [student_in, ids, TO_A, s_qkv, s_out, s_proj, spread, t_qkv, to_north],
+        [pltpu.VMEM((COLS, TALL, narrow), BF)], 5 * 10**9,
+    )
+    edge, to_west, to_east = call(
+        send_columns, "send_columns",
+        [((NE_ROWS, wide), BF)] + [((COL_SENT, width), BF)] * 2,
         [VMEM] * 5 + [ANY],
-        [student_in, ids, TO_A, s_qkv, s_out, to_north],
-        [pltpu.VMEM((COLS, TALL, narrow), BF)], 10**9,
-    )
-
-    to_west, to_east = call(
-        send_columns, "send_columns",
-        [((NC // 2, wide), BF)] * 2,
-        [VMEM] * 3 + [ANY],
-        [spread, north, south, h1], (), 10**6,
+        [spread, north, south, OPEN_ROWS, PACK_COLS, g0], (), 10**7,
     )
     east = lax.ppermute(to_west, "lon", [((j + 1) % lon_size, j) for j in range(lon_size)])
     west = lax.ppermute(to_east, "lon", [(j, (j + 1) % lon_size) for j in range(lon_size)])
 
-    g0, save1, q, k, v, att = call(
-        middle, "middle",
-        [((NA, narrow), F32), ((NA, SAVE), BF)]
-        + [((NG, width), BF), ((NK, width), BF), ((NK, width), BF), ((NG, width), BF)],
-        [VMEM] * 9 + [ANY],
-        [h1, ids, s_qkv, s_out, s_proj, spread, north, south, t_qkv, to_west],
-        (), 4 * 10**9,
-    )
-
-    args = [hidden, spread, north, south, east, west, q, k, v, att, FROM_A, G_TO_A]
-    args += [t_qkv, t_out, s_proj, s_qkv, s_out, g0, save0, save1]
+    k_edge, v_edge, n_att, s_att = call(
+        beside_columns, "beside_columns",
+        [((NE_ROWS, width), BF)] * 2 + [((AT["n"][1], width), BF)] * 2,
+        [VMEM] * 6 + [ANY],
+        [spread, edge, t_qkv, q, k, v, to_west], (), 2 * 10**9,
+    )
+    args = [hidden, spread, edge, east, west, q, k, v, k_edge, v_edge, c_att, n_att, s_att]
+    args += [OPEN_COLS, FROM_A, G_TO_A, t_qkv, t_out, s_proj, s_qkv, s_out, g0, save0, save1]
     out, grad = call(
         teacher_second, "teacher_second",
         [(teacher_in.shape, BF), (student_in.shape, F32)],

time: 66.5 us -> 47.4 us (0.71)
  the two profiles are of different devices: /device:TPU:62 before, /device:TPU:6 now
where the time goes in v2:
time: 47.4 us; the launch traced here: 46.8 us
  Pallas kernels  26 us (55%)
  starting transfers between devices  13.2 us (28%)
  waiting for transfers between devices  6.69 us (14%)
  between operations  0.84 us (2%)
    pallas_call x6, Pallas kernels, call(): pl.pallas_call(kernel, name=name, out_shape=shapes, in_specs=specs, out_s...  26 us
    ppermute x1, starting transfers between devices, shards(): lax.ppermute(to_south, 'lat', [(i, (i + 1) % lat_size) for i in range(lat...  7.19 us
    ppermute x1, waiting for transfers between devices, shards(): lax.ppermute(to_north, 'lat', [((i + 1) % lat_size, i) for i in range(lat...  5.43 us
    ppermute x1, starting transfers between devices, shards(): lax.ppermute(to_west, 'lon', [((j + 1) % lon_size, j) for j in range(lon_...  4.37 us
    ppermute x1, starting transfers between devices, shards(): lax.ppermute(to_east, 'lon', [(j, (j + 1) % lon_size) for j in range(lon_...  1.57 us
    ppermute x1, waiting for transfers between devices, shards(): lax.ppermute(to_east, 'lon', [(j, (j + 1) % lon_size) for j in range(lon_...  1.25 us
  transfers between devices with their start and end apart: 5, of which 2 were waited for; matrix products, arithmetic and copies ran while one was open for 0% of the time, Pallas kernels for 20%

profile of v2, /device:TPU:6, one launch (start us, length us, event | category | flops | bytes accessed | tf_op | source)
XLA Modules:
  0.0 46.8 jit_solution(1581371585085874474)
XLA Ops:
  0.6 0.1 collective-permute-start
  0.7 0.0 copy-start.1
  0.8 0.0 copy-start.10
  0.8 0.0 copy-start.13
  0.8 2.9 %teacher_own.1 = (bf16[320,512]{1,0:T(8,128)(2,1)S(1)}, bf16[320,128]{1,0:T(8,128)(2,1)S(1)}, bf16[320,128]{1,0:T(8,128)(2,1)S(1)}, bf16[320,512]{1,0:T(8,128)(2...) custom-call(bf16[1,12,24,512]{3,2,1,0:T(8,128)(2,1)} %bitcast.7, s32[12,2,24]{2,1,0:T(2,128)} %bitcast.8, ...), custom_call_target="tpu_custom_call" | custom-call | flops 1000000000 | bytes 3711744 | tf_op jit(solution)/shard_map/teacher_own/pallas_call | solution.py:491
  3.7 0.0 collective-permute-done.far_ref
  3.7 0.0 copy-start.5
  3.8 0.0 copy-start.6
  3.8 0.0 copy-start.7
  3.8 0.0 copy-start.8
  3.8 5.5 %teacher_first.1 = (bf16[320,512]{1,0:T(8,128)(2,1)S(1)}, bf16[400,640]{1,0:T(8,128)(2,1)S(1)}, bf16[80,512]{1,0:T(8,128)(2,1)S(1)}, bf16[80,512]{1,0:T(8,128)(2,1)S(1)}) custom-call(bf16[1,12,24,512]{3,2,1,0:T(8,128)(2,1)S(1)} %collective-permute-done.far_ref, bf16[320,512]{1,0:T(8,128)(2,1)S(1)} %get-tuple-element.28.x_ref, ...), custom_call_target="tpu_custom_call" | custom-call | flops 3000000000 | bytes 6494208 | tf_op jit(solution)/shard_map/teacher_first/pallas_call | solution.py:491
  9.3 7.2 %collective-permute-start.1 = (bf16[80,512]{1,0:T(8,128)(2,1)S(1)}, bf16[80,512]{1,0:T(8,128)(2,1)S(1)}, u32[]{:S(2)}, u32[]{:S(2)}) collective-permute-start(bf16[80,512]{1,0:T(8,128)(2,1)S(1)} %get-tuple-element.36), channel_id=1, source_target_pairs={{0,32},{32,64},{64,96},{96,128},{128,160},{160,192},{192,224},{224... | collective-permute-start | bytes 245768 | tf_op jit(solution)/shard_map/ppermute | solution.py:538
  16.5 0.0 collective-permute-start.2
  16.5 0.0 copy-start.2
  16.6 0.0 copy-start.3
  16.6 5.2 %beside_rows.1 = (f32[320,256]{1,0:T(8,128)S(1)}, bf16[320,2688]{1,0:T(8,128)(2,1)S(1)}, bf16[320,2688]{1,0:T(8,128)(2,1)S(1)}, bf16[400,512]{1,0:T(8,128)(2,1)S...) custom-call(bf16[1,12,24,256]{3,2,1,0:T(8,128)(2,1)S(1)} %bitcast.5, ...), custom_call_target="tpu_custom_call" | custom-call | flops 5000000000 | bytes 5525504 | tf_op jit(solution)/shard_map/beside_rows/pallas_call | solution.py:491
  21.7 0.0 collective-permute-done.1.north_ref
  21.7 5.4 %collective-permute-done.2.south_ref = bf16[80,512]{1,0:T(8,128)(2,1)S(1)} collective-permute-done((bf16[80,512]{1,0:T(8,128)(2,1)S(1)}, bf16[80,512]{1,0:T(8,128)(2,1)S(1)}, u32[]{:S(2)}, u32[]{:S(2)}) %collective-permute-start.2) | collective-permute-done | bytes 81952 | tf_op jit(solution)/shard_map/ppermute | solution.py:539
  27.2 0.7 %send_columns.1 = (bf16[224,640]{1,0:T(8,128)(2,1)S(1)}, bf16[112,512]{1,0:T(8,128)(2,1)S(1)}, bf16[112,512]{1,0:T(8,128)(2,1)S(1)}) custom-call(bf16[400,640]{1,0:T(8,128)(2,1)S(1)} %get-tuple-element.35.g_ref, bf16[80,512]{1,0:T(8,128)(2,1)S(1)} %collective-permute-done.1.north_ref, bf16[80,512]{1,0:T(8,128)(2,1)S(1)} %collective-permute-done.2.south_ref, ...), custom_call_target="tpu_custom_call" | custom-call | flops 10000000 | bytes 1066496 | tf_op jit(solution)/shard_map/send_columns/pallas_call | solution.py:491
  27.9 1.6 %collective-permute-start.4 = (bf16[112,512]{1,0:T(8,128)(2,1)S(1)}, bf16[112,512]{1,0:T(8,128)(2,1)S(1)}, u32[]{:S(2)}, u32[]{:S(2)}) collective-permute-start(bf16[112,512]{1,0:T(8,128)(2,1)S(1)} %get-tuple-element.41), channel_id=1, source_target_pairs={{0,2},{2,4},{4,6},{6,8},{8,10},{10,12},{12,14},{14,16},{16,18},{18... | collective-permute-start | bytes 344072 | tf_op jit(solution)/shard_map/ppermute | solution.py:556
  29.4 4.4 %collective-permute-start.3 = (bf16[112,512]{1,0:T(8,128)(2,1)S(1)}, bf16[112,512]{1,0:T(8,128)(2,1)S(1)}, u32[]{:S(2)}, u32[]{:S(2)}) collective-permute-start(bf16[112,512]{1,0:T(8,128)(2,1)S(1)} %get-tuple-element.40.after_ref), channel_id=1, source_target_pairs={{2,0},{4,2},{6,4},{8,6},{10,8},{12,10},{14,12},{16,14},{18,16},{20... | collective-permute-start | bytes 344072 | tf_op jit(solution)/shard_map/ppermute | solution.py:555
  33.8 1.5 %beside_columns.1 = (bf16[224,512]{1,0:T(8,128)(2,1)S(1)}, bf16[224,512]{1,0:T(8,128)(2,1)S(1)}, bf16[48,512]{1,0:T(8,128)(2,1)S(1)}, bf16[48,512]{1,0:T(8,128)(2,1)S(1)}) custom-call(bf16[400,640]{1,0:T(8,128)(2,1)S(1)} %get-tuple-element.35.g_ref, bf16[224,640]{1,0:T(8,128)(2,1)S(1)} %get-tuple-element.39.edge_ref, bf16[2,512,1536]{2,1,0:T(8,128)(2,1)S(1)} %copy-done, ...), custom_call_target="tpu_custom_call" | custom-call | flops 2000000000 | bytes 5287936 | tf_op jit(solution)/shard_map/beside_columns/pallas_call | solution.py:491
  35.3 1.3 %collective-permute-done.4.west_ref = bf16[112,512]{1,0:T(8,128)(2,1)S(1)} collective-permute-done((bf16[112,512]{1,0:T(8,128)(2,1)S(1)}, bf16[112,512]{1,0:T(8,128)(2,1)S(1)}, u32[]{:S(2)}, u32[]{:S(2)}) %collective-permute-start.4) | collective-permute-done | bytes 114720 | tf_op jit(solution)/shard_map/ppermute | solution.py:556
  36.6 10.2 %teacher_second.1 = (bf16[1,12,24,512]{3,2,1,0:T(8,128)(2,1)}, f32[1,12,24,256]{3,2,1,0:T(8,128)}) custom-call(bf16[320,512]{1,0:T(8,128)(2,1)S(1)} %get-tuple-element.34.h_ref, bf16[400,640]{1,0:T(8,128)(2,1)S(1)} %get-tuple-element.35.g_ref, bf16[224,640]{1,0:T(8,128)(2,1)S(1)} %get-tuple-element.39.edge_ref, ...), custom_call_target="tpu_custom_call" | custom-call | flops 6000000000 | bytes 13038080 | tf_op jit(solution)/shard_map/teacher_second/pallas_call | solution.py:491
  (20 shorter events, 0.0 us)
Async XLA Ops:
  0.6 3.1 %collective-permute-start = (bf16[1,12,24,512]{3,2,1,0:T(8,128)(2,1)}, bf16[1,12,24,512]{3,2,1,0:T(8,128)(2,1)S(1)}, u32[]{:S(2)}, u32[]{:S(2)}) collective-permute-start(bf16[1,12,24,512]{3,2,1,0:T(8,128)(2,1)} %bitcast.6), channel_id=1, source_target_pairs={{0,1},{1,0},{2,3},{3,2},{4,5},{5,4},{6,7},{7,6},{8,9},{9,8},{10,11... | collective-permute-start | bytes 884744 | tf_op jit(solution)/shard_map/ppermute | solution.py:516
  0.7 3.0 %copy-start = (bf16[2,512,1536]{2,1,0:T(8,128)(2,1)S(1)}, bf16[2,512,1536]{2,1,0:T(8,128)(2,1)}, u32[]{:S(2)}) copy-start(bf16[2,512,1536]{2,1,0:T(8,128)(2,1)} %t_qkv.9) | copy-start | bytes 9437188
  0.7 3.0 %copy-start.1 = (bf16[320,384]{1,0:T(8,128)(2,1)S(1)}, bf16[320,384]{1,0:T(8,128)(2,1)}, u32[]{:S(2)}) copy-start(bf16[320,384]{1,0:T(8,128)(2,1)} %constant.20.clone.to_a_hbm.to_a) | copy-start | bytes 737284
  0.8 3.0 %copy-start.10 = (bf16[400,320]{1,0:T(8,128)(2,1)S(1)}, bf16[400,320]{1,0:T(8,128)(2,1)}, u32[]{:S(2)}) copy-start(bf16[400,320]{1,0:T(8,128)(2,1)} %constant.23.clone.a_to_g) | copy-start | bytes 768004
  0.8 3.0 %copy-start.13 = (bf16[128,112]{1,0:T(8,128)(2,1)S(1)}, bf16[128,112]{1,0:T(8,128)(2,1)}, u32[]{:S(2)}) copy-start(bf16[128,112]{1,0:T(8,128)(2,1)} %constant.24.clone.pack) | copy-start | bytes 86020
  3.7 12.8 %copy-start.5 = (bf16[2,256,768]{2,1,0:T(8,128)(2,1)S(1)}, bf16[2,256,768]{2,1,0:T(8,128)(2,1)}, u32[]{:S(2)}) copy-start(bf16[2,256,768]{2,1,0:T(8,128)(2,1)} %s_qkv.3) | copy-start | bytes 2359300
  3.8 12.8 %copy-start.6 = (bf16[2,256,256]{2,1,0:T(8,128)(2,1)S(1)}, bf16[2,256,256]{2,1,0:T(8,128)(2,1)}, u32[]{:S(2)}) copy-start(bf16[2,256,256]{2,1,0:T(8,128)(2,1)} %s_out.3) | copy-start | bytes 786436
  3.8 12.8 %copy-start.7 = (bf16[256,512]{1,0:T(8,128)(2,1)S(1)}, bf16[256,512]{1,0:T(8,128)(2,1)}, u32[]{:S(2)}) copy-start(bf16[256,512]{1,0:T(8,128)(2,1)} %proj.3) | copy-start | bytes 786436
  3.8 12.8 %copy-start.8 = (bf16[1,24,12,256]{3,1,2,0:T(8,128)(2,1)S(1)}, bf16[1,24,12,256]{3,1,2,0:T(8,128)(2,1)}, u32[]{:S(2)}) copy-start(bf16[1,24,12,256]{3,1,2,0:T(8,128)(2,1)} %param.19) | copy-start | bytes 442372
  9.3 12.4 %collective-permute-start.1 = (bf16[80,512]{1,0:T(8,128)(2,1)S(1)}, bf16[80,512]{1,0:T(8,128)(2,1)S(1)}, u32[]{:S(2)}, u32[]{:S(2)}) collective-permute-start(bf16[80,512]{1,0:T(8,128)(2,1)S(1)} %get-tuple-element.36), channel_id=1, source_target_pairs={{0,32},{32,64},{64,96},{96,128},{128,160},{160,192},{192,224},{224... | collective-permute-start | bytes 245768 | tf_op jit(solution)/shard_map/ppermute | solution.py:538
  16.5 10.7 %collective-permute-start.2 = (bf16[80,512]{1,0:T(8,128)(2,1)S(1)}, bf16[80,512]{1,0:T(8,128)(2,1)S(1)}, u32[]{:S(2)}, u32[]{:S(2)}) collective-permute-start(bf16[80,512]{1,0:T(8,128)(2,1)S(1)} %get-tuple-element.37.after_ref), channel_id=1, source_target_pairs={{32,0},{64,32},{96,64},{128,96},{160,128},{192,160},{224,192},{0,2... | collective-permute-start | bytes 245768 | tf_op jit(solution)/shard_map/ppermute | solution.py:539
  16.5 10.6 %copy-start.2 = (bf16[128,176]{1,0:T(8,128)(2,1)S(1)}, bf16[128,176]{1,0:T(8,128)(2,1)}, u32[]{:S(2)}) copy-start(bf16[128,176]{1,0:T(8,128)(2,1)} %constant.26.clone.pack) | copy-start | bytes 135172
  16.6 10.6 %copy-start.3 = (bf16[112,80]{1,0:T(8,128)(2,1)S(1)}, bf16[112,80]{1,0:T(8,128)(2,1)}, u32[]{:S(2)}) copy-start(bf16[112,80]{1,0:T(8,128)(2,1)} %constant.25.clone.open_rows) | copy-start | bytes 53764
  27.9 8.7 %collective-permute-start.4 = (bf16[112,512]{1,0:T(8,128)(2,1)S(1)}, bf16[112,512]{1,0:T(8,128)(2,1)S(1)}, u32[]{:S(2)}, u32[]{:S(2)}) collective-permute-start(bf16[112,512]{1,0:T(8,128)(2,1)S(1)} %get-tuple-element.41), channel_id=1, source_target_pairs={{0,2},{2,4},{4,6},{6,8},{8,10},{10,12},{12,14},{14,16},{16,18},{18... | collective-permute-start | bytes 344072 | tf_op jit(solution)/shard_map/ppermute | solution.py:556
  29.4 7.1 %collective-permute-start.3 = (bf16[112,512]{1,0:T(8,128)(2,1)S(1)}, bf16[112,512]{1,0:T(8,128)(2,1)S(1)}, u32[]{:S(2)}, u32[]{:S(2)}) collective-permute-start(bf16[112,512]{1,0:T(8,128)(2,1)S(1)} %get-tuple-element.40.after_ref), channel_id=1, source_target_pairs={{2,0},{4,2},{6,4},{8,6},{10,8},{12,10},{14,12},{16,14},{18,16},{20... | collective-permute-start | bytes 344072 | tf_op jit(solution)/shard_map/ppermute | solution.py:555
  33.8 2.8 %copy-start.4 = (bf16[2,512,512]{2,1,0:T(8,128)(2,1)S(1)}, bf16[2,512,512]{2,1,0:T(8,128)(2,1)}, u32[]{:S(2)}) copy-start(bf16[2,512,512]{2,1,0:T(8,128)(2,1)} %t_out.3) | copy-start | bytes 3145732
  33.8 2.8 %copy-start.9 = (bf16[320,400]{1,0:T(8,128)(2,1)S(1)}, bf16[320,400]{1,0:T(8,128)(2,1)}, u32[]{:S(2)}) copy-start(bf16[320,400]{1,0:T(8,128)(2,1)} %constant.29.clone.g_to_a) | copy-start | bytes 768004
  33.8 2.8 %copy-start.11 = (bf16[384,320]{1,0:T(8,128)(2,1)S(1)}, bf16[384,320]{1,0:T(8,128)(2,1)}, u32[]{:S(2)}) copy-start(bf16[384,320]{1,0:T(8,128)(2,1)} %constant.28.clone.from_a) | copy-start | bytes 737284
  33.8 2.8 %copy-start.12 = (bf16[176,112]{1,0:T(8,128)(2,1)S(1)}, bf16[176,112]{1,0:T(8,128)(2,1)}, u32[]{:S(2)}) copy-start(bf16[176,112]{1,0:T(8,128)(2,1)} %constant.27.clone.open_cols) | copy-start | bytes 118276

commit v3 on v2

--- a/solution.py
+++ b/solution.py
@@ -279,7 +279,7 @@
 
 def teacher_first(
     far_ref, x_ref, id_ref, far_id_ref, q_ref, k_ref, v_ref, to_a, a_to_g, pack, t_qkv, t_out,
-    h_ref, g_ref, north_ref, south_ref, pad_ref, wout, sems,
+    h_ref, g_ref, first_ref, second_ref, pad_ref, wout, sems,
 ):
     copies = fetch((t_out.at[0], wout, sems.at[0]))
     width = x_ref.shape[1]
@@ -301,9 +301,20 @@
     h_ref[...] = h
     spread = dot(a_to_g[...], jnp.concatenate([h, id_ref[...]], axis=1)).astype(BF)
     g_ref[...] = spread
-    for ref, names in ((north_ref, TO_NORTH), (south_ref, TO_SOUTH)):
-        rows = jnp.concatenate([part(spread, n) for n in names], axis=0)
-        ref[...] = packed(rows, pack[...], ROW_TOKENS, ROW_SENT)
+    north, south = [
+        packed(
+            jnp.concatenate([part(spread, n) for n in names], axis=0),
+            pack[...], ROW_TOKENS, ROW_SENT,
+        )
+        for names in (TO_NORTH, TO_SOUTH)
+    ]
+    first_ref[...], second_ref[...] = swapped("lat", north, south)
+
+
+def swapped(axis, low, high):
+    even = lax.rem(lax.axis_index(axis), 2) == 0
+    low, high = low.astype(F32), high.astype(F32)
+    return jnp.where(even, low, high).astype(BF), jnp.where(even, high, low).astype(BF)
 
 
 def packed(rows, table, tokens, sent):
@@ -407,25 +418,29 @@
 
 
 def send_columns(
-    g_ref, north_ref, south_ref, open_rows, pack, after_ref, edge_ref, west_ref, east_ref
+    g_ref, first_ref, second_ref, open_rows, pack, after_ref, edge_ref, out_first, out_second
 ):
-    width = north_ref.shape[1]
+    width = first_ref.shape[1]
     lat = lax.axis_index("lat")
     blocks = []
     inside = (lat > 0, lat < lax.axis_size("lat") - 1)
-    for ref, there in zip((north_ref, south_ref), inside):
-        rows = opened(ref[...], open_rows[...], ROW_TOKENS)
+    for sent, there in zip(swapped("lat", first_ref[...], second_ref[...]), inside):
+        rows = opened(sent, open_rows[...], ROW_TOKENS)
         ids = rows[:, width:] * jnp.where(there, 1.0, 0.0).astype(BF)
         blocks.append(jnp.concatenate([rows[:, :width], ids], axis=1))
     edge = jnp.concatenate(blocks, axis=0)
     edge_ref[...] = edge
-    for ref, items in ((west_ref, TO_WEST), (east_ref, TO_EAST)):
-        rows = gather([(g_ref, OWN), (edge, EDGE)], items)
-        ref[...] = packed(rows, pack[...], COL_TOKENS, COL_SENT)
+    west, east = [
+        packed(
+            gather([(g_ref, OWN), (edge, EDGE)], items), pack[...], COL_TOKENS, COL_SENT
+        )
+        for items in (TO_WEST, TO_EAST)
+    ]
+    out_first[...], out_second[...] = swapped("lon", west, east)
 
 
 def beside_columns(
-    g_ref, edge_ref, t_qkv, q_ref, k_ref, v_ref, after_ref, k_out, v_out, n_ref, s_ref
+    g_ref, edge_ref, t_qkv, q_ref, k_ref, v_ref, k_out, v_out, n_ref, s_ref
 ):
     width = g_ref.shape[1] - 128
     blocks = head_blocks()
@@ -442,13 +457,14 @@
 
 
 def teacher_second(
-    h_ref, g_ref, edge_ref, east_ref, west_ref, q_ref, k_ref, v_ref, k_edge, v_edge,
+    h_ref, g_ref, edge_ref, first_ref, second_ref, q_ref, k_ref, v_ref, k_edge, v_edge,
     c_ref, n_ref, s_ref, open_cols, from_a, g_to_a, t_qkv, t_out, proj, s_qkv, s_out,
     g0_ref, save0, save1, out_ref, grad_ref,
 ):
     width = h_ref.shape[1]
     blocks = head_blocks()
-    came = [opened(ref[...], open_cols[...], COL_TOKENS) for ref in (east_ref, west_ref)]
+    west, east = swapped("lon", first_ref[...], second_ref[...])
+    came = [opened(sent, open_cols[...], COL_TOKENS) for sent in (east, west)]
     came = jnp.concatenate(came, axis=0)
     rows = came[:, :width]
     k = unit(dot(rows, t_qkv[1, :, width : 2 * width]), blocks)[0].astype(BF)
@@ -506,6 +522,14 @@
     ]
 
 
+def swaps(size, start, closed):
+    route = {i: i for i in range(size)}
+    for i in range(start, size if closed else size - 1, 2):
+        j = (i + 1) % size
+        route[i], route[j] = j, i
+    return sorted(route.items())
+
+
 def shards(teacher_in, student_in, regions, t_qkv, t_out, s_qkv, s_out, s_proj):
     width, narrow = teacher_in.shape[3], student_in.shape[3]
     lat_size, lon_size = lax.axis_size("lat"), lax.axis_size("lon")
@@ -527,7 +551,7 @@
         + buffers(teacher_in, regions, TO_A, A_ROW, A_COL, t_qkv[0]),
         10**9,
     )
-    hidden, spread, to_north, to_south = call(
+    hidden, spread, rows_1, rows_2 = call(
         teacher_first, "teacher_first",
         [((NA, width), BF), ((NG, wide), BF)] + [((ROW_SENT, width), BF)] * 2,
         [VMEM] * 11 + [HBM],
@@ -535,33 +559,33 @@
         + [pltpu.with_memory_space_constraint(t_out, pltpu.HBM)],
         [pltpu.VMEM((COLS, TALL, width), BF)] + buffers(t_out[0]), 3 * 10**9,
     )
-    north = lax.ppermute(to_south, "lat", [(i, (i + 1) % lat_size) for i in range(lat_size)])
-    south = lax.ppermute(to_north, "lat", [((i + 1) % lat_size, i) for i in range(lat_size)])
+    rows_1 = lax.ppermute(rows_1, "lat", swaps(lat_size, 1, False))
+    rows_2 = lax.ppermute(rows_2, "lat", swaps(lat_size, 0, False))
 
     g0, save0, save1, q, k, v, c_att = call(
         beside_rows, "beside_rows",
         [((NA, narrow), F32), ((NA, SAVE), BF), ((NA, SAVE), BF)]
         + [((NG, width), BF)] * 3 + [((AT["c"][1], width), BF)],
         [VMEM] * 8 + [ANY],
-        [student_in, ids, TO_A, s_qkv, s_out, s_proj, spread, t_qkv, to_north],
+        [student_in, ids, TO_A, s_qkv, s_out, s_proj, spread, t_qkv, hidden],
         [pltpu.VMEM((COLS, TALL, narrow), BF)], 5 * 10**9,
     )
-    edge, to_west, to_east = call(
+    edge, cols_1, cols_2 = call(
         send_columns, "send_columns",
         [((NE_ROWS, wide), BF)] + [((COL_SENT, width), BF)] * 2,
         [VMEM] * 5 + [ANY],
-        [spread, north, south, OPEN_ROWS, PACK_COLS, g0], (), 10**7,
-    )
-    east = lax.ppermute(to_west, "lon", [((j + 1) % lon_size, j) for j in range(lon_size)])
-    west = lax.ppermute(to_east, "lon", [(j, (j + 1) % lon_size) for j in range(lon_size)])
+        [spread, rows_1, rows_2, OPEN_ROWS, PACK_COLS, g0], (), 10**7,
+    )
+    cols_1 = lax.ppermute(cols_1, "lon", swaps(lon_size, 1, True))
+    cols_2 = lax.ppermute(cols_2, "lon", swaps(lon_size, 0, True))
 
     k_edge, v_edge, n_att, s_att = call(
         beside_columns, "beside_columns",
         [((NE_ROWS, width), BF)] * 2 + [((AT["n"][1], width), BF)] * 2,
-        [VMEM] * 6 + [ANY],
-        [spread, edge, t_qkv, q, k, v, to_west], (), 2 * 10**9,
-    )
-    args = [hidden, spread, edge, east, west, q, k, v, k_edge, v_edge, c_att, n_att, s_att]
+        [VMEM] * 6,
+        [spread, edge, t_qkv, q, k, v], (), 2 * 10**9,
+    )
+    args = [hidden, spread, edge, cols_1, cols_2, q, k, v, k_edge, v_edge, c_att, n_att, s_att]
     args += [OPEN_COLS, FROM_A, G_TO_A, t_qkv, t_out, s_proj, s_qkv, s_out, g0, save0, save1]
     out, grad = call(
         teacher_second, "teacher_second",

time: 47.4 us -> 45.1 us (0.951)
  waiting for transfers between devices: 6.69 us -> 3.27 us
  starting transfers between devices: 13.2 us -> 14.6 us
    ppermute x4, waiting for transfers between devices: 6.68 us -> 3.27 us  [the longest x1 2.19 us: shards(): cols_1 = lax.ppermute(cols_1, 'lon', swaps(lon_size, 1, True))]
    ppermute x4, starting transfers between devices: 13.1 us -> 14.5 us  [the longest x1 9.01 us: shards(): rows_1 = lax.ppermute(rows_1, 'lat', swaps(lat_size, 1, False))]
  transfers between devices with their start and end apart: 5 -> 5, of which waited for: 2 -> 2; matrix products, arithmetic and copies ran while one was open for 0% -> 0% of each run, Pallas kernels for 20% -> 21%
where the time goes in v3:
time: 45.1 us; the launch traced here: 44.9 us
  Pallas kernels  26 us (58%)
  starting transfers between devices  14.6 us (32%)
  waiting for transfers between devices  3.27 us (7%)
  between operations  0.9 us (2%)
    pallas_call x6, Pallas kernels, call(): pl.pallas_call(kernel, name=name, out_shape=shapes, in_specs=specs, out_s...  26 us
    ppermute x1, starting transfers between devices, shards(): rows_1 = lax.ppermute(rows_1, 'lat', swaps(lat_size, 1, False))  9.01 us
    ppermute x1, starting transfers between devices, shards(): cols_1 = lax.ppermute(cols_1, 'lon', swaps(lon_size, 1, True))  5.44 us
    ppermute x1, waiting for transfers between devices, shards(): cols_1 = lax.ppermute(cols_1, 'lon', swaps(lon_size, 1, True))  2.19 us
    ppermute x1, waiting for transfers between devices, shards(): cols_2 = lax.ppermute(cols_2, 'lon', swaps(lon_size, 0, True))  1.07 us
  transfers between devices with their start and end apart: 5, of which 2 were waited for; matrix products, arithmetic and copies ran while one was open for 0% of the time, Pallas kernels for 21%

profile of v3, /device:TPU:6, one launch (start us, length us, event | category | flops | bytes accessed | tf_op | source)
XLA Modules:
  0.0 44.9 jit_solution(5782441625429150264)
XLA Ops:
  0.6 0.1 collective-permute-start
  0.7 0.0 copy-start.1
  0.8 0.0 copy-start.10
  0.8 0.0 copy-start.13
  0.8 2.9 %teacher_own.1 = (bf16[320,512]{1,0:T(8,128)(2,1)S(1)}, bf16[320,128]{1,0:T(8,128)(2,1)S(1)}, bf16[320,128]{1,0:T(8,128)(2,1)S(1)}, bf16[320,512]{1,0:T(8,128)(2...) custom-call(bf16[1,12,24,512]{3,2,1,0:T(8,128)(2,1)} %bitcast.7, s32[12,2,24]{2,1,0:T(2,128)} %bitcast.8, ...), custom_call_target="tpu_custom_call" | custom-call | flops 1000000000 | bytes 3711744 | tf_op jit(solution)/shard_map/teacher_own/pallas_call | solution.py:507
  3.7 0.0 collective-permute-done.far_ref
  3.7 0.0 copy-start.5
  3.8 0.0 copy-start.6
  3.8 0.0 copy-start.7
  3.8 0.0 copy-start.8
  3.8 5.5 %teacher_first.1 = (bf16[320,512]{1,0:T(8,128)(2,1)S(1)}, bf16[400,640]{1,0:T(8,128)(2,1)S(1)}, bf16[80,512]{1,0:T(8,128)(2,1)S(1)}, bf16[80,512]{1,0:T(8,128)(2,1)S(1)}) custom-call(bf16[1,12,24,512]{3,2,1,0:T(8,128)(2,1)S(1)} %collective-permute-done.far_ref, bf16[320,512]{1,0:T(8,128)(2,1)S(1)} %get-tuple-element.28.x_ref, ...), custom_call_target="tpu_custom_call" | custom-call | flops 3000000000 | bytes 6494208 | tf_op jit(solution)/shard_map/teacher_first/pallas_call | solution.py:507
  9.3 9.0 %collective-permute-start.1 = (bf16[80,512]{1,0:T(8,128)(2,1)S(1)}, bf16[80,512]{1,0:T(8,128)(2,1)S(1)}, u32[]{:S(2)}, u32[]{:S(2)}) collective-permute-start(bf16[80,512]{1,0:T(8,128)(2,1)S(1)} %get-tuple-element.36), channel_id=1, source_target_pairs={{0,0},{32,64},{64,32},{96,128},{128,96},{160,192},{192,160},{224,2... | collective-permute-start | bytes 245768 | tf_op jit(solution)/shard_map/ppermute | solution.py:562
  18.3 0.1 collective-permute-start.2
  18.5 0.0 copy-start.2
  18.5 0.0 copy-start.3
  18.5 5.2 %beside_rows.1 = (f32[320,256]{1,0:T(8,128)S(1)}, bf16[320,2688]{1,0:T(8,128)(2,1)S(1)}, bf16[320,2688]{1,0:T(8,128)(2,1)S(1)}, bf16[400,512]{1,0:T(8,128)(2,1)S...) custom-call(bf16[1,12,24,256]{3,2,1,0:T(8,128)(2,1)S(1)} %bitcast.5, ...), custom_call_target="tpu_custom_call" | custom-call | flops 5000000000 | bytes 5771264 | tf_op jit(solution)/shard_map/beside_rows/pallas_call | solution.py:507
  23.7 0.7 %send_columns.1 = (bf16[224,640]{1,0:T(8,128)(2,1)S(1)}, bf16[112,512]{1,0:T(8,128)(2,1)S(1)}, bf16[112,512]{1,0:T(8,128)(2,1)S(1)}) custom-call(bf16[400,640]{1,0:T(8,128)(2,1)S(1)} %get-tuple-element.35.g_ref, bf16[80,512]{1,0:T(8,128)(2,1)S(1)} %collective-permute-done.1.first_ref, bf16[80,512]{1,0:T(8,128)(2,1)S(1)} %collective-permute-done.2.second_ref, ...), custom_call_target="tpu_custom_call" | custom-call | flops 10000000 | bytes 1066496 | tf_op jit(solution)/shard_map/send_columns/pallas_call | solution.py:507
  24.4 5.4 %collective-permute-start.3 = (bf16[112,512]{1,0:T(8,128)(2,1)S(1)}, bf16[112,512]{1,0:T(8,128)(2,1)S(1)}, u32[]{:S(2)}, u32[]{:S(2)}) collective-permute-start(bf16[112,512]{1,0:T(8,128)(2,1)S(1)} %get-tuple-element.40), channel_id=1, source_target_pairs={{0,30},{2,4},{4,2},{6,8},{8,6},{10,12},{12,10},{14,16},{16,14},{18... | collective-permute-start | bytes 344072 | tf_op jit(solution)/shard_map/ppermute | solution.py:579
  29.9 0.0 collective-permute-start.4
  29.9 0.0 copy-start.12
  29.9 1.5 %beside_columns.1 = (bf16[224,512]{1,0:T(8,128)(2,1)S(1)}, bf16[224,512]{1,0:T(8,128)(2,1)S(1)}, bf16[48,512]{1,0:T(8,128)(2,1)S(1)}, bf16[48,512]{1,0:T(8,128)(2,1)S(1)}) custom-call(bf16[400,640]{1,0:T(8,128)(2,1)S(1)} %get-tuple-element.35.g_ref, bf16[224,640]{1,0:T(8,128)(2,1)S(1)} %get-tuple-element.39.edge_ref, bf16[2,512,1536]{2,1,0:T(8,128)(2,1)S(1)} %copy-done, ...), custom_call_target="tpu_custom_call" | custom-call | flops 2000000000 | bytes 5173248 | tf_op jit(solution)/shard_map/beside_columns/pallas_call | solution.py:507
  31.4 2.2 %collective-permute-done.3.first_ref = bf16[112,512]{1,0:T(8,128)(2,1)S(1)} collective-permute-done((bf16[112,512]{1,0:T(8,128)(2,1)S(1)}, bf16[112,512]{1,0:T(8,128)(2,1)S(1)}, u32[]{:S(2)}, u32[]{:S(2)}) %collective-permute-start.3) | collective-permute-done | bytes 114720 | tf_op jit(solution)/shard_map/ppermute | solution.py:579
  33.6 1.1 %collective-permute-done.4.second_ref = bf16[112,512]{1,0:T(8,128)(2,1)S(1)} collective-permute-done((bf16[112,512]{1,0:T(8,128)(2,1)S(1)}, bf16[112,512]{1,0:T(8,128)(2,1)S(1)}, u32[]{:S(2)}, u32[]{:S(2)}) %collective-permute-start.4) | collective-permute-done | bytes 114720 | tf_op jit(solution)/shard_map/ppermute | solution.py:580
  34.7 10.2 %teacher_second.1 = (bf16[1,12,24,512]{3,2,1,0:T(8,128)(2,1)}, f32[1,12,24,256]{3,2,1,0:T(8,128)}) custom-call(bf16[320,512]{1,0:T(8,128)(2,1)S(1)} %get-tuple-element.34.after_ref.h_ref, bf16[400,640]{1,0:T(8,128)(2,1)S(1)} %get-tuple-element.35.g_ref, bf16[224,640]{1,0:T(8,128)(2,1)S(1)} %get-tuple-element.39.edge_ref, ...), custom_call_target="tpu_custom_call" | custom-call | flops 6000000000 | bytes 13038080 | tf_op jit(solution)/shard_map/teacher_second/pallas_call | solution.py:507
  (20 shorter events, 0.0 us)
Async XLA Ops:
  0.6 3.1 %collective-permute-start = (bf16[1,12,24,512]{3,2,1,0:T(8,128)(2,1)}, bf16[1,12,24,512]{3,2,1,0:T(8,128)(2,1)S(1)}, u32[]{:S(2)}, u32[]{:S(2)}) collective-permute-start(bf16[1,12,24,512]{3,2,1,0:T(8,128)(2,1)} %bitcast.6), channel_id=1, source_target_pairs={{0,1},{1,0},{2,3},{3,2},{4,5},{5,4},{6,7},{7,6},{8,9},{9,8},{10,11... | collective-permute-start | bytes 884744 | tf_op jit(solution)/shard_map/ppermute | solution.py:540
  0.7 3.0 %copy-start = (bf16[2,512,1536]{2,1,0:T(8,128)(2,1)S(1)}, bf16[2,512,1536]{2,1,0:T(8,128)(2,1)}, u32[]{:S(2)}) copy-start(bf16[2,512,1536]{2,1,0:T(8,128)(2,1)} %t_qkv.9) | copy-start | bytes 9437188
  0.7 3.0 %copy-start.1 = (bf16[320,384]{1,0:T(8,128)(2,1)S(1)}, bf16[320,384]{1,0:T(8,128)(2,1)}, u32[]{:S(2)}) copy-start(bf16[320,384]{1,0:T(8,128)(2,1)} %constant.20.clone.to_a_hbm.to_a) | copy-start | bytes 737284
  0.8 3.0 %copy-start.10 = (bf16[400,320]{1,0:T(8,128)(2,1)S(1)}, bf16[400,320]{1,0:T(8,128)(2,1)}, u32[]{:S(2)}) copy-start(bf16[400,320]{1,0:T(8,128)(2,1)} %constant.23.clone.a_to_g) | copy-start | bytes 768004
  0.8 3.0 %copy-start.13 = (bf16[128,112]{1,0:T(8,128)(2,1)S(1)}, bf16[128,112]{1,0:T(8,128)(2,1)}, u32[]{:S(2)}) copy-start(bf16[128,112]{1,0:T(8,128)(2,1)} %constant.24.clone.pack) | copy-start | bytes 86020
  3.7 14.7 %copy-start.5 = (bf16[2,256,768]{2,1,0:T(8,128)(2,1)S(1)}, bf16[2,256,768]{2,1,0:T(8,128)(2,1)}, u32[]{:S(2)}) copy-start(bf16[2,256,768]{2,1,0:T(8,128)(2,1)} %s_qkv.3) | copy-start | bytes 2359300
  3.8 14.7 %copy-start.6 = (bf16[2,256,256]{2,1,0:T(8,128)(2,1)S(1)}, bf16[2,256,256]{2,1,0:T(8,128)(2,1)}, u32[]{:S(2)}) copy-start(bf16[2,256,256]{2,1,0:T(8,128)(2,1)} %s_out.3) | copy-start | bytes 786436
  3.8 14.7 %copy-start.7 = (bf16[256,512]{1,0:T(8,128)(2,1)S(1)}, bf16[256,512]{1,0:T(8,128)(2,1)}, u32[]{:S(2)}) copy-start(bf16[256,512]{1,0:T(8,128)(2,1)} %proj.3) | copy-start | bytes 786436
  3.8 14.7 %copy-start.8 = (bf16[1,24,12,256]{3,1,2,0:T(8,128)(2,1)S(1)}, bf16[1,24,12,256]{3,1,2,0:T(8,128)(2,1)}, u32[]{:S(2)}) copy-start(bf16[1,24,12,256]{3,1,2,0:T(8,128)(2,1)} %param.19) | copy-start | bytes 442372
  9.3 14.3 %collective-permute-start.1 = (bf16[80,512]{1,0:T(8,128)(2,1)S(1)}, bf16[80,512]{1,0:T(8,128)(2,1)S(1)}, u32[]{:S(2)}, u32[]{:S(2)}) collective-permute-start(bf16[80,512]{1,0:T(8,128)(2,1)S(1)} %get-tuple-element.36), channel_id=1, source_target_pairs={{0,0},{32,64},{64,32},{96,128},{128,96},{160,192},{192,160},{224,2... | collective-permute-start | bytes 245768 | tf_op jit(solution)/shard_map/ppermute | solution.py:562
  18.3 5.3 %collective-permute-start.2 = (bf16[80,512]{1,0:T(8,128)(2,1)S(1)}, bf16[80,512]{1,0:T(8,128)(2,1)S(1)}, u32[]{:S(2)}, u32[]{:S(2)}) collective-permute-start(bf16[80,512]{1,0:T(8,128)(2,1)S(1)} %get-tuple-element.37), channel_id=1, source_target_pairs={{0,32},{32,0},{64,96},{96,64},{128,160},{160,128},{192,224},{224,1... | collective-permute-start | bytes 245768 | tf_op jit(solution)/shard_map/ppermute | solution.py:563
  18.5 5.2 %copy-start.2 = (bf16[128,176]{1,0:T(8,128)(2,1)S(1)}, bf16[128,176]{1,0:T(8,128)(2,1)}, u32[]{:S(2)}) copy-start(bf16[128,176]{1,0:T(8,128)(2,1)} %constant.26.clone.pack) | copy-start | bytes 135172
  18.5 5.2 %copy-start.3 = (bf16[112,80]{1,0:T(8,128)(2,1)S(1)}, bf16[112,80]{1,0:T(8,128)(2,1)}, u32[]{:S(2)}) copy-start(bf16[112,80]{1,0:T(8,128)(2,1)} %constant.25.clone.open_rows) | copy-start | bytes 53764
  24.4 9.2 %collective-permute-start.3 = (bf16[112,512]{1,0:T(8,128)(2,1)S(1)}, bf16[112,512]{1,0:T(8,128)(2,1)S(1)}, u32[]{:S(2)}, u32[]{:S(2)}) collective-permute-start(bf16[112,512]{1,0:T(8,128)(2,1)S(1)} %get-tuple-element.40), channel_id=1, source_target_pairs={{0,30},{2,4},{4,2},{6,8},{8,6},{10,12},{12,10},{14,16},{16,14},{18... | collective-permute-start | bytes 344072 | tf_op jit(solution)/shard_map/ppermute | solution.py:579
  29.9 4.8 %collective-permute-start.4 = (bf16[112,512]{1,0:T(8,128)(2,1)S(1)}, bf16[112,512]{1,0:T(8,128)(2,1)S(1)}, u32[]{:S(2)}, u32[]{:S(2)}) collective-permute-start(bf16[112,512]{1,0:T(8,128)(2,1)S(1)} %get-tuple-element.41), channel_id=1, source_target_pairs={{0,2},{2,0},{4,6},{6,4},{8,10},{10,8},{12,14},{14,12},{16,18},{18,... | collective-permute-start | bytes 344072 | tf_op jit(solution)/shard_map/ppermute | solution.py:580
  29.9 4.8 %copy-start.4 = (bf16[2,512,512]{2,1,0:T(8,128)(2,1)S(1)}, bf16[2,512,512]{2,1,0:T(8,128)(2,1)}, u32[]{:S(2)}) copy-start(bf16[2,512,512]{2,1,0:T(8,128)(2,1)} %t_out.3) | copy-start | bytes 3145732
  29.9 4.8 %copy-start.9 = (bf16[320,400]{1,0:T(8,128)(2,1)S(1)}, bf16[320,400]{1,0:T(8,128)(2,1)}, u32[]{:S(2)}) copy-start(bf16[320,400]{1,0:T(8,128)(2,1)} %constant.29.clone.g_to_a) | copy-start | bytes 768004
  29.9 4.8 %copy-start.11 = (bf16[384,320]{1,0:T(8,128)(2,1)S(1)}, bf16[384,320]{1,0:T(8,128)(2,1)}, u32[]{:S(2)}) copy-start(bf16[384,320]{1,0:T(8,128)(2,1)} %constant.28.clone.from_a) | copy-start | bytes 737284
  29.9 4.8 %copy-start.12 = (bf16[176,112]{1,0:T(8,128)(2,1)S(1)}, bf16[176,112]{1,0:T(8,128)(2,1)}, u32[]{:S(2)}) copy-start(bf16[176,112]{1,0:T(8,128)(2,1)} %constant.27.clone.open_cols) | copy-start | bytes 118276

commit v4 on v3

--- a/solution.py
+++ b/solution.py
@@ -22,7 +22,7 @@
 NA = 4 * WIN
 TALL = 32
 NAT = COLS * TALL
-QUAD = 256
+PAIR = 128
 
 PARTS = (
     ("nw", (0, 6), (0, 3), 32),
@@ -103,37 +103,35 @@
 
 
 def head_lanes(rows, h):
-    lane = lax.broadcasted_iota(jnp.int32, (rows, QUAD), 1)
+    lane = lax.broadcasted_iota(jnp.int32, (rows, PAIR), 1)
     return jnp.where((lane >> 6) == h, 1.0, 0.0).astype(BF)
 
 
 def head_blocks():
-    row = lax.broadcasted_iota(jnp.int32, (QUAD, QUAD), 0)
-    lane = lax.broadcasted_iota(jnp.int32, (QUAD, QUAD), 1)
+    row = lax.broadcasted_iota(jnp.int32, (2 * PAIR, 2 * PAIR), 0)
+    lane = lax.broadcasted_iota(jnp.int32, (2 * PAIR, 2 * PAIR), 1)
     return jnp.where((row >> 6) == (lane >> 6), 1.0, 0.0).astype(BF)
 
 
 def stack_heads(x):
-    return jnp.concatenate([x * head_lanes(1, h) for h in range(4)], axis=0)
+    return jnp.concatenate([x * head_lanes(1, h) for h in range(2)], axis=0)
 
 
 def stack_values(v):
     rows = v.shape[0]
-    ones = jnp.concatenate([head_lanes(rows, h) for h in range(4)], axis=0)
+    ones = jnp.concatenate([head_lanes(rows, h) for h in range(2)], axis=0)
     return jnp.concatenate([stack_heads(v), ones], axis=1)
 
 
 def unstack_heads(x):
-    n = x.shape[0] // 4
-    lane = lax.broadcasted_iota(jnp.int32, (1, QUAD), 1) >> 6
-    total = x[:n]
-    for h in range(1, 4):
-        total = jnp.where(lane == h, x[h * n : (h + 1) * n], total)
-    return total
+    n = x.shape[0] // 2
+    lane = lax.broadcasted_iota(jnp.int32, (1, PAIR), 1) >> 6
+    return jnp.where(lane == 0, x[:n], x[n:])
 
 
 def head_sums(x, blocks):
-    groups = [dot(x[:, i : i + QUAD].astype(BF), blocks) for i in range(0, x.shape[1], QUAD)]
+    step = blocks.shape[0]
+    groups = [dot(x[:, i : i + step].astype(BF), blocks) for i in range(0, x.shape[1], step)]
     return groups[0] if len(groups) == 1 else jnp.concatenate(groups, axis=1)
 
 
@@ -143,16 +141,17 @@
 
 
 def id_mask(id_query, id_keys):
-    keys = jnp.concatenate([id_keys] * 4, axis=0)
+    keys = jnp.concatenate([id_keys] * 2, axis=0)
     row = dot_nt(jnp.full((8, 128), 1.0 / 128, BF), keys)[0:1]
     return id_query.astype(F32)[:, 0:1] == row
 
 
 def attend(q, k, v, mask):
-    scores = dot_nt(q, stack_heads(k))
-    e = jnp.where(mask, jnp.exp2(scores), 0.0).astype(BF)
-    both = dot(e, stack_values(v))
-    return both[:, :QUAD], both[:, QUAD:], e
+    pairs = [slice(i, i + PAIR) for i in range(0, q.shape[1], PAIR)]
+    scores = [dot_nt(q[:, p], stack_heads(k[:, p])) for p in pairs]
+    es = [jnp.where(mask, jnp.exp2(s), 0.0).astype(BF) for s in scores]
+    both = [dot(e, stack_values(v[:, p])) for e, p in zip(es, pairs)]
+    return [b[:, :PAIR] for b in both], [b[:, PAIR:] for b in both], es
 
 
 def to_window_order(x_ref, pad_ref, to_a):
@@ -182,32 +181,34 @@
     return (x.astype(F32) + n).astype(BF), n, r
 
 
-SAVE = 9 * QUAD + 384
+WIDE = 2 * PAIR
+SAVE = 11 * WIDE
 
 
 def student_layer(x, w_qkv, w_out, ids, save_ref):
     blocks = head_blocks()
     qkv = dot(x, w_qkv)
-    q, sq = unit(qkv[:, :QUAD], blocks)
-    k, sk = unit(qkv[:, QUAD : 2 * QUAD], blocks)
+    q, sq = unit(qkv[:, :WIDE], blocks)
+    k, sk = unit(qkv[:, WIDE : 2 * WIDE], blocks)
     q = (q * SCALE).astype(BF)
     k = k.astype(BF)
-    v = qkv[:, 2 * QUAD :].astype(BF)
+    v = qkv[:, 2 * WIDE :].astype(BF)
     atts = []
     for w in range(4):
         rows = slice(w * WIN, (w + 1) * WIN)
         mask = id_mask(ids[rows], ids[rows])
-        num, den, e = attend(q[rows], k[rows], v[rows], mask)
-        z = 1.0 / den
-        att = num * z
-        save_ref[rows, 4 * QUAD : 5 * QUAD] = z.astype(BF)
-        save_ref[rows, 9 * QUAD : 9 * QUAD + 4 * WIN] = e
+        nums, dens, es = attend(q[rows], k[rows], v[rows], mask)
+        z = 1.0 / jnp.concatenate(dens, axis=1)
+        att = jnp.concatenate(nums, axis=1) * z
+        save_ref[rows, 4 * WIDE : 5 * WIDE] = z.astype(BF)
+        for i, e in enumerate(es):
+            save_ref[rows, (9 + i) * WIDE : (9 + i) * WIDE + 2 * WIN] = e
         atts.append(att.astype(BF))
     att = jnp.concatenate(atts, axis=0)
     h, n, r = residual(x, att, w_out)
     for i, part in ((0, q), (1, k), (2, v), (3, att), (5, sq), (6, sk), (7, n)):
-        save_ref[:, i * QUAD : (i + 1) * QUAD] = part.astype(BF)
-    save_ref[:, 8 * QUAD : 9 * QUAD] = jnp.broadcast_to(r, (NA, QUAD)).astype(BF)
+        save_ref[:, i * WIDE : (i + 1) * WIDE] = part.astype(BF)
+    save_ref[:, 8 * WIDE : 9 * WIDE] = jnp.broadcast_to(r, (NA, WIDE)).astype(BF)
     return h
 
 
@@ -220,7 +221,7 @@
 
 def student_back(g, save_ref, w_qkv, w_out):
     blocks = head_blocks()
-    part = lambda i: save_ref[:, i * QUAD : (i + 1) * QUAD]
+    part = lambda i: save_ref[:, i * WIDE : (i + 1) * WIDE]
     n, r = part(7).astype(F32), part(8).astype(F32)
     dy = r * (g - n * jnp.mean(g * n, axis=1, keepdims=True))
     datt = dot_nt(dy.astype(BF), w_out) * part(4).astype(F32)
@@ -230,12 +231,19 @@
     dqs, dks, dvs = [], [], []
     for w in range(4):
         rows = slice(w * WIN, (w + 1) * WIN)
-        e = save_ref[rows, 9 * QUAD : 9 * QUAD + 4 * WIN]
-        both = jnp.concatenate([datt[rows], drop[rows]], axis=1)
-        ds = (e.astype(F32) * dot_nt(both, stack_values(v[rows]))).astype(BF)
-        dqs.append(dot(ds, stack_heads(k[rows])))
-        dks.append(unstack_heads(dot_tn(ds, q[rows])))
-        dvs.append(unstack_heads(dot_tn(e, datt[rows])))
+        pairs = [slice(i, i + PAIR) for i in range(0, WIDE, PAIR)]
+        es = [save_ref[rows, (9 + i) * WIDE : (9 + i) * WIDE + 2 * WIN] for i in range(2)]
+        dws = [
+            dot_nt(
+                jnp.concatenate([datt[rows, p], drop[rows, p]], axis=1), stack_values(v[rows, p])
+            )
+            for p in pairs
+        ]
+        dvs.append([unstack_heads(dot_tn(e, datt[rows, p])) for e, p in zip(es, pairs)])
+        dss = [(e.astype(F32) * dw).astype(BF) for e, dw in zip(es, dws)]
+        dqs.append([dot(ds, stack_heads(k[rows, p])) for ds, p in zip(dss, pairs)])
+        dks.append([unstack_heads(dot_tn(ds, q[rows, p])) for ds, p in zip(dss, pairs)])
+    dqs, dks, dvs = [[jnp.concatenate(x, axis=1) for x in y] for y in (dqs, dks, dvs)]
     dq = 10.0 * jnp.concatenate(dqs, axis=0)
     dk = (1.0 / LOG2E) * jnp.concatenate(dks, axis=0)
     dv = jnp.concatenate(dvs, axis=0)
@@ -384,14 +392,8 @@
 
 
 def window_attention(q, keys, ids):
-    k, v = keys
-    mask = id_mask(*ids)
-    quads = []
-    for i in range(0, q.shape[1], QUAD):
-        lanes = slice(i, i + QUAD)
-        num, den, _ = attend(q[:, lanes], k[:, lanes], v[:, lanes], mask)
-        quads.append((num / den).astype(BF))
-    return jnp.concatenate(quads, axis=1)
+    nums, dens, _ = attend(q, *keys, id_mask(*ids))
+    return jnp.concatenate([(n / d).astype(BF) for n, d in zip(nums, dens)], axis=1)
 
 
 def beside_rows(

time: 45.1 us -> 41.3 us (0.916)
  Pallas kernels: 26 us -> 21.2 us
  starting transfers between devices: 14.6 us -> 15.2 us
    pallas_call x6, Pallas kernels: 26 us -> 21.2 us  [call(): pl.pallas_call(kernel, name=name, out_shape=shapes, in_specs=specs, out_s...]
    ppermute x1, waiting for transfers between devices: 1.07 us -> 1.64 us  [shards(): cols_2 = lax.ppermute(cols_2, 'lon', swaps(lon_size, 0, True))]
    ppermute x1, starting transfers between devices: 5.44 us -> 6 us  [shards(): cols_1 = lax.ppermute(cols_1, 'lon', swaps(lon_size, 1, True))]
where the time goes in v4:
time: 41.3 us; the launch traced here: 41.1 us
  Pallas kernels  21.2 us (51%)
  starting transfers between devices  15.2 us (37%)
  waiting for transfers between devices  3.71 us (9%)
  between operations  0.9 us (2%)
    pallas_call x6, Pallas kernels, call(): pl.pallas_call(kernel, name=name, out_shape=shapes, in_specs=specs, out_s...  21.2 us
    ppermute x1, starting transfers between devices, shards(): rows_1 = lax.ppermute(rows_1, 'lat', swaps(lat_size, 1, False))  9.02 us
    ppermute x1, starting transfers between devices, shards(): cols_1 = lax.ppermute(cols_1, 'lon', swaps(lon_size, 1, True))  6 us
    ppermute x1, waiting for transfers between devices, shards(): cols_1 = lax.ppermute(cols_1, 'lon', swaps(lon_size, 1, True))  2.06 us
    ppermute x1, waiting for transfers between devices, shards(): cols_2 = lax.ppermute(cols_2, 'lon', swaps(lon_size, 0, True))  1.64 us
  transfers between devices with their start and end apart: 5, of which 2 were waited for; matrix products, arithmetic and copies ran while one was open for 0% of the time, Pallas kernels for 21%

profile of v4, /device:TPU:6, one launch (start us, length us, event | category | flops | bytes accessed | tf_op | source)
XLA Modules:
  0.0 41.1 jit_solution(1755969443435578507)
XLA Ops:
  0.6 0.1 collective-permute-start
  0.7 0.0 copy-start.1
  0.8 0.0 copy-start.10
  0.8 0.0 copy-start.13
  0.8 2.9 %teacher_own.1 = (bf16[320,512]{1,0:T(8,128)(2,1)S(1)}, bf16[320,128]{1,0:T(8,128)(2,1)S(1)}, bf16[320,128]{1,0:T(8,128)(2,1)S(1)}, bf16[320,512]{1,0:T(8,128)(2...) custom-call(bf16[1,12,24,512]{3,2,1,0:T(8,128)(2,1)} %bitcast.7, s32[12,2,24]{2,1,0:T(2,128)} %bitcast.8, ...), custom_call_target="tpu_custom_call" | custom-call | flops 1000000000 | bytes 3711744 | tf_op jit(solution)/shard_map/teacher_own/pallas_call | solution.py:509
  3.7 0.0 collective-permute-done.far_ref
  3.7 0.0 copy-start.5
  3.8 0.0 copy-start.6
  3.8 0.0 copy-start.7
  3.8 0.0 copy-start.8
  3.8 4.2 %teacher_first.1 = (bf16[320,512]{1,0:T(8,128)(2,1)S(1)}, bf16[400,640]{1,0:T(8,128)(2,1)S(1)}, bf16[80,512]{1,0:T(8,128)(2,1)S(1)}, bf16[80,512]{1,0:T(8,128)(2,1)S(1)}) custom-call(bf16[1,12,24,512]{3,2,1,0:T(8,128)(2,1)S(1)} %collective-permute-done.far_ref, bf16[320,512]{1,0:T(8,128)(2,1)S(1)} %get-tuple-element.28.x_ref, ...), custom_call_target="tpu_custom_call" | custom-call | flops 3000000000 | bytes 6494208 | tf_op jit(solution)/shard_map/teacher_first/pallas_call | solution.py:509
  8.0 9.0 %collective-permute-start.1 = (bf16[80,512]{1,0:T(8,128)(2,1)S(1)}, bf16[80,512]{1,0:T(8,128)(2,1)S(1)}, u32[]{:S(2)}, u32[]{:S(2)}) collective-permute-start(bf16[80,512]{1,0:T(8,128)(2,1)S(1)} %get-tuple-element.36), channel_id=1, source_target_pairs={{0,0},{32,64},{64,32},{96,128},{128,96},{160,192},{192,160},{224,2... | collective-permute-start | bytes 245768 | tf_op jit(solution)/shard_map/ppermute | solution.py:564
  17.0 0.1 collective-permute-start.2
  17.1 0.0 copy-start.2
  17.1 0.0 copy-start.3
  17.2 4.6 %beside_rows.1 = (f32[320,256]{1,0:T(8,128)S(1)}, bf16[320,2816]{1,0:T(8,128)(2,1)S(1)}, bf16[320,2816]{1,0:T(8,128)(2,1)S(1)}, bf16[400,512]{1,0:T(8,128)(2,1)S...) custom-call(bf16[1,12,24,256]{3,2,1,0:T(8,128)(2,1)S(1)} %bitcast.5, ...), custom_call_target="tpu_custom_call" | custom-call | flops 5000000000 | bytes 5771264 | tf_op jit(solution)/shard_map/beside_rows/pallas_call | solution.py:509
  21.8 0.7 %send_columns.1 = (bf16[224,640]{1,0:T(8,128)(2,1)S(1)}, bf16[112,512]{1,0:T(8,128)(2,1)S(1)}, bf16[112,512]{1,0:T(8,128)(2,1)S(1)}) custom-call(bf16[400,640]{1,0:T(8,128)(2,1)S(1)} %get-tuple-element.35.g_ref, bf16[80,512]{1,0:T(8,128)(2,1)S(1)} %collective-permute-done.1.first_ref, bf16[80,512]{1,0:T(8,128)(2,1)S(1)} %collective-permute-done.2.second_ref, ...), custom_call_target="tpu_custom_call" | custom-call | flops 10000000 | bytes 1066496 | tf_op jit(solution)/shard_map/send_columns/pallas_call | solution.py:509
  22.5 6.0 %collective-permute-start.3 = (bf16[112,512]{1,0:T(8,128)(2,1)S(1)}, bf16[112,512]{1,0:T(8,128)(2,1)S(1)}, u32[]{:S(2)}, u32[]{:S(2)}) collective-permute-start(bf16[112,512]{1,0:T(8,128)(2,1)S(1)} %get-tuple-element.40), channel_id=1, source_target_pairs={{0,30},{2,4},{4,2},{6,8},{8,6},{10,12},{12,10},{14,16},{16,14},{18... | collective-permute-start | bytes 344072 | tf_op jit(solution)/shard_map/ppermute | solution.py:581
  28.5 0.0 collective-permute-start.4
  28.5 0.0 copy-start.12
  28.5 1.1 %beside_columns.1 = (bf16[224,512]{1,0:T(8,128)(2,1)S(1)}, bf16[224,512]{1,0:T(8,128)(2,1)S(1)}, bf16[48,512]{1,0:T(8,128)(2,1)S(1)}, bf16[48,512]{1,0:T(8,128)(2,1)S(1)}) custom-call(bf16[400,640]{1,0:T(8,128)(2,1)S(1)} %get-tuple-element.35.g_ref, bf16[224,640]{1,0:T(8,128)(2,1)S(1)} %get-tuple-element.39.edge_ref, bf16[2,512,1536]{2,1,0:T(8,128)(2,1)S(1)} %copy-done, ...), custom_call_target="tpu_custom_call" | custom-call | flops 2000000000 | bytes 5173248 | tf_op jit(solution)/shard_map/beside_columns/pallas_call | solution.py:509
  29.6 2.1 %collective-permute-done.3.first_ref = bf16[112,512]{1,0:T(8,128)(2,1)S(1)} collective-permute-done((bf16[112,512]{1,0:T(8,128)(2,1)S(1)}, bf16[112,512]{1,0:T(8,128)(2,1)S(1)}, u32[]{:S(2)}, u32[]{:S(2)}) %collective-permute-start.3) | collective-permute-done | bytes 114720 | tf_op jit(solution)/shard_map/ppermute | solution.py:581
  31.6 1.6 %collective-permute-done.4.second_ref = bf16[112,512]{1,0:T(8,128)(2,1)S(1)} collective-permute-done((bf16[112,512]{1,0:T(8,128)(2,1)S(1)}, bf16[112,512]{1,0:T(8,128)(2,1)S(1)}, u32[]{:S(2)}, u32[]{:S(2)}) %collective-permute-start.4) | collective-permute-done | bytes 114720 | tf_op jit(solution)/shard_map/ppermute | solution.py:582
  33.3 7.8 %teacher_second.1 = (bf16[1,12,24,512]{3,2,1,0:T(8,128)(2,1)}, f32[1,12,24,256]{3,2,1,0:T(8,128)}) custom-call(bf16[320,512]{1,0:T(8,128)(2,1)S(1)} %get-tuple-element.34.after_ref.h_ref, bf16[400,640]{1,0:T(8,128)(2,1)S(1)} %get-tuple-element.35.g_ref, bf16[224,640]{1,0:T(8,128)(2,1)S(1)} %get-tuple-element.39.edge_ref, ...), custom_call_target="tpu_custom_call" | custom-call | flops 6000000000 | bytes 13201920 | tf_op jit(solution)/shard_map/teacher_second/pallas_call | solution.py:509
  (20 shorter events, 0.0 us)
Async XLA Ops:
  0.6 3.1 %collective-permute-start = (bf16[1,12,24,512]{3,2,1,0:T(8,128)(2,1)}, bf16[1,12,24,512]{3,2,1,0:T(8,128)(2,1)S(1)}, u32[]{:S(2)}, u32[]{:S(2)}) collective-permute-start(bf16[1,12,24,512]{3,2,1,0:T(8,128)(2,1)} %bitcast.6), channel_id=1, source_target_pairs={{0,1},{1,0},{2,3},{3,2},{4,5},{5,4},{6,7},{7,6},{8,9},{9,8},{10,11... | collective-permute-start | bytes 884744 | tf_op jit(solution)/shard_map/ppermute | solution.py:542
  0.7 3.0 %copy-start = (bf16[2,512,1536]{2,1,0:T(8,128)(2,1)S(1)}, bf16[2,512,1536]{2,1,0:T(8,128)(2,1)}, u32[]{:S(2)}) copy-start(bf16[2,512,1536]{2,1,0:T(8,128)(2,1)} %t_qkv.9) | copy-start | bytes 9437188
  0.7 3.0 %copy-start.1 = (bf16[320,384]{1,0:T(8,128)(2,1)S(1)}, bf16[320,384]{1,0:T(8,128)(2,1)}, u32[]{:S(2)}) copy-start(bf16[320,384]{1,0:T(8,128)(2,1)} %constant.20.clone.to_a_hbm.to_a) | copy-start | bytes 737284
  0.8 3.0 %copy-start.10 = (bf16[400,320]{1,0:T(8,128)(2,1)S(1)}, bf16[400,320]{1,0:T(8,128)(2,1)}, u32[]{:S(2)}) copy-start(bf16[400,320]{1,0:T(8,128)(2,1)} %constant.23.clone.a_to_g) | copy-start | bytes 768004
  0.8 3.0 %copy-start.13 = (bf16[128,112]{1,0:T(8,128)(2,1)S(1)}, bf16[128,112]{1,0:T(8,128)(2,1)}, u32[]{:S(2)}) copy-start(bf16[128,112]{1,0:T(8,128)(2,1)} %constant.24.clone.pack) | copy-start | bytes 86020
  3.7 13.3 %copy-start.5 = (bf16[2,256,768]{2,1,0:T(8,128)(2,1)S(1)}, bf16[2,256,768]{2,1,0:T(8,128)(2,1)}, u32[]{:S(2)}) copy-start(bf16[2,256,768]{2,1,0:T(8,128)(2,1)} %s_qkv.3) | copy-start | bytes 2359300
  3.8 13.3 %copy-start.6 = (bf16[2,256,256]{2,1,0:T(8,128)(2,1)S(1)}, bf16[2,256,256]{2,1,0:T(8,128)(2,1)}, u32[]{:S(2)}) copy-start(bf16[2,256,256]{2,1,0:T(8,128)(2,1)} %s_out.3) | copy-start | bytes 786436
  3.8 13.3 %copy-start.7 = (bf16[256,512]{1,0:T(8,128)(2,1)S(1)}, bf16[256,512]{1,0:T(8,128)(2,1)}, u32[]{:S(2)}) copy-start(bf16[256,512]{1,0:T(8,128)(2,1)} %proj.3) | copy-start | bytes 786436
  3.8 13.3 %copy-start.8 = (bf16[1,24,12,256]{3,1,2,0:T(8,128)(2,1)S(1)}, bf16[1,24,12,256]{3,1,2,0:T(8,128)(2,1)}, u32[]{:S(2)}) copy-start(bf16[1,24,12,256]{3,1,2,0:T(8,128)(2,1)} %param.19) | copy-start | bytes 442372
  8.0 13.8 %collective-permute-start.1 = (bf16[80,512]{1,0:T(8,128)(2,1)S(1)}, bf16[80,512]{1,0:T(8,128)(2,1)S(1)}, u32[]{:S(2)}, u32[]{:S(2)}) collective-permute-start(bf16[80,512]{1,0:T(8,128)(2,1)S(1)} %get-tuple-element.36), channel_id=1, source_target_pairs={{0,0},{32,64},{64,32},{96,128},{128,96},{160,192},{192,160},{224,2... | collective-permute-start | bytes 245768 | tf_op jit(solution)/shard_map/ppermute | solution.py:564
  17.0 4.8 %collective-permute-start.2 = (bf16[80,512]{1,0:T(8,128)(2,1)S(1)}, bf16[80,512]{1,0:T(8,128)(2,1)S(1)}, u32[]{:S(2)}, u32[]{:S(2)}) collective-permute-start(bf16[80,512]{1,0:T(8,128)(2,1)S(1)} %get-tuple-element.37), channel_id=1, source_target_pairs={{0,32},{32,0},{64,96},{96,64},{128,160},{160,128},{192,224},{224,1... | collective-permute-start | bytes 245768 | tf_op jit(solution)/shard_map/ppermute | solution.py:565
  17.1 4.6 %copy-start.2 = (bf16[128,176]{1,0:T(8,128)(2,1)S(1)}, bf16[128,176]{1,0:T(8,128)(2,1)}, u32[]{:S(2)}) copy-start(bf16[128,176]{1,0:T(8,128)(2,1)} %constant.26.clone.pack) | copy-start | bytes 135172
  17.1 4.6 %copy-start.3 = (bf16[112,80]{1,0:T(8,128)(2,1)S(1)}, bf16[112,80]{1,0:T(8,128)(2,1)}, u32[]{:S(2)}) copy-start(bf16[112,80]{1,0:T(8,128)(2,1)} %constant.25.clone.open_rows) | copy-start | bytes 53764
  22.5 9.1 %collective-permute-start.3 = (bf16[112,512]{1,0:T(8,128)(2,1)S(1)}, bf16[112,512]{1,0:T(8,128)(2,1)S(1)}, u32[]{:S(2)}, u32[]{:S(2)}) collective-permute-start(bf16[112,512]{1,0:T(8,128)(2,1)S(1)} %get-tuple-element.40), channel_id=1, source_target_pairs={{0,30},{2,4},{4,2},{6,8},{8,6},{10,12},{12,10},{14,16},{16,14},{18... | collective-permute-start | bytes 344072 | tf_op jit(solution)/shard_map/ppermute | solution.py:581
  28.5 4.8 %collective-permute-start.4 = (bf16[112,512]{1,0:T(8,128)(2,1)S(1)}, bf16[112,512]{1,0:T(8,128)(2,1)S(1)}, u32[]{:S(2)}, u32[]{:S(2)}) collective-permute-start(bf16[112,512]{1,0:T(8,128)(2,1)S(1)} %get-tuple-element.41), channel_id=1, source_target_pairs={{0,2},{2,0},{4,6},{6,4},{8,10},{10,8},{12,14},{14,12},{16,18},{18,... | collective-permute-start | bytes 344072 | tf_op jit(solution)/shard_map/ppermute | solution.py:582
  28.5 4.8 %copy-start.4 = (bf16[2,512,512]{2,1,0:T(8,128)(2,1)S(1)}, bf16[2,512,512]{2,1,0:T(8,128)(2,1)}, u32[]{:S(2)}) copy-start(bf16[2,512,512]{2,1,0:T(8,128)(2,1)} %t_out.3) | copy-start | bytes 3145732
  28.5 4.8 %copy-start.9 = (bf16[320,400]{1,0:T(8,128)(2,1)S(1)}, bf16[320,400]{1,0:T(8,128)(2,1)}, u32[]{:S(2)}) copy-start(bf16[320,400]{1,0:T(8,128)(2,1)} %constant.29.clone.g_to_a) | copy-start | bytes 768004
  28.5 4.8 %copy-start.11 = (bf16[384,320]{1,0:T(8,128)(2,1)S(1)}, bf16[384,320]{1,0:T(8,128)(2,1)}, u32[]{:S(2)}) copy-start(bf16[384,320]{1,0:T(8,128)(2,1)} %constant.28.clone.from_a) | copy-start | bytes 737284
  28.5 4.8 %copy-start.12 = (bf16[176,112]{1,0:T(8,128)(2,1)S(1)}, bf16[176,112]{1,0:T(8,128)(2,1)}, u32[]{:S(2)}) copy-start(bf16[176,112]{1,0:T(8,128)(2,1)} %constant.27.clone.open_cols) | copy-start | bytes 118276

commit v5 on v4

--- a/solution.py
+++ b/solution.py
@@ -524,9 +524,9 @@
     ]
 
 
-def swaps(size, start, closed):
-    route = {i: i for i in range(size)}
-    for i in range(start, size if closed else size - 1, 2):
+def swaps(size, start):
+    route = {}
+    for i in range(start, size, 2):
         j = (i + 1) % size
         route[i], route[j] = j, i
     return sorted(route.items())
@@ -561,8 +561,8 @@
         + [pltpu.with_memory_space_constraint(t_out, pltpu.HBM)],
         [pltpu.VMEM((COLS, TALL, width), BF)] + buffers(t_out[0]), 3 * 10**9,
     )
-    rows_1 = lax.ppermute(rows_1, "lat", swaps(lat_size, 1, False))
-    rows_2 = lax.ppermute(rows_2, "lat", swaps(lat_size, 0, False))
+    rows_2 = lax.ppermute(rows_2, "lat", swaps(lat_size, 0))
+    rows_1 = lax.ppermute(rows_1, "lat", swaps(lat_size, 1))
 
     g0, save0, save1, q, k, v, c_att = call(
         beside_rows, "beside_rows",
@@ -578,8 +578,8 @@
         [VMEM] * 5 + [ANY],
         [spread, rows_1, rows_2, OPEN_ROWS, PACK_COLS, g0], (), 10**7,
     )
-    cols_1 = lax.ppermute(cols_1, "lon", swaps(lon_size, 1, True))
-    cols_2 = lax.ppermute(cols_2, "lon", swaps(lon_size, 0, True))
+    cols_2 = lax.ppermute(cols_2, "lon", swaps(lon_size, 0))
+    cols_1 = lax.ppermute(cols_1, "lon", swaps(lon_size, 1))
 
     k_edge, v_edge, n_att, s_att = call(
         beside_columns, "beside_columns",

time: 41.3 us -> 40.5 us (0.981)
  the two profiles are of different devices: /device:TPU:6 before, /device:TPU:2 now
where the time goes in v5:
time: 40.5 us; the launch traced here: 40.4 us
  Pallas kernels  21.2 us (52%)
  starting transfers between devices  14.5 us (36%)
  waiting for transfers between devices  3.71 us (9%)
  between operations  0.85 us (2%)
    pallas_call x6, Pallas kernels, call(): pl.pallas_call(kernel, name=name, out_shape=shapes, in_specs=specs, out_s...  21.2 us
    ppermute x1, starting transfers between devices, shards(): rows_2 = lax.ppermute(rows_2, 'lat', swaps(lat_size, 0))  8.43 us
    ppermute x1, starting transfers between devices, shards(): cols_1 = lax.ppermute(cols_1, 'lon', swaps(lon_size, 1))  4.38 us
    ppermute x1, waiting for transfers between devices, shards(): cols_1 = lax.ppermute(cols_1, 'lon', swaps(lon_size, 1))  3.39 us
    ppermute x1, starting transfers between devices, shards(): rows_1 = lax.ppermute(rows_1, 'lat', swaps(lat_size, 1))  1.58 us
  transfers between devices with their start and end apart: 5, of which 2 were waited for; matrix products, arithmetic and copies ran while one was open for 0% of the time, Pallas kernels for 21%

profile of v5, /device:TPU:2, one launch (start us, length us, event | category | flops | bytes accessed | tf_op | source)
XLA Modules:
  0.0 40.4 jit_solution(10360508352929550678)
XLA Ops:
  0.6 0.1 collective-permute-start
  0.7 0.0 copy-start.1
  0.8 0.0 copy-start.10
  0.8 0.0 copy-start.13
  0.8 2.9 %teacher_own.1 = (bf16[320,512]{1,0:T(8,128)(2,1)S(1)}, bf16[320,128]{1,0:T(8,128)(2,1)S(1)}, bf16[320,128]{1,0:T(8,128)(2,1)S(1)}, bf16[320,512]{1,0:T(8,128)(2...) custom-call(bf16[1,12,24,512]{3,2,1,0:T(8,128)(2,1)} %bitcast.7, s32[12,2,24]{2,1,0:T(2,128)} %bitcast.8, ...), custom_call_target="tpu_custom_call" | custom-call | flops 1000000000 | bytes 3711744 | tf_op jit(solution)/shard_map/teacher_own/pallas_call | solution.py:509
  3.7 0.0 collective-permute-done.far_ref
  3.7 0.0 copy-start.5
  3.7 0.0 copy-start.6
  3.8 0.0 copy-start.7
  3.8 0.0 copy-start.8
  3.8 4.2 %teacher_first.1 = (bf16[320,512]{1,0:T(8,128)(2,1)S(1)}, bf16[400,640]{1,0:T(8,128)(2,1)S(1)}, bf16[80,512]{1,0:T(8,128)(2,1)S(1)}, bf16[80,512]{1,0:T(8,128)(2,1)S(1)}) custom-call(bf16[1,12,24,512]{3,2,1,0:T(8,128)(2,1)S(1)} %collective-permute-done.far_ref, bf16[320,512]{1,0:T(8,128)(2,1)S(1)} %get-tuple-element.28.x_ref, ...), custom_call_target="tpu_custom_call" | custom-call | flops 3000000000 | bytes 6494208 | tf_op jit(solution)/shard_map/teacher_first/pallas_call | solution.py:509
  8.0 1.6 %collective-permute-start.1 = (bf16[80,512]{1,0:T(8,128)(2,1)S(1)}, bf16[80,512]{1,0:T(8,128)(2,1)S(1)}, u32[]{:S(2)}, u32[]{:S(2)}) collective-permute-start(bf16[80,512]{1,0:T(8,128)(2,1)S(1)} %get-tuple-element.36), channel_id=1, source_target_pairs={{0,224},{32,64},{64,32},{96,128},{128,96},{160,192},{192,160},{224... | collective-permute-start | bytes 245768 | tf_op jit(solution)/shard_map/ppermute | solution.py:565
  9.5 8.4 %collective-permute-start.2 = (bf16[80,512]{1,0:T(8,128)(2,1)S(1)}, bf16[80,512]{1,0:T(8,128)(2,1)S(1)}, u32[]{:S(2)}, u32[]{:S(2)}) collective-permute-start(bf16[80,512]{1,0:T(8,128)(2,1)S(1)} %get-tuple-element.37), channel_id=1, source_target_pairs={{0,32},{32,0},{64,96},{96,64},{128,160},{160,128},{192,224},{224,1... | collective-permute-start | bytes 245768 | tf_op jit(solution)/shard_map/ppermute | solution.py:564
  18.0 0.0 copy-start.2
  18.0 0.0 copy-start.3
  18.0 4.6 %beside_rows.1 = (f32[320,256]{1,0:T(8,128)S(1)}, bf16[320,2816]{1,0:T(8,128)(2,1)S(1)}, bf16[320,2816]{1,0:T(8,128)(2,1)S(1)}, bf16[400,512]{1,0:T(8,128)(2,1)S...) custom-call(bf16[1,12,24,256]{3,2,1,0:T(8,128)(2,1)S(1)} %bitcast.5, ...), custom_call_target="tpu_custom_call" | custom-call | flops 5000000000 | bytes 5771264 | tf_op jit(solution)/shard_map/beside_rows/pallas_call | solution.py:509
  22.6 0.7 %send_columns.1 = (bf16[224,640]{1,0:T(8,128)(2,1)S(1)}, bf16[112,512]{1,0:T(8,128)(2,1)S(1)}, bf16[112,512]{1,0:T(8,128)(2,1)S(1)}) custom-call(bf16[400,640]{1,0:T(8,128)(2,1)S(1)} %get-tuple-element.35.g_ref, bf16[80,512]{1,0:T(8,128)(2,1)S(1)} %collective-permute-done.1.first_ref, bf16[80,512]{1,0:T(8,128)(2,1)S(1)} %collective-permute-done.2.second_ref, ...), custom_call_target="tpu_custom_call" | custom-call | flops 10000000 | bytes 1066496 | tf_op jit(solution)/shard_map/send_columns/pallas_call | solution.py:509
  23.4 4.4 %collective-permute-start.3 = (bf16[112,512]{1,0:T(8,128)(2,1)S(1)}, bf16[112,512]{1,0:T(8,128)(2,1)S(1)}, u32[]{:S(2)}, u32[]{:S(2)}) collective-permute-start(bf16[112,512]{1,0:T(8,128)(2,1)S(1)} %get-tuple-element.40), channel_id=1, source_target_pairs={{0,30},{2,4},{4,2},{6,8},{8,6},{10,12},{12,10},{14,16},{16,14},{18... | collective-permute-start | bytes 344072 | tf_op jit(solution)/shard_map/ppermute | solution.py:582
  27.7 0.0 collective-permute-start.4
  27.8 0.0 copy-start.12
  27.8 1.1 %beside_columns.1 = (bf16[224,512]{1,0:T(8,128)(2,1)S(1)}, bf16[224,512]{1,0:T(8,128)(2,1)S(1)}, bf16[48,512]{1,0:T(8,128)(2,1)S(1)}, bf16[48,512]{1,0:T(8,128)(2,1)S(1)}) custom-call(bf16[400,640]{1,0:T(8,128)(2,1)S(1)} %get-tuple-element.35.g_ref, bf16[224,640]{1,0:T(8,128)(2,1)S(1)} %get-tuple-element.39.edge_ref, bf16[2,512,1536]{2,1,0:T(8,128)(2,1)S(1)} %copy-done, ...), custom_call_target="tpu_custom_call" | custom-call | flops 2000000000 | bytes 5173248 | tf_op jit(solution)/shard_map/beside_columns/pallas_call | solution.py:509
  28.8 3.4 %collective-permute-done.3.first_ref = bf16[112,512]{1,0:T(8,128)(2,1)S(1)} collective-permute-done((bf16[112,512]{1,0:T(8,128)(2,1)S(1)}, bf16[112,512]{1,0:T(8,128)(2,1)S(1)}, u32[]{:S(2)}, u32[]{:S(2)}) %collective-permute-start.3) | collective-permute-done | bytes 114720 | tf_op jit(solution)/shard_map/ppermute | solution.py:582
  32.2 0.3 collective-permute-done.4.second_ref
  32.6 7.8 %teacher_second.1 = (bf16[1,12,24,512]{3,2,1,0:T(8,128)(2,1)}, f32[1,12,24,256]{3,2,1,0:T(8,128)}) custom-call(bf16[320,512]{1,0:T(8,128)(2,1)S(1)} %get-tuple-element.34.after_ref.h_ref, bf16[400,640]{1,0:T(8,128)(2,1)S(1)} %get-tuple-element.35.g_ref, bf16[224,640]{1,0:T(8,128)(2,1)S(1)} %get-tuple-element.39.edge_ref, ...), custom_call_target="tpu_custom_call" | custom-call | flops 6000000000 | bytes 13201920 | tf_op jit(solution)/shard_map/teacher_second/pallas_call | solution.py:509
  (20 shorter events, 0.0 us)
Async XLA Ops:
  0.6 3.1 %collective-permute-start = (bf16[1,12,24,512]{3,2,1,0:T(8,128)(2,1)}, bf16[1,12,24,512]{3,2,1,0:T(8,128)(2,1)S(1)}, u32[]{:S(2)}, u32[]{:S(2)}) collective-permute-start(bf16[1,12,24,512]{3,2,1,0:T(8,128)(2,1)} %bitcast.6), channel_id=1, source_target_pairs={{0,1},{1,0},{2,3},{3,2},{4,5},{5,4},{6,7},{7,6},{8,9},{9,8},{10,11... | collective-permute-start | bytes 884744 | tf_op jit(solution)/shard_map/ppermute | solution.py:542
  0.7 3.0 %copy-start = (bf16[2,512,1536]{2,1,0:T(8,128)(2,1)S(1)}, bf16[2,512,1536]{2,1,0:T(8,128)(2,1)}, u32[]{:S(2)}) copy-start(bf16[2,512,1536]{2,1,0:T(8,128)(2,1)} %t_qkv.9) | copy-start | bytes 9437188
  0.7 3.0 %copy-start.1 = (bf16[320,384]{1,0:T(8,128)(2,1)S(1)}, bf16[320,384]{1,0:T(8,128)(2,1)}, u32[]{:S(2)}) copy-start(bf16[320,384]{1,0:T(8,128)(2,1)} %constant.20.clone.to_a_hbm.to_a) | copy-start | bytes 737284
  0.8 3.0 %copy-start.10 = (bf16[400,320]{1,0:T(8,128)(2,1)S(1)}, bf16[400,320]{1,0:T(8,128)(2,1)}, u32[]{:S(2)}) copy-start(bf16[400,320]{1,0:T(8,128)(2,1)} %constant.23.clone.a_to_g) | copy-start | bytes 768004
  0.8 3.0 %copy-start.13 = (bf16[128,112]{1,0:T(8,128)(2,1)S(1)}, bf16[128,112]{1,0:T(8,128)(2,1)}, u32[]{:S(2)}) copy-start(bf16[128,112]{1,0:T(8,128)(2,1)} %constant.24.clone.pack) | copy-start | bytes 86020
  3.7 14.2 %copy-start.5 = (bf16[2,256,768]{2,1,0:T(8,128)(2,1)S(1)}, bf16[2,256,768]{2,1,0:T(8,128)(2,1)}, u32[]{:S(2)}) copy-start(bf16[2,256,768]{2,1,0:T(8,128)(2,1)} %s_qkv.3) | copy-start | bytes 2359300
  3.7 14.2 %copy-start.6 = (bf16[2,256,256]{2,1,0:T(8,128)(2,1)S(1)}, bf16[2,256,256]{2,1,0:T(8,128)(2,1)}, u32[]{:S(2)}) copy-start(bf16[2,256,256]{2,1,0:T(8,128)(2,1)} %s_out.3) | copy-start | bytes 786436
  3.8 14.2 %copy-start.7 = (bf16[256,512]{1,0:T(8,128)(2,1)S(1)}, bf16[256,512]{1,0:T(8,128)(2,1)}, u32[]{:S(2)}) copy-start(bf16[256,512]{1,0:T(8,128)(2,1)} %proj.3) | copy-start | bytes 786436
  3.8 14.2 %copy-start.8 = (bf16[1,24,12,256]{3,1,2,0:T(8,128)(2,1)S(1)}, bf16[1,24,12,256]{3,1,2,0:T(8,128)(2,1)}, u32[]{:S(2)}) copy-start(bf16[1,24,12,256]{3,1,2,0:T(8,128)(2,1)} %param.19) | copy-start | bytes 442372
  8.0 14.6 %collective-permute-start.1 = (bf16[80,512]{1,0:T(8,128)(2,1)S(1)}, bf16[80,512]{1,0:T(8,128)(2,1)S(1)}, u32[]{:S(2)}, u32[]{:S(2)}) collective-permute-start(bf16[80,512]{1,0:T(8,128)(2,1)S(1)} %get-tuple-element.36), channel_id=1, source_target_pairs={{0,224},{32,64},{64,32},{96,128},{128,96},{160,192},{192,160},{224... | collective-permute-start | bytes 245768 | tf_op jit(solution)/shard_map/ppermute | solution.py:565
  9.5 13.1 %collective-permute-start.2 = (bf16[80,512]{1,0:T(8,128)(2,1)S(1)}, bf16[80,512]{1,0:T(8,128)(2,1)S(1)}, u32[]{:S(2)}, u32[]{:S(2)}) collective-permute-start(bf16[80,512]{1,0:T(8,128)(2,1)S(1)} %get-tuple-element.37), channel_id=1, source_target_pairs={{0,32},{32,0},{64,96},{96,64},{128,160},{160,128},{192,224},{224,1... | collective-permute-start | bytes 245768 | tf_op jit(solution)/shard_map/ppermute | solution.py:564
  18.0 4.6 %copy-start.2 = (bf16[128,176]{1,0:T(8,128)(2,1)S(1)}, bf16[128,176]{1,0:T(8,128)(2,1)}, u32[]{:S(2)}) copy-start(bf16[128,176]{1,0:T(8,128)(2,1)} %constant.26.clone.pack) | copy-start | bytes 135172
  18.0 4.6 %copy-start.3 = (bf16[112,80]{1,0:T(8,128)(2,1)S(1)}, bf16[112,80]{1,0:T(8,128)(2,1)}, u32[]{:S(2)}) copy-start(bf16[112,80]{1,0:T(8,128)(2,1)} %constant.25.clone.open_rows) | copy-start | bytes 53764
  23.4 8.9 %collective-permute-start.3 = (bf16[112,512]{1,0:T(8,128)(2,1)S(1)}, bf16[112,512]{1,0:T(8,128)(2,1)S(1)}, u32[]{:S(2)}, u32[]{:S(2)}) collective-permute-start(bf16[112,512]{1,0:T(8,128)(2,1)S(1)} %get-tuple-element.40), channel_id=1, source_target_pairs={{0,30},{2,4},{4,2},{6,8},{8,6},{10,12},{12,10},{14,16},{16,14},{18... | collective-permute-start | bytes 344072 | tf_op jit(solution)/shard_map/ppermute | solution.py:582
  27.7 4.8 %collective-permute-start.4 = (bf16[112,512]{1,0:T(8,128)(2,1)S(1)}, bf16[112,512]{1,0:T(8,128)(2,1)S(1)}, u32[]{:S(2)}, u32[]{:S(2)}) collective-permute-start(bf16[112,512]{1,0:T(8,128)(2,1)S(1)} %get-tuple-element.41), channel_id=1, source_target_pairs={{0,2},{2,0},{4,6},{6,4},{8,10},{10,8},{12,14},{14,12},{16,18},{18,... | collective-permute-start | bytes 344072 | tf_op jit(solution)/shard_map/ppermute | solution.py:581
  27.7 4.8 %copy-start.4 = (bf16[2,512,512]{2,1,0:T(8,128)(2,1)S(1)}, bf16[2,512,512]{2,1,0:T(8,128)(2,1)}, u32[]{:S(2)}) copy-start(bf16[2,512,512]{2,1,0:T(8,128)(2,1)} %t_out.3) | copy-start | bytes 3145732
  27.7 4.8 %copy-start.9 = (bf16[320,400]{1,0:T(8,128)(2,1)S(1)}, bf16[320,400]{1,0:T(8,128)(2,1)}, u32[]{:S(2)}) copy-start(bf16[320,400]{1,0:T(8,128)(2,1)} %constant.29.clone.g_to_a) | copy-start | bytes 768004
  27.8 4.8 %copy-start.11 = (bf16[384,320]{1,0:T(8,128)(2,1)S(1)}, bf16[384,320]{1,0:T(8,128)(2,1)}, u32[]{:S(2)}) copy-start(bf16[384,320]{1,0:T(8,128)(2,1)} %constant.28.clone.from_a) | copy-start | bytes 737284
  27.8 4.8 %copy-start.12 = (bf16[176,112]{1,0:T(8,128)(2,1)S(1)}, bf16[176,112]{1,0:T(8,128)(2,1)}, u32[]{:S(2)}) copy-start(bf16[176,112]{1,0:T(8,128)(2,1)} %constant.27.clone.open_cols) | copy-start | bytes 118276

commit v6 on v5

--- a/solution.py
+++ b/solution.py
@@ -146,12 +146,27 @@
     return id_query.astype(F32)[:, 0:1] == row
 
 
-def attend(q, k, v, mask):
-    pairs = [slice(i, i + PAIR) for i in range(0, q.shape[1], PAIR)]
-    scores = [dot_nt(q[:, p], stack_heads(k[:, p])) for p in pairs]
-    es = [jnp.where(mask, jnp.exp2(s), 0.0).astype(BF) for s in scores]
-    both = [dot(e, stack_values(v[:, p])) for e, p in zip(es, pairs)]
-    return [b[:, :PAIR] for b in both], [b[:, PAIR:] for b in both], es
+def pairs_of(x):
+    return [x[:, i : i + PAIR] for i in range(0, x.shape[1], PAIR)]
+
+
+def attend(windows):
+    scores = [
+        [dot_nt(qp, stack_heads(kp)) for qp, kp in zip(pairs_of(q), pairs_of(k))]
+        for q, k, _, _ in windows
+    ]
+    es = [
+        [jnp.where(w[3], jnp.exp2(s), 0.0).astype(BF) for s in group]
+        for w, group in zip(windows, scores)
+    ]
+    both = [
+        [dot(e, stack_values(vp)) for e, vp in zip(group, pairs_of(w[2]))]
+        for w, group in zip(windows, es)
+    ]
+    return [
+        ([b[:, :PAIR] for b in group], [b[:, PAIR:] for b in group], e)
+        for group, e in zip(both, es)
+    ]
 
 
 def to_window_order(x_ref, pad_ref, to_a):
@@ -194,10 +209,9 @@
     k = k.astype(BF)
     v = qkv[:, 2 * WIDE :].astype(BF)
     atts = []
-    for w in range(4):
-        rows = slice(w * WIN, (w + 1) * WIN)
-        mask = id_mask(ids[rows], ids[rows])
-        nums, dens, es = attend(q[rows], k[rows], v[rows], mask)
+    windows = [slice(w * WIN, (w + 1) * WIN) for w in range(4)]
+    found = attend([(q[r], k[r], v[r], id_mask(ids[r], ids[r])) for r in windows])
+    for rows, (nums, dens, es) in zip(windows, found):
         z = 1.0 / jnp.concatenate(dens, axis=1)
         att = jnp.concatenate(nums, axis=1) * z
         save_ref[rows, 4 * WIDE : 5 * WIDE] = z.astype(BF)
@@ -228,21 +242,20 @@
     drop = (datt * part(3).astype(F32)).astype(BF) * jnp.asarray(-1.0, BF)
     datt = datt.astype(BF)
     q, k, v = part(0), part(1), part(2)
-    dqs, dks, dvs = [], [], []
-    for w in range(4):
-        rows = slice(w * WIN, (w + 1) * WIN)
-        pairs = [slice(i, i + PAIR) for i in range(0, WIDE, PAIR)]
-        es = [save_ref[rows, (9 + i) * WIDE : (9 + i) * WIDE + 2 * WIN] for i in range(2)]
-        dws = [
-            dot_nt(
-                jnp.concatenate([datt[rows, p], drop[rows, p]], axis=1), stack_values(v[rows, p])
-            )
-            for p in pairs
-        ]
-        dvs.append([unstack_heads(dot_tn(e, datt[rows, p])) for e, p in zip(es, pairs)])
-        dss = [(e.astype(F32) * dw).astype(BF) for e, dw in zip(es, dws)]
-        dqs.append([dot(ds, stack_heads(k[rows, p])) for ds, p in zip(dss, pairs)])
-        dks.append([unstack_heads(dot_tn(ds, q[rows, p])) for ds, p in zip(dss, pairs)])
+    windows = [slice(w * WIN, (w + 1) * WIN) for w in range(4)]
+    blocks_of = [(r, slice(i, i + PAIR)) for r in windows for i in range(0, WIDE, PAIR)]
+    es = [
+        save_ref[r, (9 + i) * WIDE : (9 + i) * WIDE + 2 * WIN] for r in windows for i in range(2)
+    ]
+    dws = [
+        dot_nt(jnp.concatenate([datt[r, p], drop[r, p]], axis=1), stack_values(v[r, p]))
+        for r, p in blocks_of
+    ]
+    dv = [unstack_heads(dot_tn(e, datt[r, p])) for e, (r, p) in zip(es, blocks_of)]
+    dss = [(e.astype(F32) * dw).astype(BF) for e, dw in zip(es, dws)]
+    dq = [dot(ds, stack_heads(k[r, p])) for ds, (r, p) in zip(dss, blocks_of)]
+    dk = [unstack_heads(dot_tn(ds, q[r, p])) for ds, (r, p) in zip(dss, blocks_of)]
+    dqs, dks, dvs = [[x[i : i + 2] for i in range(0, len(x), 2)] for x in (dq, dk, dv)]
     dqs, dks, dvs = [[jnp.concatenate(x, axis=1) for x in y] for y in (dqs, dks, dvs)]
     dq = 10.0 * jnp.concatenate(dqs, axis=0)
     dk = (1.0 / LOG2E) * jnp.concatenate(dks, axis=0)
@@ -295,7 +308,7 @@
     far = to_window_order(far_ref, pad_ref, to_a[...])
     k_far = unit(dot(far, t_qkv[0, :, width : 2 * width]), blocks)[0].astype(BF)
     v_far = dot(far, t_qkv[0, :, 2 * width :]).astype(BF)
-    atts = []
+    windows = []
     for w in range(4):
         rows = slice(w * WIN, (w + 1) * WIN)
         id_keys = jnp.concatenate([id_ref[rows], far_id_ref[rows]], axis=0)
@@ -303,7 +316,8 @@
             jnp.concatenate([near[rows], away[rows]], axis=0)
             for near, away in ((k_ref, k_far), (v_ref, v_far))
         ]
-        atts.append(window_attention(q_ref[rows], keys, (id_ref[rows], id_keys)))
+        windows.append((q_ref[rows], keys, (id_ref[rows], id_keys)))
+    atts = window_attention(windows)
     copies[0].wait()
     h = residual(x_ref[...], jnp.concatenate(atts, axis=0), wout[...])[0]
     h_ref[...] = h
@@ -391,9 +405,12 @@
     return blocks[0] if len(blocks) == 1 else jnp.concatenate(blocks, axis=0)
 
 
-def window_attention(q, keys, ids):
-    nums, dens, _ = attend(q, *keys, id_mask(*ids))
-    return jnp.concatenate([(n / d).astype(BF) for n, d in zip(nums, dens)], axis=1)
+def window_attention(windows):
+    found = attend([(q, k, v, id_mask(*ids)) for q, (k, v), ids in windows])
+    return [
+        jnp.concatenate([(n / d).astype(BF) for n, d in zip(nums, dens)], axis=1)
+        for nums, dens, _ in found
+    ]
 
 
 def beside_rows(
@@ -416,11 +433,11 @@
     k_ref[...] = k
     v_ref[...] = v
     ids = part(g_ref, "c")[:, width:]
-    att_ref[...] = window_attention(part(q, "c"), [part(k, "c"), part(v, "c")], (ids, ids))
+    [att_ref[...]] = window_attention([(part(q, "c"), [part(k, "c"), part(v, "c")], (ids, ids))])
 
 
 def send_columns(
-    g_ref, first_ref, second_ref, open_rows, pack, after_ref, edge_ref, out_first, out_second
+    g_ref, second_ref, first_ref, open_rows, pack, after_ref, edge_ref, out_first, out_second
 ):
     width = first_ref.shape[1]
     lat = lax.axis_index("lat")
@@ -451,15 +468,17 @@
     v = dot(rows, t_qkv[1, :, 2 * width :]).astype(BF)
     k_out[...] = k
     v_out[...] = v
-    for name, ref in (("n", n_ref), ("s", s_ref)):
+    windows = []
+    for name in ("n", "s"):
         items = (("", name),) + EXTRA[name]
         keys = [gather([(own, OWN), (edge, EDGE)], items) for own, edge in ((k_ref, k), (v_ref, v))]
         ids = [gather([(g_ref, OWN), (edge_ref, EDGE)], some)[:, width:] for some in (items[:1], items)]
-        ref[...] = window_attention(part(q_ref, name), keys, ids)
+        windows.append((part(q_ref, name), keys, ids))
+    n_ref[...], s_ref[...] = window_attention(windows)
 
 
 def teacher_second(
-    h_ref, g_ref, edge_ref, first_ref, second_ref, q_ref, k_ref, v_ref, k_edge, v_edge,
+    h_ref, g_ref, edge_ref, second_ref, first_ref, q_ref, k_ref, v_ref, k_edge, v_edge,
     c_ref, n_ref, s_ref, open_cols, from_a, g_to_a, t_qkv, t_out, proj, s_qkv, s_out,
     g0_ref, save0, save1, out_ref, grad_ref,
 ):
@@ -472,6 +491,7 @@
     k = unit(dot(rows, t_qkv[1, :, width : 2 * width]), blocks)[0].astype(BF)
     v = dot(rows, t_qkv[1, :, 2 * width :]).astype(BF)
     atts = {"c": c_ref[...], "n": n_ref[...], "s": s_ref[...]}
+    windows = []
     for name in LATE:
         items = (("", name),) + EXTRA[name]
         keys = [
@@ -482,7 +502,8 @@
             gather([(g_ref, OWN), (edge_ref, EDGE), (came, COME)], some)[:, width:]
             for some in (items[:1], items)
         ]
-        atts[name] = window_attention(part(q_ref, name), keys, ids)
+        windows.append((part(q_ref, name), keys, ids))
+    atts.update(zip(LATE, window_attention(windows)))
     att = jnp.concatenate([atts[name] for name in ORDER], axis=0)
     att = dot(g_to_a[...], att).astype(BF)
     teacher = residual(h_ref[...], att, t_out[1])[0]
@@ -576,7 +597,7 @@
         send_columns, "send_columns",
         [((NE_ROWS, wide), BF)] + [((COL_SENT, width), BF)] * 2,
         [VMEM] * 5 + [ANY],
-        [spread, rows_1, rows_2, OPEN_ROWS, PACK_COLS, g0], (), 10**7,
+        [spread, rows_2, rows_1, OPEN_ROWS, PACK_COLS, g0], (), 10**7,
     )
     cols_2 = lax.ppermute(cols_2, "lon", swaps(lon_size, 0))
     cols_1 = lax.ppermute(cols_1, "lon", swaps(lon_size, 1))
@@ -587,7 +608,7 @@
         [VMEM] * 6,
         [spread, edge, t_qkv, q, k, v], (), 2 * 10**9,
     )
-    args = [hidden, spread, edge, cols_1, cols_2, q, k, v, k_edge, v_edge, c_att, n_att, s_att]
+    args = [hidden, spread, edge, cols_2, cols_1, q, k, v, k_edge, v_edge, c_att, n_att, s_att]
     args += [OPEN_COLS, FROM_A, G_TO_A, t_qkv, t_out, s_proj, s_qkv, s_out, g0, save0, save1]
     out, grad = call(
         teacher_second, "teacher_second",

time: 40.5 us -> 39.4 us (0.973)
  the two profiles are of different devices: /device:TPU:2 before, /device:TPU:128 now
where the time goes in v6:
time: 39.4 us; the launch traced here: 39.2 us
  Pallas kernels  19 us (48%)
  waiting for transfers between devices  13.9 us (35%)
  starting transfers between devices  5.52 us (14%)
  between operations  0.82 us (2%)
    pallas_call x6, Pallas kernels, call(): pl.pallas_call(kernel, name=name, out_shape=shapes, in_specs=specs, out_s...  19 us
    ppermute x1, waiting for transfers between devices, shards(): rows_1 = lax.ppermute(rows_1, 'lat', swaps(lat_size, 1))  8.16 us
    ppermute x1, waiting for transfers between devices, shards(): cols_1 = lax.ppermute(cols_1, 'lon', swaps(lon_size, 1))  5.49 us
    ppermute x1, starting transfers between devices, shards(): cols_1 = lax.ppermute(cols_1, 'lon', swaps(lon_size, 1))  2 us
    ppermute x1, starting transfers between devices, shards(): cols_2 = lax.ppermute(cols_2, 'lon', swaps(lon_size, 0))  1.59 us
    ppermute x1, starting transfers between devices, shards(): rows_2 = lax.ppermute(rows_2, 'lat', swaps(lat_size, 0))  1.57 us
  transfers between devices with their start and end apart: 5, of which 3 were waited for; matrix products, arithmetic and copies ran while one was open for 0% of the time, Pallas kernels for 19%

profile of v6, /device:TPU:128, one launch (start us, length us, event | category | flops | bytes accessed | tf_op | source)
XLA Modules:
  0.0 39.2 jit_solution(7976542795078651859)
XLA Ops:
  0.6 0.1 collective-permute-start
  0.7 0.0 copy-start.1
  0.8 0.0 copy-start.10
  0.8 0.0 copy-start.13
  0.8 2.9 %teacher_own.1 = (bf16[320,512]{1,0:T(8,128)(2,1)S(1)}, bf16[320,128]{1,0:T(8,128)(2,1)S(1)}, bf16[320,128]{1,0:T(8,128)(2,1)S(1)}, bf16[320,512]{1,0:T(8,128)(2...) custom-call(bf16[1,12,24,512]{3,2,1,0:T(8,128)(2,1)} %bitcast.7, s32[12,2,24]{2,1,0:T(2,128)} %bitcast.8, ...), custom_call_target="tpu_custom_call" | custom-call | flops 1000000000 | bytes 3711744 | tf_op jit(solution)/shard_map/teacher_own/pallas_call | solution.py:530
  3.7 0.0 collective-permute-done.far_ref
  3.7 0.0 copy-start.5
  3.8 0.0 copy-start.6
  3.8 0.0 copy-start.7
  3.8 0.0 copy-start.8
  3.8 4.2 %teacher_first.1 = (bf16[320,512]{1,0:T(8,128)(2,1)S(1)}, bf16[400,640]{1,0:T(8,128)(2,1)S(1)}, bf16[80,512]{1,0:T(8,128)(2,1)S(1)}, bf16[80,512]{1,0:T(8,128)(2,1)S(1)}) custom-call(bf16[1,12,24,512]{3,2,1,0:T(8,128)(2,1)S(1)} %collective-permute-done.far_ref, bf16[320,512]{1,0:T(8,128)(2,1)S(1)} %get-tuple-element.28.x_ref, ...), custom_call_target="tpu_custom_call" | custom-call | flops 3000000000 | bytes 6494208 | tf_op jit(solution)/shard_map/teacher_first/pallas_call | solution.py:530
  8.0 1.6 %collective-permute-start.1 = (bf16[80,512]{1,0:T(8,128)(2,1)S(1)}, bf16[80,512]{1,0:T(8,128)(2,1)S(1)}, u32[]{:S(2)}, u32[]{:S(2)}) collective-permute-start(bf16[80,512]{1,0:T(8,128)(2,1)S(1)} %get-tuple-element.36), channel_id=1, source_target_pairs={{0,32},{32,0},{64,96},{96,64},{128,160},{160,128},{192,224},{224,1... | collective-permute-start | bytes 245768 | tf_op jit(solution)/shard_map/ppermute | solution.py:585
  9.6 0.3 collective-permute-start.2
  9.9 0.0 copy-start.2
  9.9 0.0 copy-start.3
  9.9 3.7 %beside_rows.1 = (f32[320,256]{1,0:T(8,128)S(1)}, bf16[320,2816]{1,0:T(8,128)(2,1)S(1)}, bf16[320,2816]{1,0:T(8,128)(2,1)S(1)}, bf16[400,512]{1,0:T(8,128)(2,1)S...) custom-call(bf16[1,12,24,256]{3,2,1,0:T(8,128)(2,1)S(1)} %bitcast.5, ...), custom_call_target="tpu_custom_call" | custom-call | flops 5000000000 | bytes 5771264 | tf_op jit(solution)/shard_map/beside_rows/pallas_call | solution.py:530
  13.6 8.2 %collective-permute-done.2.first_ref = bf16[80,512]{1,0:T(8,128)(2,1)S(1)} collective-permute-done((bf16[80,512]{1,0:T(8,128)(2,1)S(1)}, bf16[80,512]{1,0:T(8,128)(2,1)S(1)}, u32[]{:S(2)}, u32[]{:S(2)}) %collective-permute-start.2) | collective-permute-done | bytes 81952 | tf_op jit(solution)/shard_map/ppermute | solution.py:586
  21.8 0.7 %send_columns.1 = (bf16[224,640]{1,0:T(8,128)(2,1)S(1)}, bf16[112,512]{1,0:T(8,128)(2,1)S(1)}, bf16[112,512]{1,0:T(8,128)(2,1)S(1)}) custom-call(bf16[400,640]{1,0:T(8,128)(2,1)S(1)} %get-tuple-element.35.g_ref, bf16[80,512]{1,0:T(8,128)(2,1)S(1)} %collective-permute-done.1.second_ref, bf16[80,512]{1,0:T(8,128)(2,1)S(1)} %collective-permute-done.2.first_ref, ...), custom_call_target="tpu_custom_call" | custom-call | flops 10000000 | bytes 1066496 | tf_op jit(solution)/shard_map/send_columns/pallas_call | solution.py:530
  22.5 1.6 %collective-permute-start.3 = (bf16[112,512]{1,0:T(8,128)(2,1)S(1)}, bf16[112,512]{1,0:T(8,128)(2,1)S(1)}, u32[]{:S(2)}, u32[]{:S(2)}) collective-permute-start(bf16[112,512]{1,0:T(8,128)(2,1)S(1)} %get-tuple-element.40), channel_id=1, source_target_pairs={{0,2},{2,0},{4,6},{6,4},{8,10},{10,8},{12,14},{14,12},{16,18},{18,... | collective-permute-start | bytes 344072 | tf_op jit(solution)/shard_map/ppermute | solution.py:602
  24.1 2.0 %collective-permute-start.4 = (bf16[112,512]{1,0:T(8,128)(2,1)S(1)}, bf16[112,512]{1,0:T(8,128)(2,1)S(1)}, u32[]{:S(2)}, u32[]{:S(2)}) collective-permute-start(bf16[112,512]{1,0:T(8,128)(2,1)S(1)} %get-tuple-element.41), channel_id=1, source_target_pairs={{0,30},{2,4},{4,2},{6,8},{8,6},{10,12},{12,10},{14,16},{16,14},{18... | collective-permute-start | bytes 344072 | tf_op jit(solution)/shard_map/ppermute | solution.py:603
  26.1 1.0 %beside_columns.1 = (bf16[224,512]{1,0:T(8,128)(2,1)S(1)}, bf16[224,512]{1,0:T(8,128)(2,1)S(1)}, bf16[48,512]{1,0:T(8,128)(2,1)S(1)}, bf16[48,512]{1,0:T(8,128)(2,1)S(1)}) custom-call(bf16[400,640]{1,0:T(8,128)(2,1)S(1)} %get-tuple-element.35.g_ref, bf16[224,640]{1,0:T(8,128)(2,1)S(1)} %get-tuple-element.39.edge_ref, bf16[2,512,1536]{2,1,0:T(8,128)(2,1)S(1)} %copy-done, ...), custom_call_target="tpu_custom_call" | custom-call | flops 2000000000 | bytes 5173248 | tf_op jit(solution)/shard_map/beside_columns/pallas_call | solution.py:530
  27.1 0.2 collective-permute-done.3.second_ref
  27.3 5.5 %collective-permute-done.4.first_ref = bf16[112,512]{1,0:T(8,128)(2,1)S(1)} collective-permute-done((bf16[112,512]{1,0:T(8,128)(2,1)S(1)}, bf16[112,512]{1,0:T(8,128)(2,1)S(1)}, u32[]{:S(2)}, u32[]{:S(2)}) %collective-permute-start.4) | collective-permute-done | bytes 114720 | tf_op jit(solution)/shard_map/ppermute | solution.py:603
  32.8 6.4 %teacher_second.1 = (bf16[1,12,24,512]{3,2,1,0:T(8,128)(2,1)}, f32[1,12,24,256]{3,2,1,0:T(8,128)}) custom-call(bf16[320,512]{1,0:T(8,128)(2,1)S(1)} %get-tuple-element.34.after_ref.h_ref, bf16[400,640]{1,0:T(8,128)(2,1)S(1)} %get-tuple-element.35.g_ref, bf16[224,640]{1,0:T(8,128)(2,1)S(1)} %get-tuple-element.39.edge_ref, ...), custom_call_target="tpu_custom_call" | custom-call | flops 6000000000 | bytes 13201920 | tf_op jit(solution)/shard_map/teacher_second/pallas_call | solution.py:530
  (20 shorter events, 0.0 us)
Async XLA Ops:
  0.6 3.1 %collective-permute-start = (bf16[1,12,24,512]{3,2,1,0:T(8,128)(2,1)}, bf16[1,12,24,512]{3,2,1,0:T(8,128)(2,1)S(1)}, u32[]{:S(2)}, u32[]{:S(2)}) collective-permute-start(bf16[1,12,24,512]{3,2,1,0:T(8,128)(2,1)} %bitcast.6), channel_id=1, source_target_pairs={{0,1},{1,0},{2,3},{3,2},{4,5},{5,4},{6,7},{7,6},{8,9},{9,8},{10,11... | collective-permute-start | bytes 884744 | tf_op jit(solution)/shard_map/ppermute | solution.py:563
  0.7 3.0 %copy-start = (bf16[2,512,1536]{2,1,0:T(8,128)(2,1)S(1)}, bf16[2,512,1536]{2,1,0:T(8,128)(2,1)}, u32[]{:S(2)}) copy-start(bf16[2,512,1536]{2,1,0:T(8,128)(2,1)} %t_qkv.9) | copy-start | bytes 9437188
  0.7 3.0 %copy-start.1 = (bf16[320,384]{1,0:T(8,128)(2,1)S(1)}, bf16[320,384]{1,0:T(8,128)(2,1)}, u32[]{:S(2)}) copy-start(bf16[320,384]{1,0:T(8,128)(2,1)} %constant.20.clone.to_a_hbm.to_a) | copy-start | bytes 737284
  0.8 3.0 %copy-start.10 = (bf16[400,320]{1,0:T(8,128)(2,1)S(1)}, bf16[400,320]{1,0:T(8,128)(2,1)}, u32[]{:S(2)}) copy-start(bf16[400,320]{1,0:T(8,128)(2,1)} %constant.23.clone.a_to_g) | copy-start | bytes 768004
  0.8 3.0 %copy-start.13 = (bf16[128,112]{1,0:T(8,128)(2,1)S(1)}, bf16[128,112]{1,0:T(8,128)(2,1)}, u32[]{:S(2)}) copy-start(bf16[128,112]{1,0:T(8,128)(2,1)} %constant.24.clone.pack) | copy-start | bytes 86020
  3.7 6.1 %copy-start.5 = (bf16[2,256,768]{2,1,0:T(8,128)(2,1)S(1)}, bf16[2,256,768]{2,1,0:T(8,128)(2,1)}, u32[]{:S(2)}) copy-start(bf16[2,256,768]{2,1,0:T(8,128)(2,1)} %s_qkv.3) | copy-start | bytes 2359300
  3.8 6.1 %copy-start.6 = (bf16[2,256,256]{2,1,0:T(8,128)(2,1)S(1)}, bf16[2,256,256]{2,1,0:T(8,128)(2,1)}, u32[]{:S(2)}) copy-start(bf16[2,256,256]{2,1,0:T(8,128)(2,1)} %s_out.3) | copy-start | bytes 786436
  3.8 6.1 %copy-start.7 = (bf16[256,512]{1,0:T(8,128)(2,1)S(1)}, bf16[256,512]{1,0:T(8,128)(2,1)}, u32[]{:S(2)}) copy-start(bf16[256,512]{1,0:T(8,128)(2,1)} %proj.3) | copy-start | bytes 786436
  3.8 6.1 %copy-start.8 = (bf16[1,24,12,256]{3,1,2,0:T(8,128)(2,1)S(1)}, bf16[1,24,12,256]{3,1,2,0:T(8,128)(2,1)}, u32[]{:S(2)}) copy-start(bf16[1,24,12,256]{3,1,2,0:T(8,128)(2,1)} %param.19) | copy-start | bytes 442372
  8.0 5.6 %collective-permute-start.1 = (bf16[80,512]{1,0:T(8,128)(2,1)S(1)}, bf16[80,512]{1,0:T(8,128)(2,1)S(1)}, u32[]{:S(2)}, u32[]{:S(2)}) collective-permute-start(bf16[80,512]{1,0:T(8,128)(2,1)S(1)} %get-tuple-element.36), channel_id=1, source_target_pairs={{0,32},{32,0},{64,96},{96,64},{128,160},{160,128},{192,224},{224,1... | collective-permute-start | bytes 245768 | tf_op jit(solution)/shard_map/ppermute | solution.py:585
  9.6 12.2 %collective-permute-start.2 = (bf16[80,512]{1,0:T(8,128)(2,1)S(1)}, bf16[80,512]{1,0:T(8,128)(2,1)S(1)}, u32[]{:S(2)}, u32[]{:S(2)}) collective-permute-start(bf16[80,512]{1,0:T(8,128)(2,1)S(1)} %get-tuple-element.37), channel_id=1, source_target_pairs={{0,224},{32,64},{64,32},{96,128},{128,96},{160,192},{192,160},{224... | collective-permute-start | bytes 245768 | tf_op jit(solution)/shard_map/ppermute | solution.py:586
  9.9 11.9 %copy-start.2 = (bf16[128,176]{1,0:T(8,128)(2,1)S(1)}, bf16[128,176]{1,0:T(8,128)(2,1)}, u32[]{:S(2)}) copy-start(bf16[128,176]{1,0:T(8,128)(2,1)} %constant.26.clone.pack) | copy-start | bytes 135172
  9.9 11.9 %copy-start.3 = (bf16[112,80]{1,0:T(8,128)(2,1)S(1)}, bf16[112,80]{1,0:T(8,128)(2,1)}, u32[]{:S(2)}) copy-start(bf16[112,80]{1,0:T(8,128)(2,1)} %constant.25.clone.open_rows) | copy-start | bytes 53764
  22.5 4.8 %collective-permute-start.3 = (bf16[112,512]{1,0:T(8,128)(2,1)S(1)}, bf16[112,512]{1,0:T(8,128)(2,1)S(1)}, u32[]{:S(2)}, u32[]{:S(2)}) collective-permute-start(bf16[112,512]{1,0:T(8,128)(2,1)S(1)} %get-tuple-element.40), channel_id=1, source_target_pairs={{0,2},{2,0},{4,6},{6,4},{8,10},{10,8},{12,14},{14,12},{16,18},{18,... | collective-permute-start | bytes 344072 | tf_op jit(solution)/shard_map/ppermute | solution.py:602
  24.1 8.7 %collective-permute-start.4 = (bf16[112,512]{1,0:T(8,128)(2,1)S(1)}, bf16[112,512]{1,0:T(8,128)(2,1)S(1)}, u32[]{:S(2)}, u32[]{:S(2)}) collective-permute-start(bf16[112,512]{1,0:T(8,128)(2,1)S(1)} %get-tuple-element.41), channel_id=1, source_target_pairs={{0,30},{2,4},{4,2},{6,8},{8,6},{10,12},{12,10},{14,16},{16,14},{18... | collective-permute-start | bytes 344072 | tf_op jit(solution)/shard_map/ppermute | solution.py:603
  26.1 6.7 %copy-start.4 = (bf16[2,512,512]{2,1,0:T(8,128)(2,1)S(1)}, bf16[2,512,512]{2,1,0:T(8,128)(2,1)}, u32[]{:S(2)}) copy-start(bf16[2,512,512]{2,1,0:T(8,128)(2,1)} %t_out.3) | copy-start | bytes 3145732
  26.1 6.7 %copy-start.9 = (bf16[320,400]{1,0:T(8,128)(2,1)S(1)}, bf16[320,400]{1,0:T(8,128)(2,1)}, u32[]{:S(2)}) copy-start(bf16[320,400]{1,0:T(8,128)(2,1)} %constant.29.clone.g_to_a) | copy-start | bytes 768004
  26.1 6.7 %copy-start.11 = (bf16[384,320]{1,0:T(8,128)(2,1)S(1)}, bf16[384,320]{1,0:T(8,128)(2,1)}, u32[]{:S(2)}) copy-start(bf16[384,320]{1,0:T(8,128)(2,1)} %constant.28.clone.from_a) | copy-start | bytes 737284
  26.1 6.7 %copy-start.12 = (bf16[176,112]{1,0:T(8,128)(2,1)S(1)}, bf16[176,112]{1,0:T(8,128)(2,1)}, u32[]{:S(2)}) copy-start(bf16[176,112]{1,0:T(8,128)(2,1)} %constant.27.clone.open_cols) | copy-start | bytes 118276

commit v7 on v6

--- a/solution.py
+++ b/solution.py
@@ -437,7 +437,7 @@
 
 
 def send_columns(
-    g_ref, second_ref, first_ref, open_rows, pack, after_ref, edge_ref, out_first, out_second
+    g_ref, first_ref, second_ref, open_rows, pack, after_ref, edge_ref, out_first, out_second
 ):
     width = first_ref.shape[1]
     lat = lax.axis_index("lat")
@@ -478,9 +478,9 @@
 
 
 def teacher_second(
-    h_ref, g_ref, edge_ref, second_ref, first_ref, q_ref, k_ref, v_ref, k_edge, v_edge,
+    h_ref, g_ref, edge_ref, first_ref, second_ref, q_ref, k_ref, v_ref, k_edge, v_edge,
     c_ref, n_ref, s_ref, open_cols, from_a, g_to_a, t_qkv, t_out, proj, s_qkv, s_out,
-    g0_ref, save0, save1, out_ref, grad_ref,
+    g0_ref, save0, save1, out_hbm, grad_hbm, out_ref, grad_ref, sems,
 ):
     width = h_ref.shape[1]
     blocks = head_blocks()
@@ -509,14 +509,22 @@
     teacher = residual(h_ref[...], att, t_out[1])[0]
     natural = dot(from_a[...], teacher).astype(BF)
     out_ref[0] = natural.reshape(COLS, TALL, width)[:, :ROWS, :]
+    copies = fetch((out_ref, out_hbm, sems.at[0]))
 
     g = g0_ref[...] - dot_nt(teacher, proj[...])
     g = student_back(g, save1, s_qkv[1], s_out[1])
     g = student_back(g, save0, s_qkv[0], s_out[0])
     high = g.astype(BF)
     low = (g - high.astype(F32)).astype(BF)
-    natural = dot(from_a[...], high) + dot(from_a[...], low)
-    grad_ref[0] = natural.reshape(COLS, TALL, g.shape[1])[:, :ROWS, :]
+    half = COLS // 2
+    for i in range(2):
+        table = from_a[i * half * TALL : (i + 1) * half * TALL]
+        natural = dot(table, high) + dot(table, low)
+        cols = pl.ds(i * half, half)
+        grad_ref[0, cols] = natural.reshape(half, TALL, g.shape[1])[:, :ROWS, :]
+        copies += fetch((grad_ref.at[0, cols], grad_hbm.at[0, cols], sems.at[1 + i]))
+    for copy in copies:
+        copy.wait()
 
 
 VMEM = pl.BlockSpec(memory_space=pltpu.VMEM)
@@ -524,7 +532,7 @@
 HBM = pl.BlockSpec(memory_space=pltpu.HBM)
 
 
-def call(kernel, name, outs, specs, args, scratch=(), flops=0):
+def call(kernel, name, outs, specs, args, scratch=(), flops=0, out_space=VMEM):
     shapes = [jax.ShapeDtypeStruct(s, d) for s, d in outs]
     touched = sum(a.size * a.dtype.itemsize for a in args)
     return pl.pallas_call(
@@ -532,7 +540,7 @@
         name=name,
         out_shape=shapes,
         in_specs=specs,
-        out_specs=[VMEM] * len(outs),
+        out_specs=[out_space] * len(outs),
         scratch_shapes=list(scratch),
         compiler_params=pltpu.CompilerParams(vmem_limit_bytes=28 << 20),
         cost_estimate=pl.CostEstimate(flops=flops, bytes_accessed=touched, transcendentals=0),
@@ -597,7 +605,7 @@
         send_columns, "send_columns",
         [((NE_ROWS, wide), BF)] + [((COL_SENT, width), BF)] * 2,
         [VMEM] * 5 + [ANY],
-        [spread, rows_2, rows_1, OPEN_ROWS, PACK_COLS, g0], (), 10**7,
+        [spread, rows_1, rows_2, OPEN_ROWS, PACK_COLS, g0], (), 10**7,
     )
     cols_2 = lax.ppermute(cols_2, "lon", swaps(lon_size, 0))
     cols_1 = lax.ppermute(cols_1, "lon", swaps(lon_size, 1))
@@ -608,12 +616,18 @@
         [VMEM] * 6,
         [spread, edge, t_qkv, q, k, v], (), 2 * 10**9,
     )
-    args = [hidden, spread, edge, cols_2, cols_1, q, k, v, k_edge, v_edge, c_att, n_att, s_att]
+    args = [hidden, spread, edge, cols_1, cols_2, q, k, v, k_edge, v_edge, c_att, n_att, s_att]
     args += [OPEN_COLS, FROM_A, G_TO_A, t_qkv, t_out, s_proj, s_qkv, s_out, g0, save0, save1]
     out, grad = call(
         teacher_second, "teacher_second",
         [(teacher_in.shape, BF), (student_in.shape, F32)],
-        [VMEM] * len(args), args, (), 6 * 10**9,
+        [VMEM] * len(args), args,
+        [
+            pltpu.VMEM(teacher_in.shape, BF),
+            pltpu.VMEM(student_in.shape, F32),
+            pltpu.SemaphoreType.DMA((3,)),
+        ],
+        6 * 10**9, ANY,
     )
     return out.transpose(0, 2, 1, 3), grad.transpose(0, 2, 1, 3)
 

time: 39.4 us -> 38.4 us (0.975)
  the two profiles are of different devices: /device:TPU:128 before, /device:TPU:6 now
where the time goes in v7:
time: 38.4 us; the launch traced here: 38.1 us
  Pallas kernels  18.9 us (49%)
  starting transfers between devices  13.6 us (35%)
  waiting for transfers between devices  4.54 us (12%)
  between operations  1 us (3%)
    pallas_call x6, Pallas kernels, call(): pl.pallas_call(kernel, name=name, out_shape=shapes, in_specs=specs, out_s...  18.9 us
    ppermute x1, starting transfers between devices, shards(): rows_1 = lax.ppermute(rows_1, 'lat', swaps(lat_size, 1))  7.2 us
    ppermute x1, starting transfers between devices, shards(): cols_1 = lax.ppermute(cols_1, 'lon', swaps(lon_size, 1))  6.28 us
    ppermute x1, waiting for transfers between devices, shards(): cols_1 = lax.ppermute(cols_1, 'lon', swaps(lon_size, 1))  1.98 us
    ppermute x1, waiting for transfers between devices, shards(): cols_2 = lax.ppermute(cols_2, 'lon', swaps(lon_size, 0))  1.81 us
  transfers between devices with their start and end apart: 5, of which 3 were waited for; matrix products, arithmetic and copies ran while one was open for 0% of the time, Pallas kernels for 20%

profile of v7, /device:TPU:6, one launch (start us, length us, event | category | flops | bytes accessed | tf_op | source)
XLA Modules:
  0.0 38.1 jit_solution(13555736678937364052)
XLA Ops:
  0.6 0.1 collective-permute-start
  0.7 0.0 copy-start.1
  0.8 0.0 copy-start.10
  0.8 0.0 copy-start.13
  0.8 2.9 %teacher_own.1 = (bf16[320,512]{1,0:T(8,128)(2,1)S(1)}, bf16[320,128]{1,0:T(8,128)(2,1)S(1)}, bf16[320,128]{1,0:T(8,128)(2,1)S(1)}, bf16[320,512]{1,0:T(8,128)(2...) custom-call(bf16[1,12,24,512]{3,2,1,0:T(8,128)(2,1)} %bitcast.7, s32[12,2,24]{2,1,0:T(2,128)} %bitcast.8, ...), custom_call_target="tpu_custom_call" | custom-call | flops 1000000000 | bytes 3711744 | tf_op jit(solution)/shard_map/teacher_own/pallas_call | solution.py:538
  3.7 0.0 copy-start.5
  3.8 0.0 copy-start.6
  3.8 0.0 copy-start.7
  3.8 0.0 copy-start.8
  3.8 4.2 %teacher_first.1 = (bf16[320,512]{1,0:T(8,128)(2,1)S(1)}, bf16[400,640]{1,0:T(8,128)(2,1)S(1)}, bf16[80,512]{1,0:T(8,128)(2,1)S(1)}, bf16[80,512]{1,0:T(8,128)(2,1)S(1)}) custom-call(bf16[1,12,24,512]{3,2,1,0:T(8,128)(2,1)S(1)} %collective-permute-done.far_ref, bf16[320,512]{1,0:T(8,128)(2,1)S(1)} %get-tuple-element.28.x_ref, ...), custom_call_target="tpu_custom_call" | custom-call | flops 3000000000 | bytes 6494208 | tf_op jit(solution)/shard_map/teacher_first/pallas_call | solution.py:538
  8.0 7.2 %collective-permute-start.1 = (bf16[80,512]{1,0:T(8,128)(2,1)S(1)}, bf16[80,512]{1,0:T(8,128)(2,1)S(1)}, u32[]{:S(2)}, u32[]{:S(2)}) collective-permute-start(bf16[80,512]{1,0:T(8,128)(2,1)S(1)} %get-tuple-element.36), channel_id=1, source_target_pairs={{0,224},{32,64},{64,32},{96,128},{128,96},{160,192},{192,160},{224... | collective-permute-start | bytes 245768 | tf_op jit(solution)/shard_map/ppermute | solution.py:594
  15.2 0.0 copy-start.2
  15.2 0.0 copy-start.3
  15.3 3.7 %beside_rows.1 = (f32[320,256]{1,0:T(8,128)S(1)}, bf16[320,2816]{1,0:T(8,128)(2,1)S(1)}, bf16[320,2816]{1,0:T(8,128)(2,1)S(1)}, bf16[400,512]{1,0:T(8,128)(2,1)S...) custom-call(bf16[1,12,24,256]{3,2,1,0:T(8,128)(2,1)S(1)} %bitcast.5, ...), custom_call_target="tpu_custom_call" | custom-call | flops 5000000000 | bytes 5771264 | tf_op jit(solution)/shard_map/beside_rows/pallas_call | solution.py:538
  19.0 0.0 collective-permute-done.1.first_ref
  19.0 0.7 %collective-permute-done.2.second_ref = bf16[80,512]{1,0:T(8,128)(2,1)S(1)} collective-permute-done((bf16[80,512]{1,0:T(8,128)(2,1)S(1)}, bf16[80,512]{1,0:T(8,128)(2,1)S(1)}, u32[]{:S(2)}, u32[]{:S(2)}) %collective-permute-start.2) | collective-permute-done | bytes 81952 | tf_op jit(solution)/shard_map/ppermute | solution.py:593
  19.7 0.7 %send_columns.1 = (bf16[224,640]{1,0:T(8,128)(2,1)S(1)}, bf16[112,512]{1,0:T(8,128)(2,1)S(1)}, bf16[112,512]{1,0:T(8,128)(2,1)S(1)}) custom-call(bf16[400,640]{1,0:T(8,128)(2,1)S(1)} %get-tuple-element.35.g_ref, bf16[80,512]{1,0:T(8,128)(2,1)S(1)} %collective-permute-done.1.first_ref, bf16[80,512]{1,0:T(8,128)(2,1)S(1)} %collective-permute-done.2.second_ref, ...), custom_call_target="tpu_custom_call" | custom-call | flops 10000000 | bytes 1066496 | tf_op jit(solution)/shard_map/send_columns/pallas_call | solution.py:538
  20.4 6.3 %collective-permute-start.3 = (bf16[112,512]{1,0:T(8,128)(2,1)S(1)}, bf16[112,512]{1,0:T(8,128)(2,1)S(1)}, u32[]{:S(2)}, u32[]{:S(2)}) collective-permute-start(bf16[112,512]{1,0:T(8,128)(2,1)S(1)} %get-tuple-element.40), channel_id=1, source_target_pairs={{0,30},{2,4},{4,2},{6,8},{8,6},{10,12},{12,10},{14,16},{16,14},{18... | collective-permute-start | bytes 344072 | tf_op jit(solution)/shard_map/ppermute | solution.py:611
  26.7 0.0 collective-permute-start.4
  26.7 0.0 copy-start.12
  26.8 1.0 %beside_columns.1 = (bf16[224,512]{1,0:T(8,128)(2,1)S(1)}, bf16[224,512]{1,0:T(8,128)(2,1)S(1)}, bf16[48,512]{1,0:T(8,128)(2,1)S(1)}, bf16[48,512]{1,0:T(8,128)(2,1)S(1)}) custom-call(bf16[400,640]{1,0:T(8,128)(2,1)S(1)} %get-tuple-element.35.g_ref, bf16[224,640]{1,0:T(8,128)(2,1)S(1)} %get-tuple-element.39.edge_ref, bf16[2,512,1536]{2,1,0:T(8,128)(2,1)S(1)} %copy-done, ...), custom_call_target="tpu_custom_call" | custom-call | flops 2000000000 | bytes 5173248 | tf_op jit(solution)/shard_map/beside_columns/pallas_call | solution.py:538
  27.7 2.0 %collective-permute-done.3.first_ref = bf16[112,512]{1,0:T(8,128)(2,1)S(1)} collective-permute-done((bf16[112,512]{1,0:T(8,128)(2,1)S(1)}, bf16[112,512]{1,0:T(8,128)(2,1)S(1)}, u32[]{:S(2)}, u32[]{:S(2)}) %collective-permute-start.3) | collective-permute-done | bytes 114720 | tf_op jit(solution)/shard_map/ppermute | solution.py:611
  29.7 1.8 %collective-permute-done.4.second_ref = bf16[112,512]{1,0:T(8,128)(2,1)S(1)} collective-permute-done((bf16[112,512]{1,0:T(8,128)(2,1)S(1)}, bf16[112,512]{1,0:T(8,128)(2,1)S(1)}, u32[]{:S(2)}, u32[]{:S(2)}) %collective-permute-start.4) | collective-permute-done | bytes 114720 | tf_op jit(solution)/shard_map/ppermute | solution.py:610
  31.5 6.4 %teacher_second.1 = (bf16[1,12,24,512]{3,2,1,0:T(8,128)(2,1)}, f32[1,12,24,256]{3,2,1,0:T(8,128)}) custom-call(bf16[320,512]{1,0:T(8,128)(2,1)S(1)} %get-tuple-element.34.after_ref.h_ref, bf16[400,640]{1,0:T(8,128)(2,1)S(1)} %get-tuple-element.35.g_ref, bf16[224,640]{1,0:T(8,128)(2,1)S(1)} %get-tuple-element.39.edge_ref, ...), custom_call_target="tpu_custom_call" | custom-call | flops 6000000000 | bytes 13201920 | tf_op jit(solution)/shard_map/teacher_second/pallas_call | solution.py:538
  (20 shorter events, 0.0 us)
Async XLA Ops:
  0.6 3.1 %collective-permute-start = (bf16[1,12,24,512]{3,2,1,0:T(8,128)(2,1)}, bf16[1,12,24,512]{3,2,1,0:T(8,128)(2,1)S(1)}, u32[]{:S(2)}, u32[]{:S(2)}) collective-permute-start(bf16[1,12,24,512]{3,2,1,0:T(8,128)(2,1)} %bitcast.6), channel_id=1, source_target_pairs={{0,1},{1,0},{2,3},{3,2},{4,5},{5,4},{6,7},{7,6},{8,9},{9,8},{10,11... | collective-permute-start | bytes 884744 | tf_op jit(solution)/shard_map/ppermute | solution.py:571
  0.7 3.0 %copy-start = (bf16[2,512,1536]{2,1,0:T(8,128)(2,1)S(1)}, bf16[2,512,1536]{2,1,0:T(8,128)(2,1)}, u32[]{:S(2)}) copy-start(bf16[2,512,1536]{2,1,0:T(8,128)(2,1)} %t_qkv.9) | copy-start | bytes 9437188
  0.7 3.0 %copy-start.1 = (bf16[320,384]{1,0:T(8,128)(2,1)S(1)}, bf16[320,384]{1,0:T(8,128)(2,1)}, u32[]{:S(2)}) copy-start(bf16[320,384]{1,0:T(8,128)(2,1)} %constant.20.clone.to_a_hbm.to_a) | copy-start | bytes 737284
  0.8 3.0 %copy-start.10 = (bf16[400,320]{1,0:T(8,128)(2,1)S(1)}, bf16[400,320]{1,0:T(8,128)(2,1)}, u32[]{:S(2)}) copy-start(bf16[400,320]{1,0:T(8,128)(2,1)} %constant.23.clone.a_to_g) | copy-start | bytes 768004
  0.8 3.0 %copy-start.13 = (bf16[128,112]{1,0:T(8,128)(2,1)S(1)}, bf16[128,112]{1,0:T(8,128)(2,1)}, u32[]{:S(2)}) copy-start(bf16[128,112]{1,0:T(8,128)(2,1)} %constant.24.clone.pack) | copy-start | bytes 86020
  3.7 11.5 %copy-start.5 = (bf16[2,256,768]{2,1,0:T(8,128)(2,1)S(1)}, bf16[2,256,768]{2,1,0:T(8,128)(2,1)}, u32[]{:S(2)}) copy-start(bf16[2,256,768]{2,1,0:T(8,128)(2,1)} %s_qkv.3) | copy-start | bytes 2359300
  3.8 11.5 %copy-start.6 = (bf16[2,256,256]{2,1,0:T(8,128)(2,1)S(1)}, bf16[2,256,256]{2,1,0:T(8,128)(2,1)}, u32[]{:S(2)}) copy-start(bf16[2,256,256]{2,1,0:T(8,128)(2,1)} %s_out.3) | copy-start | bytes 786436
  3.8 11.4 %copy-start.7 = (bf16[256,512]{1,0:T(8,128)(2,1)S(1)}, bf16[256,512]{1,0:T(8,128)(2,1)}, u32[]{:S(2)}) copy-start(bf16[256,512]{1,0:T(8,128)(2,1)} %proj.3) | copy-start | bytes 786436
  3.8 11.4 %copy-start.8 = (bf16[1,24,12,256]{3,1,2,0:T(8,128)(2,1)S(1)}, bf16[1,24,12,256]{3,1,2,0:T(8,128)(2,1)}, u32[]{:S(2)}) copy-start(bf16[1,24,12,256]{3,1,2,0:T(8,128)(2,1)} %param.19) | copy-start | bytes 442372
  8.0 11.0 %collective-permute-start.1 = (bf16[80,512]{1,0:T(8,128)(2,1)S(1)}, bf16[80,512]{1,0:T(8,128)(2,1)S(1)}, u32[]{:S(2)}, u32[]{:S(2)}) collective-permute-start(bf16[80,512]{1,0:T(8,128)(2,1)S(1)} %get-tuple-element.36), channel_id=1, source_target_pairs={{0,224},{32,64},{64,32},{96,128},{128,96},{160,192},{192,160},{224... | collective-permute-start | bytes 245768 | tf_op jit(solution)/shard_map/ppermute | solution.py:594
  15.2 4.5 %collective-permute-start.2 = (bf16[80,512]{1,0:T(8,128)(2,1)S(1)}, bf16[80,512]{1,0:T(8,128)(2,1)S(1)}, u32[]{:S(2)}, u32[]{:S(2)}) collective-permute-start(bf16[80,512]{1,0:T(8,128)(2,1)S(1)} %get-tuple-element.37), channel_id=1, source_target_pairs={{0,32},{32,0},{64,96},{96,64},{128,160},{160,128},{192,224},{224,1... | collective-permute-start | bytes 245768 | tf_op jit(solution)/shard_map/ppermute | solution.py:593
  15.2 4.5 %copy-start.2 = (bf16[128,176]{1,0:T(8,128)(2,1)S(1)}, bf16[128,176]{1,0:T(8,128)(2,1)}, u32[]{:S(2)}) copy-start(bf16[128,176]{1,0:T(8,128)(2,1)} %constant.26.clone.pack) | copy-start | bytes 135172
  15.2 4.5 %copy-start.3 = (bf16[112,80]{1,0:T(8,128)(2,1)S(1)}, bf16[112,80]{1,0:T(8,128)(2,1)}, u32[]{:S(2)}) copy-start(bf16[112,80]{1,0:T(8,128)(2,1)} %constant.25.clone.open_rows) | copy-start | bytes 53764
  20.4 9.3 %collective-permute-start.3 = (bf16[112,512]{1,0:T(8,128)(2,1)S(1)}, bf16[112,512]{1,0:T(8,128)(2,1)S(1)}, u32[]{:S(2)}, u32[]{:S(2)}) collective-permute-start(bf16[112,512]{1,0:T(8,128)(2,1)S(1)} %get-tuple-element.40), channel_id=1, source_target_pairs={{0,30},{2,4},{4,2},{6,8},{8,6},{10,12},{12,10},{14,16},{16,14},{18... | collective-permute-start | bytes 344072 | tf_op jit(solution)/shard_map/ppermute | solution.py:611
  26.7 4.8 %collective-permute-start.4 = (bf16[112,512]{1,0:T(8,128)(2,1)S(1)}, bf16[112,512]{1,0:T(8,128)(2,1)S(1)}, u32[]{:S(2)}, u32[]{:S(2)}) collective-permute-start(bf16[112,512]{1,0:T(8,128)(2,1)S(1)} %get-tuple-element.41), channel_id=1, source_target_pairs={{0,2},{2,0},{4,6},{6,4},{8,10},{10,8},{12,14},{14,12},{16,18},{18,... | collective-permute-start | bytes 344072 | tf_op jit(solution)/shard_map/ppermute | solution.py:610
  26.7 4.8 %copy-start.4 = (bf16[2,512,512]{2,1,0:T(8,128)(2,1)S(1)}, bf16[2,512,512]{2,1,0:T(8,128)(2,1)}, u32[]{:S(2)}) copy-start(bf16[2,512,512]{2,1,0:T(8,128)(2,1)} %t_out.3) | copy-start | bytes 3145732
  26.7 4.8 %copy-start.9 = (bf16[320,400]{1,0:T(8,128)(2,1)S(1)}, bf16[320,400]{1,0:T(8,128)(2,1)}, u32[]{:S(2)}) copy-start(bf16[320,400]{1,0:T(8,128)(2,1)} %constant.29.clone.g_to_a) | copy-start | bytes 768004
  26.7 4.8 %copy-start.11 = (bf16[384,320]{1,0:T(8,128)(2,1)S(1)}, bf16[384,320]{1,0:T(8,128)(2,1)}, u32[]{:S(2)}) copy-start(bf16[384,320]{1,0:T(8,128)(2,1)} %constant.28.clone.from_a) | copy-start | bytes 737284
  26.7 4.8 %copy-start.12 = (bf16[176,112]{1,0:T(8,128)(2,1)S(1)}, bf16[176,112]{1,0:T(8,128)(2,1)}, u32[]{:S(2)}) copy-start(bf16[176,112]{1,0:T(8,128)(2,1)} %constant.27.clone.open_cols) | copy-start | bytes 118276

commit v8 on v7

--- a/solution.py
+++ b/solution.py
@@ -82,10 +82,21 @@
     return table
 
 
+def _corners(start, west, east):
+    table = np.zeros((256, ROW_SENT), ml_dtypes.bfloat16)
+    for i in range(18):
+        table[start + i, west + i] = 1
+        table[128 + start + i, east + i] = 1
+    return table
+
+
 PACK_ROWS = _packing((32, 48, 32))
+PACK_OWN = np.roll(PACK_ROWS, 18, axis=0)
 PACK_COLS = _packing((32, 32, 48, 32, 32))
 ROW_TOKENS, ROW_SENT = 72, 80
 COL_TOKENS, COL_SENT = 108, 112
+FROM_NORTH = _corners(0, 0, 54)
+FROM_SOUTH = _corners(90, 0, 54)
 OPEN_ROWS = np.ascontiguousarray(PACK_ROWS.T[:, :ROW_SENT])
 OPEN_COLS = np.ascontiguousarray(PACK_COLS.T[:, :COL_SENT])
 
@@ -414,8 +425,8 @@
 
 
 def beside_rows(
-    x_ref, id_ref, to_a, s_qkv, s_out, proj, g_ref, t_qkv, after_ref,
-    g0_ref, save0, save1, q_ref, k_ref, v_ref, att_ref, pad_ref,
+    x_ref, id_ref, to_a, s_qkv, s_out, proj, g_ref, t_qkv, pack, after_ref,
+    g0_ref, save0, save1, q_ref, k_ref, v_ref, att_ref, west_ref, east_ref, pad_ref,
 ):
     width = g_ref.shape[1] - 128
     blocks = head_blocks()
@@ -424,6 +435,10 @@
     h = student_layer(h, s_qkv[1], s_out[1], id_ref[...], save1)
     predicted = dot(h, proj[...])
     g0_ref[...] = dot_nt(predicted.astype(BF), proj[...])
+
+    for ref, items in ((west_ref, TO_WEST), (east_ref, TO_EAST)):
+        rows = gather([(g_ref, OWN)], items[1:4])
+        ref[...] = packed(rows, pack[...], COL_TOKENS, COL_SENT)
 
     rows = g_ref[:, :width]
     q = (unit(dot(rows, t_qkv[1, :, :width]), blocks)[0] * SCALE).astype(BF)
@@ -436,33 +451,44 @@
     [att_ref[...]] = window_attention([(part(q, "c"), [part(k, "c"), part(v, "c")], (ids, ids))])
 
 
+def on_map():
+    lat = lax.axis_index("lat")
+    inside = (lat > 0, lat < lax.axis_size("lat") - 1)
+    return [jnp.where(x, 1.0, 0.0) for x in inside]
+
+
 def send_columns(
-    g_ref, first_ref, second_ref, open_rows, pack, after_ref, edge_ref, out_first, out_second
+    first_ref, second_ref, from_north, from_south, west_ref, east_ref, after_ref,
+    out_first, out_second,
 ):
-    width = first_ref.shape[1]
-    lat = lax.axis_index("lat")
-    blocks = []
-    inside = (lat > 0, lat < lax.axis_size("lat") - 1)
-    for sent, there in zip(swapped("lat", first_ref[...], second_ref[...]), inside):
-        rows = opened(sent, open_rows[...], ROW_TOKENS)
-        ids = rows[:, width:] * jnp.where(there, 1.0, 0.0).astype(BF)
-        blocks.append(jnp.concatenate([rows[:, :width], ids], axis=1))
-    edge = jnp.concatenate(blocks, axis=0)
-    edge_ref[...] = edge
-    west, east = [
-        packed(
-            gather([(g_ref, OWN), (edge, EDGE)], items), pack[...], COL_TOKENS, COL_SENT
-        )
-        for items in (TO_WEST, TO_EAST)
-    ]
-    out_first[...], out_second[...] = swapped("lon", west, east)
+    rows = swapped("lat", first_ref[...], second_ref[...])
+    tables = (from_north[...], from_south[...])
+    values = sum(dot(table, sent) for table, sent in zip(tables, rows))
+    ids = 0.0
+    for table, sent, there in zip(tables, rows, on_map()):
+        row = sent.astype(F32)[ROW_TOKENS : ROW_TOKENS + 1, :ROW_SENT] * there
+        ids += dot_nt(jnp.broadcast_to(row, (8, ROW_SENT)).astype(BF), table)
+    at = lax.broadcasted_iota(jnp.int32, (COL_SENT, 1), 0)
+    empty = jnp.zeros((1, first_ref.shape[1] - 128), F32)
+    payloads = []
+    for i, ref in ((0, west_ref), (128, east_ref)):
+        row = jnp.concatenate([ids[0:1, i : i + 128], empty], axis=1)
+        corners = jnp.where(at == COL_TOKENS, row, values[i : i + COL_SENT])
+        payloads.append((ref[...].astype(F32) + corners).astype(BF))
+    out_first[...], out_second[...] = swapped("lon", *payloads)
 
 
 def beside_columns(
-    g_ref, edge_ref, t_qkv, q_ref, k_ref, v_ref, k_out, v_out, n_ref, s_ref
+    g_ref, first_ref, second_ref, open_rows, t_qkv, q_ref, k_ref, v_ref, after_ref,
+    edge_ref, k_out, v_out, n_ref, s_ref,
 ):
     width = g_ref.shape[1] - 128
     blocks = head_blocks()
+    edge = []
+    for sent, there in zip(swapped("lat", first_ref[...], second_ref[...]), on_map()):
+        rows = opened(sent, open_rows[...], ROW_TOKENS)
+        edge.append(jnp.concatenate([rows[:, :width], rows[:, width:] * there.astype(BF)], axis=1))
+    edge_ref[...] = jnp.concatenate(edge, axis=0)
     rows = edge_ref[:, :width]
     k = unit(dot(rows, t_qkv[1, :, width : 2 * width]), blocks)[0].astype(BF)
     v = dot(rows, t_qkv[1, :, 2 * width :]).astype(BF)
@@ -561,6 +587,18 @@
     return sorted(route.items())
 
 
+def inner_swaps(lat_size, lon_size):
+    route = []
+    for i in range(lat_size):
+        for j in range(lon_size):
+            if 0 < i < lat_size - 1:
+                to = (i - 1 + 2 * (i % 2)) * lon_size + j
+            else:
+                to = i * lon_size + (j ^ 1)
+            route.append((i * lon_size + j, to))
+    return route
+
+
 def shards(teacher_in, student_in, regions, t_qkv, t_out, s_qkv, s_out, s_proj):
     width, narrow = teacher_in.shape[3], student_in.shape[3]
     lat_size, lon_size = lax.axis_size("lat"), lax.axis_size("lon")
@@ -591,30 +629,31 @@
         [pltpu.VMEM((COLS, TALL, width), BF)] + buffers(t_out[0]), 3 * 10**9,
     )
     rows_2 = lax.ppermute(rows_2, "lat", swaps(lat_size, 0))
-    rows_1 = lax.ppermute(rows_1, "lat", swaps(lat_size, 1))
-
-    g0, save0, save1, q, k, v, c_att = call(
+    rows_1 = lax.ppermute(rows_1, ("lat", "lon"), inner_swaps(lat_size, lon_size))
+
+    g0, save0, save1, q, k, v, c_att, west, east = call(
         beside_rows, "beside_rows",
         [((NA, narrow), F32), ((NA, SAVE), BF), ((NA, SAVE), BF)]
-        + [((NG, width), BF)] * 3 + [((AT["c"][1], width), BF)],
-        [VMEM] * 8 + [ANY],
-        [student_in, ids, TO_A, s_qkv, s_out, s_proj, spread, t_qkv, hidden],
+        + [((NG, width), BF)] * 3 + [((AT["c"][1], width), BF)] + [((COL_SENT, width), BF)] * 2,
+        [VMEM] * 9 + [ANY],
+        [student_in, ids, TO_A, s_qkv, s_out, s_proj, spread, t_qkv, PACK_OWN, hidden],
         [pltpu.VMEM((COLS, TALL, narrow), BF)], 5 * 10**9,
     )
-    edge, cols_1, cols_2 = call(
+    cols_1, cols_2 = call(
         send_columns, "send_columns",
-        [((NE_ROWS, wide), BF)] + [((COL_SENT, width), BF)] * 2,
-        [VMEM] * 5 + [ANY],
-        [spread, rows_1, rows_2, OPEN_ROWS, PACK_COLS, g0], (), 10**7,
-    )
+        [((COL_SENT, width), BF)] * 2,
+        [VMEM] * 6 + [ANY],
+        [rows_1, rows_2, FROM_NORTH, FROM_SOUTH, west, east, g0], (), 10**7,
+    )
+    sent = cols_2
     cols_2 = lax.ppermute(cols_2, "lon", swaps(lon_size, 0))
     cols_1 = lax.ppermute(cols_1, "lon", swaps(lon_size, 1))
 
-    k_edge, v_edge, n_att, s_att = call(
+    edge, k_edge, v_edge, n_att, s_att = call(
         beside_columns, "beside_columns",
-        [((NE_ROWS, width), BF)] * 2 + [((AT["n"][1], width), BF)] * 2,
-        [VMEM] * 6,
-        [spread, edge, t_qkv, q, k, v], (), 2 * 10**9,
+        [((NE_ROWS, wide), BF)] + [((NE_ROWS, width), BF)] * 2 + [((AT["n"][1], width), BF)] * 2,
+        [VMEM] * 8 + [ANY],
+        [spread, rows_1, rows_2, OPEN_ROWS, t_qkv, q, k, v, sent], (), 2 * 10**9,
     )
     args = [hidden, spread, edge, cols_1, cols_2, q, k, v, k_edge, v_edge, c_att, n_att, s_att]
     args += [OPEN_COLS, FROM_A, G_TO_A, t_qkv, t_out, s_proj, s_qkv, s_out, g0, save0, save1]

time: 38.4 us -> 37.9 us (0.987)
  transfers between devices with their start and end apart: 5 -> 5, of which waited for: 3 -> 3; matrix products, arithmetic and copies ran while one was open for 0% -> 0% of each run, Pallas kernels for 20% -> 21%
where the time goes in v8:
time: 37.9 us; the launch traced here: 37.8 us
  Pallas kernels  18.8 us (50%)
  starting transfers between devices  13.7 us (36%)
  waiting for transfers between devices  4.23 us (11%)
  between operations  1.05 us (3%)
    pallas_call x6, Pallas kernels, call(): pl.pallas_call(kernel, name=name, out_shape=shapes, in_specs=specs, out_s...  18.8 us
    ppermute x1, starting transfers between devices, shards(): lax.ppermute(rows_1, ('lat', 'lon'), inner_swaps(lat_size, lon_size))  7.2 us
    ppermute x1, starting transfers between devices, shards(): cols_1 = lax.ppermute(cols_1, 'lon', swaps(lon_size, 1))  6.37 us
    ppermute x1, waiting for transfers between devices, shards(): cols_1 = lax.ppermute(cols_1, 'lon', swaps(lon_size, 1))  1.82 us
    ppermute x1, waiting for transfers between devices, shards(): cols_2 = lax.ppermute(cols_2, 'lon', swaps(lon_size, 0))  1.82 us
  transfers between devices with their start and end apart: 5, of which 3 were waited for; matrix products, arithmetic and copies ran while one was open for 0% of the time, Pallas kernels for 21%

profile of v8, /device:TPU:6, one launch (start us, length us, event | category | flops | bytes accessed | tf_op | source)
XLA Modules:
  0.0 37.8 jit_solution(334154079972089562)
XLA Ops:
  0.6 0.1 collective-permute-start
  0.7 0.0 copy-start.1
  0.8 0.0 copy-start.10
  0.8 0.0 copy-start.14
  0.8 2.9 %teacher_own.1 = (bf16[320,512]{1,0:T(8,128)(2,1)S(1)}, bf16[320,128]{1,0:T(8,128)(2,1)S(1)}, bf16[320,128]{1,0:T(8,128)(2,1)S(1)}, bf16[320,512]{1,0:T(8,128)(2...) custom-call(bf16[1,12,24,512]{3,2,1,0:T(8,128)(2,1)} %bitcast.7, s32[12,2,24]{2,1,0:T(2,128)} %bitcast.8, ...), custom_call_target="tpu_custom_call" | custom-call | flops 1000000000 | bytes 3711744 | tf_op jit(solution)/shard_map/teacher_own/pallas_call | solution.py:564
  3.7 0.0 copy-start.5
  3.8 0.0 copy-start.6
  3.8 0.0 copy-start.13
  3.8 4.2 %teacher_first.1 = (bf16[320,512]{1,0:T(8,128)(2,1)S(1)}, bf16[400,640]{1,0:T(8,128)(2,1)S(1)}, bf16[80,512]{1,0:T(8,128)(2,1)S(1)}, bf16[80,512]{1,0:T(8,128)(2,1)S(1)}) custom-call(bf16[1,12,24,512]{3,2,1,0:T(8,128)(2,1)S(1)} %collective-permute-done.far_ref, bf16[320,512]{1,0:T(8,128)(2,1)S(1)} %get-tuple-element.30.x_ref, ...), custom_call_target="tpu_custom_call" | custom-call | flops 3000000000 | bytes 6494208 | tf_op jit(solution)/shard_map/teacher_first/pallas_call | solution.py:564
  8.0 7.2 %collective-permute-start.1 = (bf16[80,512]{1,0:T(8,128)(2,1)S(1)}, bf16[80,512]{1,0:T(8,128)(2,1)S(1)}, u32[]{:S(2)}, u32[]{:S(2)}) collective-permute-start(bf16[80,512]{1,0:T(8,128)(2,1)S(1)} %get-tuple-element.38), channel_id=1, source_target_pairs={{0,2},{2,0},{4,6},{6,4},{8,10},{10,8},{12,14},{14,12},{16,18},{18,... | collective-permute-start | bytes 245768 | tf_op jit(solution)/shard_map/ppermute | solution.py:632
  15.3 0.0 copy-start.2
  15.3 0.0 copy-start.3
  15.3 0.0 copy-start.15
  15.3 3.8 %beside_rows.1 = (f32[320,256]{1,0:T(8,128)S(1)}, bf16[320,2816]{1,0:T(8,128)(2,1)S(1)}, bf16[320,2816]{1,0:T(8,128)(2,1)S(1)}, bf16[400,512]{1,0:T(8,128)(2,1)S...) custom-call(bf16[1,12,24,256]{3,2,1,0:T(8,128)(2,1)S(1)} %bitcast.5,, ...), custom_call_target="tpu_custom_call" | custom-call | flops 5000000000 | bytes 5799936 | tf_op jit(solution)/shard_map/beside_rows/pallas_call | solution.py:564
  19.1 0.6 %collective-permute-done.2.second_ref = bf16[80,512]{1,0:T(8,128)(2,1)S(1)} collective-permute-done((bf16[80,512]{1,0:T(8,128)(2,1)S(1)}, bf16[80,512]{1,0:T(8,128)(2,1)S(1)}, u32[]{:S(2)}, u32[]{:S(2)}) %collective-permute-start.2) | collective-permute-done | bytes 81952 | tf_op jit(solution)/shard_map/ppermute | solution.py:631
  19.7 0.3 send_columns.1
  20.1 6.4 %collective-permute-start.3 = (bf16[112,512]{1,0:T(8,128)(2,1)S(1)}, bf16[112,512]{1,0:T(8,128)(2,1)S(1)}, u32[]{:S(2)}, u32[]{:S(2)}) collective-permute-start(bf16[112,512]{1,0:T(8,128)(2,1)S(1)} %get-tuple-element.48), channel_id=1, source_target_pairs={{0,30},{2,4},{4,2},{6,8},{8,6},{10,12},{12,10},{14,16},{16,14},{18... | collective-permute-start | bytes 344072 | tf_op jit(solution)/shard_map/ppermute | solution.py:650
  26.4 0.0 copy-start.9
  26.4 0.0 copy-start.11
  26.5 0.0 copy-start.12
  26.5 1.1 %beside_columns.1 = (bf16[224,640]{1,0:T(8,128)(2,1)S(1)}, bf16[224,512]{1,0:T(8,128)(2,1)S(1)}, bf16[224,512]{1,0:T(8,128)(2,1)S(1)}, bf16[48,512]{1,0:T(8,128)(2,1)S(1)}, bf16[48,512]{1,0:T(8,128)(2,1)S(1)}) custom-call(bf16[400,640]{1,0:T(8,128)(2,1)S(1)} %get-tuple-element.37.g_ref, bf16[80,512]{1,0:T(8,128)(2,1)S(1)} %collective-permute-done.1.first_ref, ...), custom_call_target="tpu_custom_call" | custom-call | flops 2000000000 | bytes 5182976 | tf_op jit(solution)/shard_map/beside_columns/pallas_call | solution.py:564
  27.6 1.8 %collective-permute-done.3.first_ref = bf16[112,512]{1,0:T(8,128)(2,1)S(1)} collective-permute-done((bf16[112,512]{1,0:T(8,128)(2,1)S(1)}, bf16[112,512]{1,0:T(8,128)(2,1)S(1)}, u32[]{:S(2)}, u32[]{:S(2)}) %collective-permute-start.3) | collective-permute-done | bytes 114720 | tf_op jit(solution)/shard_map/ppermute | solution.py:650
  29.4 1.8 %collective-permute-done.4.second_ref = bf16[112,512]{1,0:T(8,128)(2,1)S(1)} collective-permute-done((bf16[112,512]{1,0:T(8,128)(2,1)S(1)}, bf16[112,512]{1,0:T(8,128)(2,1)S(1)}, u32[]{:S(2)}, u32[]{:S(2)}) %collective-permute-start.4) | collective-permute-done | bytes 114720 | tf_op jit(solution)/shard_map/ppermute | solution.py:649
  31.2 6.4 %teacher_second.1 = (bf16[1,12,24,512]{3,2,1,0:T(8,128)(2,1)}, f32[1,12,24,256]{3,2,1,0:T(8,128)}) custom-call(bf16[320,512]{1,0:T(8,128)(2,1)S(1)} %get-tuple-element.36.after_ref.h_ref, bf16[400,640]{1,0:T(8,128)(2,1)S(1)} %get-tuple-element.37.g_ref, bf16[224,640]{1,0:T(8,128)(2,1)S(1)} %get-tuple-element.47.edge_ref, ...), custom_call_target="tpu_custom_call" | custom-call | flops 6000000000 | bytes 13201920 | tf_op jit(solution)/shard_map/teacher_second/pallas_call | solution.py:564
  (24 shorter events, 0.1 us)
Async XLA Ops:
  0.6 3.1 %collective-permute-start = (bf16[1,12,24,512]{3,2,1,0:T(8,128)(2,1)}, bf16[1,12,24,512]{3,2,1,0:T(8,128)(2,1)S(1)}, u32[]{:S(2)}, u32[]{:S(2)}) collective-permute-start(bf16[1,12,24,512]{3,2,1,0:T(8,128)(2,1)} %bitcast.6), channel_id=1, source_target_pairs={{0,1},{1,0},{2,3},{3,2},{4,5},{5,4},{6,7},{7,6},{8,9},{9,8},{10,11... | collective-permute-start | bytes 884744 | tf_op jit(solution)/shard_map/ppermute | solution.py:609
  0.7 3.0 %copy-start = (bf16[2,512,1536]{2,1,0:T(8,128)(2,1)S(1)}, bf16[2,512,1536]{2,1,0:T(8,128)(2,1)}, u32[]{:S(2)}) copy-start(bf16[2,512,1536]{2,1,0:T(8,128)(2,1)} %t_qkv.9) | copy-start | bytes 9437188
  0.7 3.0 %copy-start.1 = (bf16[320,384]{1,0:T(8,128)(2,1)S(1)}, bf16[320,384]{1,0:T(8,128)(2,1)}, u32[]{:S(2)}) copy-start(bf16[320,384]{1,0:T(8,128)(2,1)} %constant.24.clone.to_a_hbm.to_a) | copy-start | bytes 737284
  0.8 3.0 %copy-start.10 = (bf16[400,320]{1,0:T(8,128)(2,1)S(1)}, bf16[400,320]{1,0:T(8,128)(2,1)}, u32[]{:S(2)}) copy-start(bf16[400,320]{1,0:T(8,128)(2,1)} %constant.27.clone.a_to_g) | copy-start | bytes 768004
  0.8 3.0 %copy-start.14 = (bf16[128,112]{1,0:T(8,128)(2,1)S(1)}, bf16[128,112]{1,0:T(8,128)(2,1)}, u32[]{:S(2)}) copy-start(bf16[128,112]{1,0:T(8,128)(2,1)} %constant.28.clone.pack) | copy-start | bytes 86020
  3.7 11.5 %copy-start.5 = (bf16[2,256,768]{2,1,0:T(8,128)(2,1)S(1)}, bf16[2,256,768]{2,1,0:T(8,128)(2,1)}, u32[]{:S(2)}) copy-start(bf16[2,256,768]{2,1,0:T(8,128)(2,1)} %s_qkv.3) | copy-start | bytes 2359300
  3.8 11.5 %copy-start.6 = (bf16[2,256,256]{2,1,0:T(8,128)(2,1)S(1)}, bf16[2,256,256]{2,1,0:T(8,128)(2,1)}, u32[]{:S(2)}) copy-start(bf16[2,256,256]{2,1,0:T(8,128)(2,1)} %s_out.3) | copy-start | bytes 786436
  3.8 11.5 %copy-start.7 = (bf16[256,512]{1,0:T(8,128)(2,1)S(1)}, bf16[256,512]{1,0:T(8,128)(2,1)}, u32[]{:S(2)}) copy-start(bf16[256,512]{1,0:T(8,128)(2,1)} %proj.3) | copy-start | bytes 786436
  3.8 11.5 %copy-start.8 = (bf16[1,24,12,256]{3,1,2,0:T(8,128)(2,1)S(1)}, bf16[1,24,12,256]{3,1,2,0:T(8,128)(2,1)}, u32[]{:S(2)}) copy-start(bf16[1,24,12,256]{3,1,2,0:T(8,128)(2,1)} %param.21) | copy-start | bytes 442372
  3.8 11.5 %copy-start.13 = (bf16[128,112]{1,0:T(8,128)(2,1)S(1)}, bf16[128,112]{1,0:T(8,128)(2,1)}, u32[]{:S(2)}) copy-start(bf16[128,112]{1,0:T(8,128)(2,1)} %constant.29.clone.pack) | copy-start | bytes 86020
  8.0 11.1 %collective-permute-start.1 = (bf16[80,512]{1,0:T(8,128)(2,1)S(1)}, bf16[80,512]{1,0:T(8,128)(2,1)S(1)}, u32[]{:S(2)}, u32[]{:S(2)}) collective-permute-start(bf16[80,512]{1,0:T(8,128)(2,1)S(1)} %get-tuple-element.38), channel_id=1, source_target_pairs={{0,2},{2,0},{4,6},{6,4},{8,10},{10,8},{12,14},{14,12},{16,18},{18,... | collective-permute-start | bytes 245768 | tf_op jit(solution)/shard_map/ppermute | solution.py:632
  15.2 4.5 %collective-permute-start.2 = (bf16[80,512]{1,0:T(8,128)(2,1)S(1)}, bf16[80,512]{1,0:T(8,128)(2,1)S(1)}, u32[]{:S(2)}, u32[]{:S(2)}) collective-permute-start(bf16[80,512]{1,0:T(8,128)(2,1)S(1)} %get-tuple-element.39), channel_id=1, source_target_pairs={{0,32},{32,0},{64,96},{96,64},{128,160},{160,128},{192,224},{224,1... | collective-permute-start | bytes 245768 | tf_op jit(solution)/shard_map/ppermute | solution.py:631
  15.3 4.5 %copy-start.2 = (bf16[256,80]{1,0:T(8,128)(2,1)S(1)}, bf16[256,80]{1,0:T(8,128)(2,1)}, u32[]{:S(2)}) copy-start(bf16[256,80]{1,0:T(8,128)(2,1)} %constant.31.clone.from_south) | copy-start | bytes 122884
  15.3 4.5 %copy-start.3 = (bf16[256,80]{1,0:T(8,128)(2,1)S(1)}, bf16[256,80]{1,0:T(8,128)(2,1)}, u32[]{:S(2)}) copy-start(bf16[256,80]{1,0:T(8,128)(2,1)} %constant.30.clone.from_north) | copy-start | bytes 122884
  15.3 11.2 %copy-start.15 = (bf16[112,80]{1,0:T(8,128)(2,1)S(1)}, bf16[112,80]{1,0:T(8,128)(2,1)}, u32[]{:S(2)}) copy-start(bf16[112,80]{1,0:T(8,128)(2,1)} %constant.32.clone.open_rows) | copy-start | bytes 53764
  20.1 9.3 %collective-permute-start.3 = (bf16[112,512]{1,0:T(8,128)(2,1)S(1)}, bf16[112,512]{1,0:T(8,128)(2,1)S(1)}, u32[]{:S(2)}, u32[]{:S(2)}) collective-permute-start(bf16[112,512]{1,0:T(8,128)(2,1)S(1)} %get-tuple-element.48), channel_id=1, source_target_pairs={{0,30},{2,4},{4,2},{6,8},{8,6},{10,12},{12,10},{14,16},{16,14},{18... | collective-permute-start | bytes 344072 | tf_op jit(solution)/shard_map/ppermute | solution.py:650
  26.4 4.8 %collective-permute-start.4 = (bf16[112,512]{1,0:T(8,128)(2,1)S(1)}, bf16[112,512]{1,0:T(8,128)(2,1)S(1)}, u32[]{:S(2)}, u32[]{:S(2)}) collective-permute-start(bf16[112,512]{1,0:T(8,128)(2,1)S(1)} %get-tuple-element.46.after_ref), channel_id=1, source_target_pairs={{0,2},{2,0},{4,6},{6,4},{8,10},{10,8},{12,14},{14,12},{16,18},{18,... | collective-permute-start | bytes 344072 | tf_op jit(solution)/shard_map/ppermute | solution.py:649
  26.4 4.8 %copy-start.4 = (bf16[2,512,512]{2,1,0:T(8,128)(2,1)S(1)}, bf16[2,512,512]{2,1,0:T(8,128)(2,1)}, u32[]{:S(2)}) copy-start(bf16[2,512,512]{2,1,0:T(8,128)(2,1)} %t_out.3) | copy-start | bytes 3145732
  26.4 4.8 %copy-start.9 = (bf16[320,400]{1,0:T(8,128)(2,1)S(1)}, bf16[320,400]{1,0:T(8,128)(2,1)}, u32[]{:S(2)}) copy-start(bf16[320,400]{1,0:T(8,128)(2,1)} %constant.35.clone.g_to_a) | copy-start | bytes 768004
  26.4 4.8 %copy-start.11 = (bf16[384,320]{1,0:T(8,128)(2,1)S(1)}, bf16[384,320]{1,0:T(8,128)(2,1)}, u32[]{:S(2)}) copy-start(bf16[384,320]{1,0:T(8,128)(2,1)} %constant.34.clone.from_a) | copy-start | bytes 737284
  26.5 4.8 %copy-start.12 = (bf16[176,112]{1,0:T(8,128)(2,1)S(1)}, bf16[176,112]{1,0:T(8,128)(2,1)}, u32[]{:S(2)}) copy-start(bf16[176,112]{1,0:T(8,128)(2,1)} %constant.33.clone.open_cols) | copy-start | bytes 118276

commit v9 on v8

--- a/solution.py
+++ b/solution.py
@@ -281,44 +281,49 @@
 
 def teacher_own(
     x_hbm, reg_hbm, to_a_hbm, a_row_hbm, a_col_hbm, t_qkv,
-    x_out, id_ref, far_id_ref, q_ref, k_ref, v_ref,
-    pad_ref, x_ref, reg_ref, to_a, a_row, a_col, wqkv, sems,
+    x_out, id_ref, far_id_ref, q_ref, k_ref, v_ref, to_a, wqkv,
+    pad_ref, x_ref, reg_ref, a_row, a_col, sems,
 ):
+    width = x_ref.shape[3]
+    thirds = [pl.ds(i * width, width) for i in range(3)]
     copies = fetch(
         (x_hbm, x_ref, sems.at[0]),
-        (to_a_hbm, to_a, sems.at[2]),
-        (reg_hbm, reg_ref, sems.at[1]),
-        (a_row_hbm, a_row, sems.at[3]),
-        (a_col_hbm, a_col, sems.at[4]),
-        (t_qkv.at[0], wqkv, sems.at[5]),
-    )
-    width = x_ref.shape[3]
+        (to_a_hbm, to_a, sems.at[1]),
+        (t_qkv.at[0, :, thirds[0]], wqkv.at[:, thirds[0]], sems.at[2]),
+        (t_qkv.at[0, :, thirds[1]], wqkv.at[:, thirds[1]], sems.at[3]),
+        (t_qkv.at[0, :, thirds[2]], wqkv.at[:, thirds[2]], sems.at[4]),
+        (reg_hbm, reg_ref, sems.at[5]),
+        (a_row_hbm, a_row, sems.at[6]),
+        (a_col_hbm, a_col, sems.at[7]),
+    )
     blocks = head_blocks()
     copies[0].wait()
     copies[1].wait()
     x = to_window_order(x_ref, pad_ref, to_a[...])
     x_out[...] = x
-    for copy in copies[2:5]:
+    copies[2].wait()
+    q_ref[...] = (unit(dot(x, wqkv[:, :width]), blocks)[0] * SCALE).astype(BF)
+    copies[3].wait()
+    k_ref[...] = unit(dot(x, wqkv[:, width : 2 * width]), blocks)[0].astype(BF)
+    copies[4].wait()
+    v_ref[...] = dot(x, wqkv[:, 2 * width :]).astype(BF)
+    for copy in copies[5:]:
         copy.wait()
     reg, reg_far = by_level(reg_ref)
     id_ref[...] = window_ids(reg, a_row[...], a_col[...])
     far_id_ref[...] = window_ids(reg_far, a_row[...], a_col[...])
-    copies[5].wait()
-    q_ref[...] = (unit(dot(x, wqkv[:, :width]), blocks)[0] * SCALE).astype(BF)
-    k_ref[...] = unit(dot(x, wqkv[:, width : 2 * width]), blocks)[0].astype(BF)
-    v_ref[...] = dot(x, wqkv[:, 2 * width :]).astype(BF)
 
 
 def teacher_first(
-    far_ref, x_ref, id_ref, far_id_ref, q_ref, k_ref, v_ref, to_a, a_to_g, pack, t_qkv, t_out,
+    far_ref, x_ref, id_ref, far_id_ref, q_ref, k_ref, v_ref, to_a, a_to_g, pack, wqkv, t_out,
     h_ref, g_ref, first_ref, second_ref, pad_ref, wout, sems,
 ):
     copies = fetch((t_out.at[0], wout, sems.at[0]))
     width = x_ref.shape[1]
     blocks = head_blocks()
     far = to_window_order(far_ref, pad_ref, to_a[...])
-    k_far = unit(dot(far, t_qkv[0, :, width : 2 * width]), blocks)[0].astype(BF)
-    v_far = dot(far, t_qkv[0, :, 2 * width :]).astype(BF)
+    k_far = unit(dot(far, wqkv[:, width : 2 * width]), blocks)[0].astype(BF)
+    v_far = dot(far, wqkv[:, 2 * width :]).astype(BF)
     windows = []
     for w in range(4):
         rows = slice(w * WIN, (w + 1) * WIN)
@@ -612,19 +617,21 @@
         pltpu.with_memory_space_constraint(jnp.asarray(a), pltpu.HBM)
         for a in (teacher_in, regions, TO_A, A_ROW, A_COL, t_qkv)
     ]
-    x, ids, far_ids, q, k, v = call(
+    x, ids, far_ids, q, k, v, to_a, wqkv = call(
         teacher_own, "teacher_own",
-        [((NA, width), BF), ((NA, 128), BF), ((NA, 128), BF)] + [((NA, width), BF)] * 3,
+        [((NA, width), BF), ((NA, 128), BF), ((NA, 128), BF)] + [((NA, width), BF)] * 3
+        + [((NA, NAT), BF), (t_qkv.shape[1:], BF)],
         [HBM] * 6, pinned,
         [pltpu.VMEM((COLS, TALL, width), BF)]
-        + buffers(teacher_in, regions, TO_A, A_ROW, A_COL, t_qkv[0]),
+        + buffers(teacher_in, regions, A_ROW, A_COL)[:-1]
+        + [pltpu.SemaphoreType.DMA((8,))],
         10**9,
     )
     hidden, spread, rows_1, rows_2 = call(
         teacher_first, "teacher_first",
         [((NA, width), BF), ((NG, wide), BF)] + [((ROW_SENT, width), BF)] * 2,
         [VMEM] * 11 + [HBM],
-        [far, x, ids, far_ids, q, k, v, TO_A, A_TO_G, PACK_ROWS, t_qkv]
+        [far, x, ids, far_ids, q, k, v, to_a, A_TO_G, PACK_ROWS, wqkv]
         + [pltpu.with_memory_space_constraint(t_out, pltpu.HBM)],
         [pltpu.VMEM((COLS, TALL, width), BF)] + buffers(t_out[0]), 3 * 10**9,
     )
@@ -636,7 +643,7 @@
         [((NA, narrow), F32), ((NA, SAVE), BF), ((NA, SAVE), BF)]
         + [((NG, width), BF)] * 3 + [((AT["c"][1], width), BF)] + [((COL_SENT, width), BF)] * 2,
         [VMEM] * 9 + [ANY],
-        [student_in, ids, TO_A, s_qkv, s_out, s_proj, spread, t_qkv, PACK_OWN, hidden],
+        [student_in, ids, to_a, s_qkv, s_out, s_proj, spread, t_qkv, PACK_OWN, hidden],
         [pltpu.VMEM((COLS, TALL, narrow), BF)], 5 * 10**9,
     )
     cols_1, cols_2 = call(

time: 37.9 us -> 38.2 us (level)
  no operation moved by 1% of the time
where the time goes in v9:
time: 38.2 us; the launch traced here: 38.1 us
  Pallas kernels  19 us (50%)
  starting transfers between devices  13.6 us (36%)
  waiting for transfers between devices  4.25 us (11%)
  between operations  1.03 us (3%)
    pallas_call x6, Pallas kernels, call(): pl.pallas_call(kernel, name=name, out_shape=shapes, in_specs=specs, out_s...  19 us
    ppermute x1, starting transfers between devices, shards(): lax.ppermute(rows_1, ('lat', 'lon'), inner_swaps(lat_size, lon_size))  7.21 us
    ppermute x1, starting transfers between devices, shards(): cols_1 = lax.ppermute(cols_1, 'lon', swaps(lon_size, 1))  6.34 us
    ppermute x1, waiting for transfers between devices, shards(): cols_1 = lax.ppermute(cols_1, 'lon', swaps(lon_size, 1))  1.85 us
    ppermute x1, waiting for transfers between devices, shards(): cols_2 = lax.ppermute(cols_2, 'lon', swaps(lon_size, 0))  1.79 us
  transfers between devices with their start and end apart: 5, of which 3 were waited for; matrix products, arithmetic and copies ran while one was open for 0% of the time, Pallas kernels for 21%

profile of v9, /device:TPU:6, one launch (start us, length us, event | category | flops | bytes accessed | tf_op | source)
XLA Modules:
  0.0 38.1 jit_solution(18165486708587819248)
XLA Ops:
  0.6 0.1 collective-permute-start
  0.7 0.0 copy-start.9
  0.7 0.0 copy-start.13
  0.8 3.2 %teacher_own.1 = (bf16[320,512]{1,0:T(8,128)(2,1)S(1)}, bf16[320,128]{1,0:T(8,128)(2,1)S(1)}, bf16[320,128]{1,0:T(8,128)(2,1)S(1)}, bf16[320,512]{1,0:T(8,128)(2...) custom-call(bf16[1,12,24,512]{3,2,1,0:T(8,128)(2,1)} %bitcast.7, ...), custom_call_target="tpu_custom_call" | custom-call | flops 1000000000 | bytes 3711744 | tf_op jit(solution)/shard_map/teacher_own/pallas_call | solution.py:569
  4.0 0.0 copy-start
  4.0 0.0 copy-start.4
  4.0 0.0 copy-start.5
  4.0 0.0 copy-start.12
  4.0 4.2 %teacher_first.1 = (bf16[320,512]{1,0:T(8,128)(2,1)S(1)}, bf16[400,640]{1,0:T(8,128)(2,1)S(1)}, bf16[80,512]{1,0:T(8,128)(2,1)S(1)}, bf16[80,512]{1,0:T(8,128)(2,1)S(1)}) custom-call(bf16[1,12,24,512]{3,2,1,0:T(8,128)(2,1)S(1)} %collective-permute-done.far_ref, bf16[320,512]{1,0:T(8,128)(2,1)S(1)} %get-tuple-element.32.x_ref, ...), custom_call_target="tpu_custom_call" | custom-call | flops 3000000000 | bytes 4921344 | tf_op jit(solution)/shard_map/teacher_first/pallas_call | solution.py:569
  8.2 7.2 %collective-permute-start.1 = (bf16[80,512]{1,0:T(8,128)(2,1)S(1)}, bf16[80,512]{1,0:T(8,128)(2,1)S(1)}, u32[]{:S(2)}, u32[]{:S(2)}) collective-permute-start(bf16[80,512]{1,0:T(8,128)(2,1)S(1)} %get-tuple-element.42), channel_id=1, source_target_pairs={{0,2},{2,0},{4,6},{6,4},{8,10},{10,8},{12,14},{14,12},{16,18},{18,... | collective-permute-start | bytes 245768 | tf_op jit(solution)/shard_map/ppermute | solution.py:639
  15.5 0.0 copy-start.1
  15.5 0.0 copy-start.2
  15.5 0.0 copy-start.14
  15.5 3.8 %beside_rows.1 = (f32[320,256]{1,0:T(8,128)S(1)}, bf16[320,2816]{1,0:T(8,128)(2,1)S(1)}, bf16[320,2816]{1,0:T(8,128)(2,1)S(1)}, bf16[400,512]{1,0:T(8,128)(2,1)S...) custom-call(bf16[1,12,24,256]{3,2,1,0:T(8,128)(2,1)S(1)} %bitcast.5,, ...), custom_call_target="tpu_custom_call" | custom-call | flops 5000000000 | bytes 5799936 | tf_op jit(solution)/shard_map/beside_rows/pallas_call | solution.py:569
  19.4 0.6 %collective-permute-done.2.second_ref = bf16[80,512]{1,0:T(8,128)(2,1)S(1)} collective-permute-done((bf16[80,512]{1,0:T(8,128)(2,1)S(1)}, bf16[80,512]{1,0:T(8,128)(2,1)S(1)}, u32[]{:S(2)}, u32[]{:S(2)}) %collective-permute-start.2) | collective-permute-done | bytes 81952 | tf_op jit(solution)/shard_map/ppermute | solution.py:638
  20.0 0.3 send_columns.1
  20.3 6.3 %collective-permute-start.3 = (bf16[112,512]{1,0:T(8,128)(2,1)S(1)}, bf16[112,512]{1,0:T(8,128)(2,1)S(1)}, u32[]{:S(2)}, u32[]{:S(2)}) collective-permute-start(bf16[112,512]{1,0:T(8,128)(2,1)S(1)} %get-tuple-element.52), channel_id=1, source_target_pairs={{0,30},{2,4},{4,2},{6,8},{8,6},{10,12},{12,10},{14,16},{16,14},{18... | collective-permute-start | bytes 344072 | tf_op jit(solution)/shard_map/ppermute | solution.py:657
  26.7 0.0 copy-start.8
  26.7 0.0 copy-start.10
  26.7 0.0 copy-start.11
  26.7 1.1 %beside_columns.1 = (bf16[224,640]{1,0:T(8,128)(2,1)S(1)}, bf16[224,512]{1,0:T(8,128)(2,1)S(1)}, bf16[224,512]{1,0:T(8,128)(2,1)S(1)}, bf16[48,512]{1,0:T(8,128)(2,1)S(1)}, bf16[48,512]{1,0:T(8,128)(2,1)S(1)}) custom-call(bf16[400,640]{1,0:T(8,128)(2,1)S(1)} %get-tuple-element.41.g_ref, bf16[80,512]{1,0:T(8,128)(2,1)S(1)} %collective-permute-done.1.first_ref, ...), custom_call_target="tpu_custom_call" | custom-call | flops 2000000000 | bytes 5182976 | tf_op jit(solution)/shard_map/beside_columns/pallas_call | solution.py:569
  27.8 1.9 %collective-permute-done.3.first_ref = bf16[112,512]{1,0:T(8,128)(2,1)S(1)} collective-permute-done((bf16[112,512]{1,0:T(8,128)(2,1)S(1)}, bf16[112,512]{1,0:T(8,128)(2,1)S(1)}, u32[]{:S(2)}, u32[]{:S(2)}) %collective-permute-start.3) | collective-permute-done | bytes 114720 | tf_op jit(solution)/shard_map/ppermute | solution.py:657
  29.7 1.8 %collective-permute-done.4.second_ref = bf16[112,512]{1,0:T(8,128)(2,1)S(1)} collective-permute-done((bf16[112,512]{1,0:T(8,128)(2,1)S(1)}, bf16[112,512]{1,0:T(8,128)(2,1)S(1)}, u32[]{:S(2)}, u32[]{:S(2)}) %collective-permute-start.4) | collective-permute-done | bytes 114720 | tf_op jit(solution)/shard_map/ppermute | solution.py:656
  31.5 6.4 %teacher_second.1 = (bf16[1,12,24,512]{3,2,1,0:T(8,128)(2,1)}, f32[1,12,24,256]{3,2,1,0:T(8,128)}) custom-call(bf16[320,512]{1,0:T(8,128)(2,1)S(1)} %get-tuple-element.40.after_ref.h_ref, bf16[400,640]{1,0:T(8,128)(2,1)S(1)} %get-tuple-element.41.g_ref, bf16[224,640]{1,0:T(8,128)(2,1)S(1)} %get-tuple-element.51.edge_ref, ...), custom_call_target="tpu_custom_call" | custom-call | flops 6000000000 | bytes 13201920 | tf_op jit(solution)/shard_map/teacher_second/pallas_call | solution.py:569
  (22 shorter events, 0.1 us)
Async XLA Ops:
  0.6 3.3 %collective-permute-start = (bf16[1,12,24,512]{3,2,1,0:T(8,128)(2,1)}, bf16[1,12,24,512]{3,2,1,0:T(8,128)(2,1)S(1)}, u32[]{:S(2)}, u32[]{:S(2)}) collective-permute-start(bf16[1,12,24,512]{3,2,1,0:T(8,128)(2,1)} %bitcast.6), channel_id=1, source_target_pairs={{0,1},{1,0},{2,3},{3,2},{4,5},{5,4},{6,7},{7,6},{8,9},{9,8},{10,11... | collective-permute-start | bytes 884744 | tf_op jit(solution)/shard_map/ppermute | solution.py:614
  0.7 3.2 %copy-start.9 = (bf16[400,320]{1,0:T(8,128)(2,1)S(1)}, bf16[400,320]{1,0:T(8,128)(2,1)}, u32[]{:S(2)}) copy-start(bf16[400,320]{1,0:T(8,128)(2,1)} %constant.27.clone.a_to_g) | copy-start | bytes 768004
  0.7 3.2 %copy-start.13 = (bf16[128,112]{1,0:T(8,128)(2,1)S(1)}, bf16[128,112]{1,0:T(8,128)(2,1)}, u32[]{:S(2)}) copy-start(bf16[128,112]{1,0:T(8,128)(2,1)} %constant.28.clone.pack) | copy-start | bytes 86020
  4.0 11.5 %copy-start = (bf16[2,512,1536]{2,1,0:T(8,128)(2,1)S(1)}, bf16[2,512,1536]{2,1,0:T(8,128)(2,1)}, u32[]{:S(2)}) copy-start(bf16[2,512,1536]{2,1,0:T(8,128)(2,1)} %t_qkv.7) | copy-start | bytes 9437188
  4.0 11.5 %copy-start.4 = (bf16[2,256,768]{2,1,0:T(8,128)(2,1)S(1)}, bf16[2,256,768]{2,1,0:T(8,128)(2,1)}, u32[]{:S(2)}) copy-start(bf16[2,256,768]{2,1,0:T(8,128)(2,1)} %s_qkv.3) | copy-start | bytes 2359300
  4.0 11.5 %copy-start.5 = (bf16[2,256,256]{2,1,0:T(8,128)(2,1)S(1)}, bf16[2,256,256]{2,1,0:T(8,128)(2,1)}, u32[]{:S(2)}) copy-start(bf16[2,256,256]{2,1,0:T(8,128)(2,1)} %s_out.3) | copy-start | bytes 786436
  4.0 11.5 %copy-start.6 = (bf16[256,512]{1,0:T(8,128)(2,1)S(1)}, bf16[256,512]{1,0:T(8,128)(2,1)}, u32[]{:S(2)}) copy-start(bf16[256,512]{1,0:T(8,128)(2,1)} %proj.3) | copy-start | bytes 786436
  4.0 11.5 %copy-start.7 = (bf16[1,24,12,256]{3,1,2,0:T(8,128)(2,1)S(1)}, bf16[1,24,12,256]{3,1,2,0:T(8,128)(2,1)}, u32[]{:S(2)}) copy-start(bf16[1,24,12,256]{3,1,2,0:T(8,128)(2,1)} %param.21) | copy-start | bytes 442372
  4.0 11.5 %copy-start.12 = (bf16[128,112]{1,0:T(8,128)(2,1)S(1)}, bf16[128,112]{1,0:T(8,128)(2,1)}, u32[]{:S(2)}) copy-start(bf16[128,112]{1,0:T(8,128)(2,1)} %constant.29.clone.pack) | copy-start | bytes 86020
  8.2 11.1 %collective-permute-start.1 = (bf16[80,512]{1,0:T(8,128)(2,1)S(1)}, bf16[80,512]{1,0:T(8,128)(2,1)S(1)}, u32[]{:S(2)}, u32[]{:S(2)}) collective-permute-start(bf16[80,512]{1,0:T(8,128)(2,1)S(1)} %get-tuple-element.42), channel_id=1, source_target_pairs={{0,2},{2,0},{4,6},{6,4},{8,10},{10,8},{12,14},{14,12},{16,18},{18,... | collective-permute-start | bytes 245768 | tf_op jit(solution)/shard_map/ppermute | solution.py:639
  15.5 4.5 %collective-permute-start.2 = (bf16[80,512]{1,0:T(8,128)(2,1)S(1)}, bf16[80,512]{1,0:T(8,128)(2,1)S(1)}, u32[]{:S(2)}, u32[]{:S(2)}) collective-permute-start(bf16[80,512]{1,0:T(8,128)(2,1)S(1)} %get-tuple-element.43), channel_id=1, source_target_pairs={{0,32},{32,0},{64,96},{96,64},{128,160},{160,128},{192,224},{224,1... | collective-permute-start | bytes 245768 | tf_op jit(solution)/shard_map/ppermute | solution.py:638
  15.5 4.5 %copy-start.1 = (bf16[256,80]{1,0:T(8,128)(2,1)S(1)}, bf16[256,80]{1,0:T(8,128)(2,1)}, u32[]{:S(2)}) copy-start(bf16[256,80]{1,0:T(8,128)(2,1)} %constant.31.clone.from_south) | copy-start | bytes 122884
  15.5 4.5 %copy-start.2 = (bf16[256,80]{1,0:T(8,128)(2,1)S(1)}, bf16[256,80]{1,0:T(8,128)(2,1)}, u32[]{:S(2)}) copy-start(bf16[256,80]{1,0:T(8,128)(2,1)} %constant.30.clone.from_north) | copy-start | bytes 122884
  15.5 11.1 %copy-start.14 = (bf16[112,80]{1,0:T(8,128)(2,1)S(1)}, bf16[112,80]{1,0:T(8,128)(2,1)}, u32[]{:S(2)}) copy-start(bf16[112,80]{1,0:T(8,128)(2,1)} %constant.32.clone.open_rows) | copy-start | bytes 53764
  20.3 9.3 %collective-permute-start.3 = (bf16[112,512]{1,0:T(8,128)(2,1)S(1)}, bf16[112,512]{1,0:T(8,128)(2,1)S(1)}, u32[]{:S(2)}, u32[]{:S(2)}) collective-permute-start(bf16[112,512]{1,0:T(8,128)(2,1)S(1)} %get-tuple-element.52), channel_id=1, source_target_pairs={{0,30},{2,4},{4,2},{6,8},{8,6},{10,12},{12,10},{14,16},{16,14},{18... | collective-permute-start | bytes 344072 | tf_op jit(solution)/shard_map/ppermute | solution.py:657
  26.7 4.8 %collective-permute-start.4 = (bf16[112,512]{1,0:T(8,128)(2,1)S(1)}, bf16[112,512]{1,0:T(8,128)(2,1)S(1)}, u32[]{:S(2)}, u32[]{:S(2)}) collective-permute-start(bf16[112,512]{1,0:T(8,128)(2,1)S(1)} %get-tuple-element.50.after_ref), channel_id=1, source_target_pairs={{0,2},{2,0},{4,6},{6,4},{8,10},{10,8},{12,14},{14,12},{16,18},{18,... | collective-permute-start | bytes 344072 | tf_op jit(solution)/shard_map/ppermute | solution.py:656
  26.7 4.8 %copy-start.3 = (bf16[2,512,512]{2,1,0:T(8,128)(2,1)S(1)}, bf16[2,512,512]{2,1,0:T(8,128)(2,1)}, u32[]{:S(2)}) copy-start(bf16[2,512,512]{2,1,0:T(8,128)(2,1)} %t_out.3) | copy-start | bytes 3145732
  26.7 4.8 %copy-start.8 = (bf16[320,400]{1,0:T(8,128)(2,1)S(1)}, bf16[320,400]{1,0:T(8,128)(2,1)}, u32[]{:S(2)}) copy-start(bf16[320,400]{1,0:T(8,128)(2,1)} %constant.35.clone.g_to_a) | copy-start | bytes 768004
  26.7 4.8 %copy-start.10 = (bf16[384,320]{1,0:T(8,128)(2,1)S(1)}, bf16[384,320]{1,0:T(8,128)(2,1)}, u32[]{:S(2)}) copy-start(bf16[384,320]{1,0:T(8,128)(2,1)} %constant.34.clone.from_a) | copy-start | bytes 737284
  26.7 4.8 %copy-start.11 = (bf16[176,112]{1,0:T(8,128)(2,1)S(1)}, bf16[176,112]{1,0:T(8,128)(2,1)}, u32[]{:S(2)}) copy-start(bf16[176,112]{1,0:T(8,128)(2,1)} %constant.33.clone.open_cols) | copy-start | bytes 118276

commit v10 on v8

--- a/solution.py
+++ b/solution.py
@@ -281,18 +281,18 @@
 
 def teacher_own(
     x_hbm, reg_hbm, to_a_hbm, a_row_hbm, a_col_hbm, t_qkv,
-    x_out, id_ref, far_id_ref, q_ref, k_ref, v_ref,
-    pad_ref, x_ref, reg_ref, to_a, a_row, a_col, wqkv, sems,
+    x_out, id_ref, far_id_ref, q_ref, k_ref, v_ref, to_a, wqkv,
+    pad_ref, x_ref, reg_ref, a_row, a_col, sems,
 ):
+    width = x_ref.shape[3]
     copies = fetch(
         (x_hbm, x_ref, sems.at[0]),
-        (to_a_hbm, to_a, sems.at[2]),
-        (reg_hbm, reg_ref, sems.at[1]),
+        (to_a_hbm, to_a, sems.at[1]),
+        (reg_hbm, reg_ref, sems.at[2]),
         (a_row_hbm, a_row, sems.at[3]),
         (a_col_hbm, a_col, sems.at[4]),
         (t_qkv.at[0], wqkv, sems.at[5]),
     )
-    width = x_ref.shape[3]
     blocks = head_blocks()
     copies[0].wait()
     copies[1].wait()
@@ -310,15 +310,19 @@
 
 
 def teacher_first(
-    far_ref, x_ref, id_ref, far_id_ref, q_ref, k_ref, v_ref, to_a, a_to_g, pack, t_qkv, t_out,
-    h_ref, g_ref, first_ref, second_ref, pad_ref, wout, sems,
+    far_ref, x_ref, id_ref, far_id_ref, q_ref, k_ref, v_ref, to_a, rows_from_a, wqkv, t_out,
+    h_ref, first_ref, second_ref, pad_ref, wout, sems,
 ):
     copies = fetch((t_out.at[0], wout, sems.at[0]))
     width = x_ref.shape[1]
     blocks = head_blocks()
+    sent_ids = dot(rows_from_a[...], id_ref[...]).astype(BF)
+    sent_ids = dot_nt(jnp.full((8, 128), 1.0 / 128, BF), sent_ids)[0:1]
+    empty = jnp.zeros((1, width - 128), F32)
+    id_rows = [jnp.concatenate([sent_ids[:, i : i + 128], empty], axis=1) for i in (0, 128)]
     far = to_window_order(far_ref, pad_ref, to_a[...])
-    k_far = unit(dot(far, t_qkv[0, :, width : 2 * width]), blocks)[0].astype(BF)
-    v_far = dot(far, t_qkv[0, :, 2 * width :]).astype(BF)
+    k_far = unit(dot(far, wqkv[:, width : 2 * width]), blocks)[0].astype(BF)
+    v_far = dot(far, wqkv[:, 2 * width :]).astype(BF)
     windows = []
     for w in range(4):
         rows = slice(w * WIN, (w + 1) * WIN)
@@ -332,16 +336,10 @@
     copies[0].wait()
     h = residual(x_ref[...], jnp.concatenate(atts, axis=0), wout[...])[0]
     h_ref[...] = h
-    spread = dot(a_to_g[...], jnp.concatenate([h, id_ref[...]], axis=1)).astype(BF)
-    g_ref[...] = spread
-    north, south = [
-        packed(
-            jnp.concatenate([part(spread, n) for n in names], axis=0),
-            pack[...], ROW_TOKENS, ROW_SENT,
-        )
-        for names in (TO_NORTH, TO_SOUTH)
-    ]
-    first_ref[...], second_ref[...] = swapped("lat", north, south)
+    values = [dot(rows_from_a[i : i + ROW_SENT], h) for i in (0, 128)]
+    at = lax.broadcasted_iota(jnp.int32, (ROW_SENT, 1), 0)
+    payloads = [jnp.where(at == ROW_TOKENS, row, x) for row, x in zip(id_rows, values)]
+    first_ref[...], second_ref[...] = swapped("lat", *payloads)
 
 
 def swapped(axis, low, high):
@@ -374,6 +372,17 @@
 
 TO_NORTH = ("nw", "n", "ne")
 TO_SOUTH = ("sw", "s", "se")
+
+
+def _row_table():
+    table = np.zeros((256, NA), ml_dtypes.bfloat16)
+    for start, names in ((0, TO_NORTH), (128, TO_SOUTH)):
+        rows = np.concatenate([A_TO_G[AT[n][0] : AT[n][0] + AT[n][1]] for n in names])
+        table[start : start + 128] = PACK_ROWS.astype(np.float32) @ rows.astype(np.float32)
+    return table
+
+
+ROWS_FROM_A = _row_table()
 TO_WEST = (("N", "sw"), ("", "nw"), ("", "w"), ("", "sw"), ("S", "nw"))
 TO_EAST = (("N", "se"), ("", "ne"), ("", "e"), ("", "se"), ("S", "ne"))
 EXTRA = {
@@ -425,11 +434,14 @@
 
 
 def beside_rows(
-    x_ref, id_ref, to_a, s_qkv, s_out, proj, g_ref, t_qkv, pack, after_ref,
-    g0_ref, save0, save1, q_ref, k_ref, v_ref, att_ref, west_ref, east_ref, pad_ref,
+    x_ref, id_ref, to_a, s_qkv, s_out, proj, hidden_ref, a_to_g, t_qkv, pack, after_ref,
+    g_ref, g0_ref, save0, save1, q_ref, k_ref, v_ref, att_ref, west_ref, east_ref, pad_ref,
 ):
-    width = g_ref.shape[1] - 128
+    width = hidden_ref.shape[1]
     blocks = head_blocks()
+    spread = jnp.concatenate([hidden_ref[...], id_ref[...]], axis=1)
+    spread = dot(a_to_g[...], spread).astype(BF)
+    g_ref[...] = spread
     x = to_window_order(x_ref, pad_ref, to_a[...])
     h = student_layer(x, s_qkv[0], s_out[0], id_ref[...], save0)
     h = student_layer(h, s_qkv[1], s_out[1], id_ref[...], save1)
@@ -437,17 +449,17 @@
     g0_ref[...] = dot_nt(predicted.astype(BF), proj[...])
 
     for ref, items in ((west_ref, TO_WEST), (east_ref, TO_EAST)):
-        rows = gather([(g_ref, OWN)], items[1:4])
+        rows = gather([(spread, OWN)], items[1:4])
         ref[...] = packed(rows, pack[...], COL_TOKENS, COL_SENT)
 
-    rows = g_ref[:, :width]
+    rows = spread[:, :width]
     q = (unit(dot(rows, t_qkv[1, :, :width]), blocks)[0] * SCALE).astype(BF)
     k = unit(dot(rows, t_qkv[1, :, width : 2 * width]), blocks)[0].astype(BF)
     v = dot(rows, t_qkv[1, :, 2 * width :]).astype(BF)
     q_ref[...] = q
     k_ref[...] = k
     v_ref[...] = v
-    ids = part(g_ref, "c")[:, width:]
+    ids = part(spread, "c")[:, width:]
     [att_ref[...]] = window_attention([(part(q, "c"), [part(k, "c"), part(v, "c")], (ids, ids))])
 
 
@@ -612,31 +624,34 @@
         pltpu.with_memory_space_constraint(jnp.asarray(a), pltpu.HBM)
         for a in (teacher_in, regions, TO_A, A_ROW, A_COL, t_qkv)
     ]
-    x, ids, far_ids, q, k, v = call(
+    x, ids, far_ids, q, k, v, to_a, wqkv = call(
         teacher_own, "teacher_own",
-        [((NA, width), BF), ((NA, 128), BF), ((NA, 128), BF)] + [((NA, width), BF)] * 3,
+        [((NA, width), BF), ((NA, 128), BF), ((NA, 128), BF)] + [((NA, width), BF)] * 3
+        + [((NA, NAT), BF), (t_qkv.shape[1:], BF)],
         [HBM] * 6, pinned,
         [pltpu.VMEM((COLS, TALL, width), BF)]
-        + buffers(teacher_in, regions, TO_A, A_ROW, A_COL, t_qkv[0]),
+        + buffers(teacher_in, regions, A_ROW, A_COL)[:-1]
+        + [pltpu.SemaphoreType.DMA((6,))],
         10**9,
     )
-    hidden, spread, rows_1, rows_2 = call(
+    hidden, rows_1, rows_2 = call(
         teacher_first, "teacher_first",
-        [((NA, width), BF), ((NG, wide), BF)] + [((ROW_SENT, width), BF)] * 2,
-        [VMEM] * 11 + [HBM],
-        [far, x, ids, far_ids, q, k, v, TO_A, A_TO_G, PACK_ROWS, t_qkv]
+        [((NA, width), BF)] + [((ROW_SENT, width), BF)] * 2,
+        [VMEM] * 10 + [HBM],
+        [far, x, ids, far_ids, q, k, v, to_a, ROWS_FROM_A, wqkv]
         + [pltpu.with_memory_space_constraint(t_out, pltpu.HBM)],
         [pltpu.VMEM((COLS, TALL, width), BF)] + buffers(t_out[0]), 3 * 10**9,
     )
+    sent = rows_2
     rows_2 = lax.ppermute(rows_2, "lat", swaps(lat_size, 0))
     rows_1 = lax.ppermute(rows_1, ("lat", "lon"), inner_swaps(lat_size, lon_size))
 
-    g0, save0, save1, q, k, v, c_att, west, east = call(
+    spread, g0, save0, save1, q, k, v, c_att, west, east = call(
         beside_rows, "beside_rows",
-        [((NA, narrow), F32), ((NA, SAVE), BF), ((NA, SAVE), BF)]
+        [((NG, wide), BF), ((NA, narrow), F32), ((NA, SAVE), BF), ((NA, SAVE), BF)]
         + [((NG, width), BF)] * 3 + [((AT["c"][1], width), BF)] + [((COL_SENT, width), BF)] * 2,
-        [VMEM] * 9 + [ANY],
-        [student_in, ids, TO_A, s_qkv, s_out, s_proj, spread, t_qkv, PACK_OWN, hidden],
+        [VMEM] * 10 + [ANY],
+        [student_in, ids, to_a, s_qkv, s_out, s_proj, hidden, A_TO_G, t_qkv, PACK_OWN, sent],
         [pltpu.VMEM((COLS, TALL, narrow), BF)], 5 * 10**9,
     )
     cols_1, cols_2 = call(

time: 37.9 us -> 37.3 us (0.984)
  Pallas kernels: 18.8 us -> 18.3 us
    pallas_call x6, Pallas kernels: 18.8 us -> 18.3 us  [call(): pl.pallas_call(kernel, name=name, out_shape=shapes, in_specs=specs, out_s...]
where the time goes in v10:
time: 37.3 us; the launch traced here: 37.1 us
  Pallas kernels  18.3 us (49%)
  starting transfers between devices  13.6 us (36%)
  waiting for transfers between devices  4.11 us (11%)
  between operations  1.03 us (3%)
    pallas_call x6, Pallas kernels, call(): pl.pallas_call(kernel, name=name, out_shape=shapes, in_specs=specs, out_s...  18.3 us
    ppermute x1, starting transfers between devices, shards(): lax.ppermute(rows_1, ('lat', 'lon'), inner_swaps(lat_size, lon_size))  7.18 us
    ppermute x1, starting transfers between devices, shards(): cols_1 = lax.ppermute(cols_1, 'lon', swaps(lon_size, 1))  6.36 us
    ppermute x1, waiting for transfers between devices, shards(): cols_1 = lax.ppermute(cols_1, 'lon', swaps(lon_size, 1))  1.85 us
    ppermute x1, waiting for transfers between devices, shards(): cols_2 = lax.ppermute(cols_2, 'lon', swaps(lon_size, 0))  1.79 us
  transfers between devices with their start and end apart: 5, of which 3 were waited for; matrix products, arithmetic and copies ran while one was open for 0% of the time, Pallas kernels for 21%

profile of v10, /device:TPU:6, one launch (start us, length us, event | category | flops | bytes accessed | tf_op | source)
XLA Modules:
  0.0 37.1 jit_solution(12318142068472706735)
XLA Ops:
  0.6 0.1 collective-permute-start
  0.7 0.0 copy-start.11
  0.7 2.8 %teacher_own.1 = (bf16[320,512]{1,0:T(8,128)(2,1)S(1)}, bf16[320,128]{1,0:T(8,128)(2,1)S(1)}, bf16[320,128]{1,0:T(8,128)(2,1)S(1)}, bf16[320,512]{1,0:T(8,128)(2...) custom-call(bf16[1,12,24,512]{3,2,1,0:T(8,128)(2,1)} %bitcast.7, ...), custom_call_target="tpu_custom_call" | custom-call | flops 1000000000 | bytes 3711744 | tf_op jit(solution)/shard_map/teacher_own/pallas_call | solution.py:576
  3.6 0.0 copy-start
  3.6 0.0 copy-start.5
  3.6 0.0 copy-start.6
  3.6 0.0 copy-start.9
  3.6 0.0 copy-start.13
  3.7 3.7 %teacher_first.1 = (bf16[320,512]{1,0:T(8,128)(2,1)S(1)}, bf16[80,512]{1,0:T(8,128)(2,1)S(1)}, bf16[80,512]{1,0:T(8,128)(2,1)S(1)}) custom-call(bf16[1,12,24,512]{3,2,1,0:T(8,128)(2,1)S(1)} %collective-permute-done.far_ref, bf16[320,512]{1,0:T(8,128)(2,1)S(1)} %get-tuple-element.32.x_ref, bf16[320,128]{1,0:T(8,128)(2,1)S(1)} %get-tuple-element.33.id_ref, ...), custom_call_target="tpu_custom_call" | custom-call | flops 3000000000 | bytes 4800512 | tf_op jit(solution)/shard_map/teacher_first/pallas_call | solution.py:576
  7.3 7.2 %collective-permute-start.1 = (bf16[80,512]{1,0:T(8,128)(2,1)S(1)}, bf16[80,512]{1,0:T(8,128)(2,1)S(1)}, u32[]{:S(2)}, u32[]{:S(2)}) collective-permute-start(bf16[80,512]{1,0:T(8,128)(2,1)S(1)} %get-tuple-element.43), channel_id=1, source_target_pairs={{0,2},{2,0},{4,6},{6,4},{8,10},{10,8},{12,14},{14,12},{16,18},{18,... | collective-permute-start | bytes 245768 | tf_op jit(solution)/shard_map/ppermute | solution.py:647
  14.6 0.0 copy-start.1
  14.6 0.0 copy-start.2
  14.6 0.0 copy-start.14
  14.6 4.0 %beside_rows.1 = (bf16[400,640]{1,0:T(8,128)(2,1)S(1)}, f32[320,256]{1,0:T(8,128)S(1)}, bf16[320,2816]{1,0:T(8,128)(2,1)S(1)}, bf16[320,2816]{1,0:T(8,128)(2,1)S...) custom-call(bf16[1,12,24,256]{3,2,1,0:T(8,128)(2,1)S(1)} %bitcast.5,, ...), custom_call_target="tpu_custom_call" | custom-call | flops 5000000000 | bytes 5625856 | tf_op jit(solution)/shard_map/beside_rows/pallas_call | solution.py:576
  18.6 0.5 %collective-permute-done.2.second_ref = bf16[80,512]{1,0:T(8,128)(2,1)S(1)} collective-permute-done((bf16[80,512]{1,0:T(8,128)(2,1)S(1)}, bf16[80,512]{1,0:T(8,128)(2,1)S(1)}, u32[]{:S(2)}, u32[]{:S(2)}) %collective-permute-start.2) | collective-permute-done | bytes 81952 | tf_op jit(solution)/shard_map/ppermute | solution.py:646
  19.1 0.3 send_columns.1
  19.4 6.4 %collective-permute-start.3 = (bf16[112,512]{1,0:T(8,128)(2,1)S(1)}, bf16[112,512]{1,0:T(8,128)(2,1)S(1)}, u32[]{:S(2)}, u32[]{:S(2)}) collective-permute-start(bf16[112,512]{1,0:T(8,128)(2,1)S(1)} %get-tuple-element.52), channel_id=1, source_target_pairs={{0,30},{2,4},{4,2},{6,8},{8,6},{10,12},{12,10},{14,16},{16,14},{18... | collective-permute-start | bytes 344072 | tf_op jit(solution)/shard_map/ppermute | solution.py:665
  25.8 0.0 copy-start.8
  25.8 0.0 copy-start.10
  25.8 0.0 copy-start.12
  25.8 1.1 %beside_columns.1 = (bf16[224,640]{1,0:T(8,128)(2,1)S(1)}, bf16[224,512]{1,0:T(8,128)(2,1)S(1)}, bf16[224,512]{1,0:T(8,128)(2,1)S(1)}, bf16[48,512]{1,0:T(8,128)(2,1)S(1)}, bf16[48,512]{1,0:T(8,128)(2,1)S(1)}) custom-call(bf16[400,640]{1,0:T(8,128)(2,1)S(1)} %get-tuple-element.42.g_ref, bf16[80,512]{1,0:T(8,128)(2,1)S(1)} %collective-permute-done.1.first_ref, ...), custom_call_target="tpu_custom_call" | custom-call | flops 2000000000 | bytes 5182976 | tf_op jit(solution)/shard_map/beside_columns/pallas_call | solution.py:576
  26.9 1.8 %collective-permute-done.3.first_ref = bf16[112,512]{1,0:T(8,128)(2,1)S(1)} collective-permute-done((bf16[112,512]{1,0:T(8,128)(2,1)S(1)}, bf16[112,512]{1,0:T(8,128)(2,1)S(1)}, u32[]{:S(2)}, u32[]{:S(2)}) %collective-permute-start.3) | collective-permute-done | bytes 114720 | tf_op jit(solution)/shard_map/ppermute | solution.py:665
  28.7 1.8 %collective-permute-done.4.second_ref = bf16[112,512]{1,0:T(8,128)(2,1)S(1)} collective-permute-done((bf16[112,512]{1,0:T(8,128)(2,1)S(1)}, bf16[112,512]{1,0:T(8,128)(2,1)S(1)}, u32[]{:S(2)}, u32[]{:S(2)}) %collective-permute-start.4) | collective-permute-done | bytes 114720 | tf_op jit(solution)/shard_map/ppermute | solution.py:664
  30.6 6.4 %teacher_second.1 = (bf16[1,12,24,512]{3,2,1,0:T(8,128)(2,1)}, f32[1,12,24,256]{3,2,1,0:T(8,128)}) custom-call(bf16[320,512]{1,0:T(8,128)(2,1)S(1)} %get-tuple-element.40.hidden_ref.h_ref, bf16[400,640]{1,0:T(8,128)(2,1)S(1)} %get-tuple-element.42.g_ref, bf16[224,640]{1,0:T(8,128)(2,1)S(1)} %get-tuple-element.51.edge_ref, ...), custom_call_target="tpu_custom_call" | custom-call | flops 6000000000 | bytes 13201920 | tf_op jit(solution)/shard_map/teacher_second/pallas_call | solution.py:576
  (22 shorter events, 0.1 us)
Async XLA Ops:
  0.6 2.9 %collective-permute-start = (bf16[1,12,24,512]{3,2,1,0:T(8,128)(2,1)}, bf16[1,12,24,512]{3,2,1,0:T(8,128)(2,1)S(1)}, u32[]{:S(2)}, u32[]{:S(2)}) collective-permute-start(bf16[1,12,24,512]{3,2,1,0:T(8,128)(2,1)} %bitcast.6), channel_id=1, source_target_pairs={{0,1},{1,0},{2,3},{3,2},{4,5},{5,4},{6,7},{7,6},{8,9},{9,8},{10,11... | collective-permute-start | bytes 884744 | tf_op jit(solution)/shard_map/ppermute | solution.py:621
  0.7 2.8 %copy-start.11 = (bf16[256,320]{1,0:T(8,128)(2,1)S(1)}, bf16[256,320]{1,0:T(8,128)(2,1)}, u32[]{:S(2)}) copy-start(bf16[256,320]{1,0:T(8,128)(2,1)} %constant.27.clone.rows_from_a) | copy-start | bytes 491524
  3.6 10.9 %copy-start = (bf16[2,512,1536]{2,1,0:T(8,128)(2,1)S(1)}, bf16[2,512,1536]{2,1,0:T(8,128)(2,1)}, u32[]{:S(2)}) copy-start(bf16[2,512,1536]{2,1,0:T(8,128)(2,1)} %t_qkv.7) | copy-start | bytes 9437188
  3.6 10.9 %copy-start.4 = (bf16[2,256,768]{2,1,0:T(8,128)(2,1)S(1)}, bf16[2,256,768]{2,1,0:T(8,128)(2,1)}, u32[]{:S(2)}) copy-start(bf16[2,256,768]{2,1,0:T(8,128)(2,1)} %s_qkv.3) | copy-start | bytes 2359300
  3.6 10.9 %copy-start.5 = (bf16[2,256,256]{2,1,0:T(8,128)(2,1)S(1)}, bf16[2,256,256]{2,1,0:T(8,128)(2,1)}, u32[]{:S(2)}) copy-start(bf16[2,256,256]{2,1,0:T(8,128)(2,1)} %s_out.3) | copy-start | bytes 786436
  3.6 10.9 %copy-start.6 = (bf16[256,512]{1,0:T(8,128)(2,1)S(1)}, bf16[256,512]{1,0:T(8,128)(2,1)}, u32[]{:S(2)}) copy-start(bf16[256,512]{1,0:T(8,128)(2,1)} %proj.3) | copy-start | bytes 786436
  3.6 10.9 %copy-start.7 = (bf16[1,24,12,256]{3,1,2,0:T(8,128)(2,1)S(1)}, bf16[1,24,12,256]{3,1,2,0:T(8,128)(2,1)}, u32[]{:S(2)}) copy-start(bf16[1,24,12,256]{3,1,2,0:T(8,128)(2,1)} %param.21) | copy-start | bytes 442372
  3.6 10.9 %copy-start.9 = (bf16[400,320]{1,0:T(8,128)(2,1)S(1)}, bf16[400,320]{1,0:T(8,128)(2,1)}, u32[]{:S(2)}) copy-start(bf16[400,320]{1,0:T(8,128)(2,1)} %constant.28.clone.a_to_g) | copy-start | bytes 768004
  3.6 10.9 %copy-start.13 = (bf16[128,112]{1,0:T(8,128)(2,1)S(1)}, bf16[128,112]{1,0:T(8,128)(2,1)}, u32[]{:S(2)}) copy-start(bf16[128,112]{1,0:T(8,128)(2,1)} %constant.29.clone.pack) | copy-start | bytes 86020
  7.3 11.3 %collective-permute-start.1 = (bf16[80,512]{1,0:T(8,128)(2,1)S(1)}, bf16[80,512]{1,0:T(8,128)(2,1)S(1)}, u32[]{:S(2)}, u32[]{:S(2)}) collective-permute-start(bf16[80,512]{1,0:T(8,128)(2,1)S(1)} %get-tuple-element.43), channel_id=1, source_target_pairs={{0,2},{2,0},{4,6},{6,4},{8,10},{10,8},{12,14},{14,12},{16,18},{18,... | collective-permute-start | bytes 245768 | tf_op jit(solution)/shard_map/ppermute | solution.py:647
  14.5 4.6 %collective-permute-start.2 = (bf16[80,512]{1,0:T(8,128)(2,1)S(1)}, bf16[80,512]{1,0:T(8,128)(2,1)S(1)}, u32[]{:S(2)}, u32[]{:S(2)}) collective-permute-start(bf16[80,512]{1,0:T(8,128)(2,1)S(1)} %get-tuple-element.41.after_ref), channel_id=1, source_target_pairs={{0,32},{32,0},{64,96},{96,64},{128,160},{160,128},{192,224},{224,1... | collective-permute-start | bytes 245768 | tf_op jit(solution)/shard_map/ppermute | solution.py:646
  14.6 4.5 %copy-start.1 = (bf16[256,80]{1,0:T(8,128)(2,1)S(1)}, bf16[256,80]{1,0:T(8,128)(2,1)}, u32[]{:S(2)}) copy-start(bf16[256,80]{1,0:T(8,128)(2,1)} %constant.31.clone.from_south) | copy-start | bytes 122884
  14.6 4.5 %copy-start.2 = (bf16[256,80]{1,0:T(8,128)(2,1)S(1)}, bf16[256,80]{1,0:T(8,128)(2,1)}, u32[]{:S(2)}) copy-start(bf16[256,80]{1,0:T(8,128)(2,1)} %constant.30.clone.from_north) | copy-start | bytes 122884
  14.6 11.2 %copy-start.14 = (bf16[112,80]{1,0:T(8,128)(2,1)S(1)}, bf16[112,80]{1,0:T(8,128)(2,1)}, u32[]{:S(2)}) copy-start(bf16[112,80]{1,0:T(8,128)(2,1)} %constant.32.clone.open_rows) | copy-start | bytes 53764
  19.4 9.4 %collective-permute-start.3 = (bf16[112,512]{1,0:T(8,128)(2,1)S(1)}, bf16[112,512]{1,0:T(8,128)(2,1)S(1)}, u32[]{:S(2)}, u32[]{:S(2)}) collective-permute-start(bf16[112,512]{1,0:T(8,128)(2,1)S(1)} %get-tuple-element.52), channel_id=1, source_target_pairs={{0,30},{2,4},{4,2},{6,8},{8,6},{10,12},{12,10},{14,16},{16,14},{18... | collective-permute-start | bytes 344072 | tf_op jit(solution)/shard_map/ppermute | solution.py:665
  25.7 4.8 %collective-permute-start.4 = (bf16[112,512]{1,0:T(8,128)(2,1)S(1)}, bf16[112,512]{1,0:T(8,128)(2,1)S(1)}, u32[]{:S(2)}, u32[]{:S(2)}) collective-permute-start(bf16[112,512]{1,0:T(8,128)(2,1)S(1)} %get-tuple-element.50.after_ref), channel_id=1, source_target_pairs={{0,2},{2,0},{4,6},{6,4},{8,10},{10,8},{12,14},{14,12},{16,18},{18,... | collective-permute-start | bytes 344072 | tf_op jit(solution)/shard_map/ppermute | solution.py:664
  25.7 4.8 %copy-start.3 = (bf16[2,512,512]{2,1,0:T(8,128)(2,1)S(1)}, bf16[2,512,512]{2,1,0:T(8,128)(2,1)}, u32[]{:S(2)}) copy-start(bf16[2,512,512]{2,1,0:T(8,128)(2,1)} %t_out.3) | copy-start | bytes 3145732
  25.8 4.8 %copy-start.8 = (bf16[320,400]{1,0:T(8,128)(2,1)S(1)}, bf16[320,400]{1,0:T(8,128)(2,1)}, u32[]{:S(2)}) copy-start(bf16[320,400]{1,0:T(8,128)(2,1)} %constant.35.clone.g_to_a) | copy-start | bytes 768004
  25.8 4.8 %copy-start.10 = (bf16[384,320]{1,0:T(8,128)(2,1)S(1)}, bf16[384,320]{1,0:T(8,128)(2,1)}, u32[]{:S(2)}) copy-start(bf16[384,320]{1,0:T(8,128)(2,1)} %constant.34.clone.from_a) | copy-start | bytes 737284
  25.8 4.8 %copy-start.12 = (bf16[176,112]{1,0:T(8,128)(2,1)S(1)}, bf16[176,112]{1,0:T(8,128)(2,1)}, u32[]{:S(2)}) copy-start(bf16[176,112]{1,0:T(8,128)(2,1)} %constant.33.clone.open_cols) | copy-start | bytes 118276

commit v11 on v10

--- a/solution.py
+++ b/solution.py
@@ -411,7 +411,6 @@
 OWN = {("", name): AT[name][0] for name in ORDER}
 EDGE = _spots([("N", n) for n in TO_SOUTH] + [("S", n) for n in TO_NORTH])
 COME = _spots([(s + "E", n) for s, n in TO_WEST] + [(s + "W", n) for s, n in TO_EAST])
-NE_ROWS = 2 * sum(AT[n][1] for n in TO_NORTH)
 
 
 def gather(sources, items):
@@ -425,12 +424,15 @@
     return blocks[0] if len(blocks) == 1 else jnp.concatenate(blocks, axis=0)
 
 
-def window_attention(windows):
+def window_sums(windows):
     found = attend([(q, k, v, id_mask(*ids)) for q, (k, v), ids in windows])
     return [
-        jnp.concatenate([(n / d).astype(BF) for n, d in zip(nums, dens)], axis=1)
-        for nums, dens, _ in found
-    ]
+        (jnp.concatenate(nums, axis=1), jnp.concatenate(dens, axis=1)) for nums, dens, _ in found
+    ]
+
+
+def window_attention(windows):
+    return [(num / den).astype(BF) for num, den in window_sums(windows)]
 
 
 def beside_rows(
@@ -492,7 +494,7 @@
 
 def beside_columns(
     g_ref, first_ref, second_ref, open_rows, t_qkv, q_ref, k_ref, v_ref, after_ref,
-    edge_ref, k_out, v_out, n_ref, s_ref,
+    n_ref, s_ref, num_ref, den_ref,
 ):
     width = g_ref.shape[1] - 128
     blocks = head_blocks()
@@ -500,23 +502,24 @@
     for sent, there in zip(swapped("lat", first_ref[...], second_ref[...]), on_map()):
         rows = opened(sent, open_rows[...], ROW_TOKENS)
         edge.append(jnp.concatenate([rows[:, :width], rows[:, width:] * there.astype(BF)], axis=1))
-    edge_ref[...] = jnp.concatenate(edge, axis=0)
-    rows = edge_ref[:, :width]
+    edge = jnp.concatenate(edge, axis=0)
+    rows = edge[:, :width]
     k = unit(dot(rows, t_qkv[1, :, width : 2 * width]), blocks)[0].astype(BF)
     v = dot(rows, t_qkv[1, :, 2 * width :]).astype(BF)
-    k_out[...] = k
-    v_out[...] = v
     windows = []
-    for name in ("n", "s"):
-        items = (("", name),) + EXTRA[name]
-        keys = [gather([(own, OWN), (edge, EDGE)], items) for own, edge in ((k_ref, k), (v_ref, v))]
-        ids = [gather([(g_ref, OWN), (edge_ref, EDGE)], some)[:, width:] for some in (items[:1], items)]
+    for name in ("n", "s") + LATE:
+        items = [("", name)] + [item for item in EXTRA[name] if item in EDGE]
+        keys = [gather([(own, OWN), (x, EDGE)], items) for own, x in ((k_ref, k), (v_ref, v))]
+        ids = [gather([(g_ref, OWN), (edge, EDGE)], some)[:, width:] for some in (items[:1], items)]
         windows.append((part(q_ref, name), keys, ids))
-    n_ref[...], s_ref[...] = window_attention(windows)
+    sums = window_sums(windows)
+    for ref, (num, den) in zip((n_ref, s_ref), sums):
+        ref[...] = (num / den).astype(BF)
+    num_ref[...], den_ref[...] = [jnp.concatenate(x, axis=0) for x in zip(*sums[2:])]
 
 
 def teacher_second(
-    h_ref, g_ref, edge_ref, first_ref, second_ref, q_ref, k_ref, v_ref, k_edge, v_edge,
+    h_ref, g_ref, first_ref, second_ref, q_ref, num_ref, den_ref,
     c_ref, n_ref, s_ref, open_cols, from_a, g_to_a, t_qkv, t_out, proj, s_qkv, s_out,
     g0_ref, save0, save1, out_hbm, grad_hbm, out_ref, grad_ref, sems,
 ):
@@ -531,17 +534,15 @@
     atts = {"c": c_ref[...], "n": n_ref[...], "s": s_ref[...]}
     windows = []
     for name in LATE:
-        items = (("", name),) + EXTRA[name]
-        keys = [
-            gather([(own, OWN), (edge, EDGE), (new, COME)], items)
-            for own, edge, new in ((k_ref, k_edge, k), (v_ref, v_edge, v))
-        ]
-        ids = [
-            gather([(g_ref, OWN), (edge_ref, EDGE), (came, COME)], some)[:, width:]
-            for some in (items[:1], items)
-        ]
+        items = [item for item in EXTRA[name] if item in COME]
+        keys = [gather([(new, COME)], items) for new in (k, v)]
+        ids = (part(g_ref, name)[:, width:], gather([(came, COME)], items)[:, width:])
         windows.append((part(q_ref, name), keys, ids))
-    atts.update(zip(LATE, window_attention(windows)))
+    start = 0
+    for name, (num, den) in zip(LATE, window_sums(windows)):
+        early = slice(start, start + num.shape[0])
+        atts[name] = ((num_ref[early] + num) / (den_ref[early] + den)).astype(BF)
+        start += num.shape[0]
     att = jnp.concatenate([atts[name] for name in ORDER], axis=0)
     att = dot(g_to_a[...], att).astype(BF)
     teacher = residual(h_ref[...], att, t_out[1])[0]
@@ -664,13 +665,14 @@
     cols_2 = lax.ppermute(cols_2, "lon", swaps(lon_size, 0))
     cols_1 = lax.ppermute(cols_1, "lon", swaps(lon_size, 1))
 
-    edge, k_edge, v_edge, n_att, s_att = call(
+    late = sum(AT[name][1] for name in LATE)
+    n_att, s_att, nums, dens = call(
         beside_columns, "beside_columns",
-        [((NE_ROWS, wide), BF)] + [((NE_ROWS, width), BF)] * 2 + [((AT["n"][1], width), BF)] * 2,
+        [((AT["n"][1], width), BF)] * 2 + [((late, width), F32)] * 2,
         [VMEM] * 8 + [ANY],
         [spread, rows_1, rows_2, OPEN_ROWS, t_qkv, q, k, v, sent], (), 2 * 10**9,
     )
-    args = [hidden, spread, edge, cols_1, cols_2, q, k, v, k_edge, v_edge, c_att, n_att, s_att]
+    args = [hidden, spread, cols_1, cols_2, q, nums, dens, c_att, n_att, s_att]
     args += [OPEN_COLS, FROM_A, G_TO_A, t_qkv, t_out, s_proj, s_qkv, s_out, g0, save0, save1]
     out, grad = call(
         teacher_second, "teacher_second",

time: 37.3 us -> 36.9 us (0.989)
  waiting for transfers between devices: 4.11 us -> 3.46 us
    ppermute x1, waiting for transfers between devices: 1.85 us -> 1.19 us  [shards(): cols_1 = lax.ppermute(cols_1, 'lon', swaps(lon_size, 1))]
  transfers between devices with their start and end apart: 5 -> 5, of which waited for: 3 -> 3; matrix products, arithmetic and copies ran while one was open for 0% -> 0% of each run, Pallas kernels for 21% -> 23%
where the time goes in v11:
time: 36.9 us; the launch traced here: 36.8 us
  Pallas kernels  18.5 us (50%)
  starting transfers between devices  13.6 us (37%)
  waiting for transfers between devices  3.46 us (9%)
  between operations  1.03 us (3%)
    pallas_call x6, Pallas kernels, call(): pl.pallas_call(kernel, name=name, out_shape=shapes, in_specs=specs, out_s...  18.5 us
    ppermute x1, starting transfers between devices, shards(): lax.ppermute(rows_1, ('lat', 'lon'), inner_swaps(lat_size, lon_size))  7.18 us
    ppermute x1, starting transfers between devices, shards(): cols_1 = lax.ppermute(cols_1, 'lon', swaps(lon_size, 1))  6.36 us
    ppermute x1, waiting for transfers between devices, shards(): cols_2 = lax.ppermute(cols_2, 'lon', swaps(lon_size, 0))  1.79 us
    ppermute x1, waiting for transfers between devices, shards(): cols_1 = lax.ppermute(cols_1, 'lon', swaps(lon_size, 1))  1.19 us
  transfers between devices with their start and end apart: 5, of which 3 were waited for; matrix products, arithmetic and copies ran while one was open for 0% of the time, Pallas kernels for 23%

profile of v11, /device:TPU:6, one launch (start us, length us, event | category | flops | bytes accessed | tf_op | source)
XLA Modules:
  0.0 36.8 jit_solution(16766621547270467174)
XLA Ops:
  0.6 0.1 collective-permute-start
  0.7 0.0 copy-start.11
  0.7 2.8 %teacher_own.1 = (bf16[320,512]{1,0:T(8,128)(2,1)S(1)}, bf16[320,128]{1,0:T(8,128)(2,1)S(1)}, bf16[320,128]{1,0:T(8,128)(2,1)S(1)}, bf16[320,512]{1,0:T(8,128)(2...) custom-call(bf16[1,12,24,512]{3,2,1,0:T(8,128)(2,1)} %bitcast.7, ...), custom_call_target="tpu_custom_call" | custom-call | flops 1000000000 | bytes 3711744 | tf_op jit(solution)/shard_map/teacher_own/pallas_call | solution.py:577
  3.6 0.0 copy-start
  3.6 0.0 copy-start.6
  3.6 0.0 copy-start.7
  3.6 0.0 copy-start.9
  3.6 0.0 copy-start.13
  3.7 3.7 %teacher_first.1 = (bf16[320,512]{1,0:T(8,128)(2,1)S(1)}, bf16[80,512]{1,0:T(8,128)(2,1)S(1)}, bf16[80,512]{1,0:T(8,128)(2,1)S(1)}) custom-call(bf16[1,12,24,512]{3,2,1,0:T(8,128)(2,1)S(1)} %collective-permute-done.far_ref, bf16[320,512]{1,0:T(8,128)(2,1)S(1)} %get-tuple-element.31.x_ref, bf16[320,128]{1,0:T(8,128)(2,1)S(1)} %get-tuple-element.32.id_ref, ...), custom_call_target="tpu_custom_call" | custom-call | flops 3000000000 | bytes 4800512 | tf_op jit(solution)/shard_map/teacher_first/pallas_call | solution.py:577
  7.3 7.2 %collective-permute-start.1 = (bf16[80,512]{1,0:T(8,128)(2,1)S(1)}, bf16[80,512]{1,0:T(8,128)(2,1)S(1)}, u32[]{:S(2)}, u32[]{:S(2)}) collective-permute-start(bf16[80,512]{1,0:T(8,128)(2,1)S(1)} %get-tuple-element.42), channel_id=1, source_target_pairs={{0,2},{2,0},{4,6},{6,4},{8,10},{10,8},{12,14},{14,12},{16,18},{18,... | collective-permute-start | bytes 245768 | tf_op jit(solution)/shard_map/ppermute | solution.py:648
  14.6 0.0 copy-start.1
  14.6 0.0 copy-start.2
  14.6 0.0 copy-start.14
  14.6 4.0 %beside_rows.1 = (bf16[400,640]{1,0:T(8,128)(2,1)S(1)}, f32[320,256]{1,0:T(8,128)S(1)}, bf16[320,2816]{1,0:T(8,128)(2,1)S(1)}, bf16[320,2816]{1,0:T(8,128)(2,1)S...) custom-call(bf16[1,12,24,256]{3,2,1,0:T(8,128)(2,1)S(1)} %bitcast.5,, ...), custom_call_target="tpu_custom_call" | custom-call | flops 5000000000 | bytes 5625856 | tf_op jit(solution)/shard_map/beside_rows/pallas_call | solution.py:577
  18.6 0.5 %collective-permute-done.2.second_ref = bf16[80,512]{1,0:T(8,128)(2,1)S(1)} collective-permute-done((bf16[80,512]{1,0:T(8,128)(2,1)S(1)}, bf16[80,512]{1,0:T(8,128)(2,1)S(1)}, u32[]{:S(2)}, u32[]{:S(2)}) %collective-permute-start.2) | collective-permute-done | bytes 81952 | tf_op jit(solution)/shard_map/ppermute | solution.py:647
  19.1 0.3 send_columns.1
  19.4 6.4 %collective-permute-start.3 = (bf16[112,512]{1,0:T(8,128)(2,1)S(1)}, bf16[112,512]{1,0:T(8,128)(2,1)S(1)}, u32[]{:S(2)}, u32[]{:S(2)}) collective-permute-start(bf16[112,512]{1,0:T(8,128)(2,1)S(1)} %get-tuple-element.46), channel_id=1, source_target_pairs={{0,30},{2,4},{4,2},{6,8},{8,6},{10,12},{12,10},{14,16},{16,14},{18... | collective-permute-start | bytes 344072 | tf_op jit(solution)/shard_map/ppermute | solution.py:666
  25.8 0.0 copy-start.8
  25.8 0.0 copy-start.10
  25.8 0.0 copy-start.12
  25.8 1.8 %beside_columns.1 = (bf16[48,512]{1,0:T(8,128)(2,1)S(1)}, bf16[48,512]{1,0:T(8,128)(2,1)S(1)}, f32[224,512]{1,0:T(8,128)S(1)}, f32[224,512]{1,0:T(8,128)S(1)}) custom-call(bf16[400,640]{1,0:T(8,128)(2,1)S(1)} %get-tuple-element.41.g_ref, bf16[80,512]{1,0:T(8,128)(2,1)S(1)} %collective-permute-done.1.first_ref, ...), custom_call_target="tpu_custom_call" | custom-call | flops 2000000000 | bytes 5182976 | tf_op jit(solution)/shard_map/beside_columns/pallas_call | solution.py:577
  27.6 1.2 %collective-permute-done.3.first_ref = bf16[112,512]{1,0:T(8,128)(2,1)S(1)} collective-permute-done((bf16[112,512]{1,0:T(8,128)(2,1)S(1)}, bf16[112,512]{1,0:T(8,128)(2,1)S(1)}, u32[]{:S(2)}, u32[]{:S(2)}) %collective-permute-start.3) | collective-permute-done | bytes 114720 | tf_op jit(solution)/shard_map/ppermute | solution.py:666
  28.7 1.8 %collective-permute-done.4.second_ref = bf16[112,512]{1,0:T(8,128)(2,1)S(1)} collective-permute-done((bf16[112,512]{1,0:T(8,128)(2,1)S(1)}, bf16[112,512]{1,0:T(8,128)(2,1)S(1)}, u32[]{:S(2)}, u32[]{:S(2)}) %collective-permute-start.4) | collective-permute-done | bytes 114720 | tf_op jit(solution)/shard_map/ppermute | solution.py:665
  30.6 6.0 %teacher_second.1 = (bf16[1,12,24,512]{3,2,1,0:T(8,128)(2,1)}, f32[1,12,24,256]{3,2,1,0:T(8,128)}) custom-call(bf16[320,512]{1,0:T(8,128)(2,1)S(1)} %get-tuple-element.39.hidden_ref.h_ref, bf16[400,640]{1,0:T(8,128)(2,1)S(1)} %get-tuple-element.41.g_ref, bf16[112,512]{1,0:T(8,128)(2,1)S(1)} %collective-permute-done.3.first_ref, ...), custom_call_target="tpu_custom_call" | custom-call | flops 6000000000 | bytes 12554752 | tf_op jit(solution)/shard_map/teacher_second/pallas_call | solution.py:577
  (22 shorter events, 0.1 us)
Async XLA Ops:
  0.6 2.9 %collective-permute-start = (bf16[1,12,24,512]{3,2,1,0:T(8,128)(2,1)}, bf16[1,12,24,512]{3,2,1,0:T(8,128)(2,1)S(1)}, u32[]{:S(2)}, u32[]{:S(2)}) collective-permute-start(bf16[1,12,24,512]{3,2,1,0:T(8,128)(2,1)} %bitcast.6), channel_id=1, source_target_pairs={{0,1},{1,0},{2,3},{3,2},{4,5},{5,4},{6,7},{7,6},{8,9},{9,8},{10,11... | collective-permute-start | bytes 884744 | tf_op jit(solution)/shard_map/ppermute | solution.py:622
  0.7 2.8 %copy-start.11 = (bf16[256,320]{1,0:T(8,128)(2,1)S(1)}, bf16[256,320]{1,0:T(8,128)(2,1)}, u32[]{:S(2)}) copy-start(bf16[256,320]{1,0:T(8,128)(2,1)} %constant.27.clone.rows_from_a) | copy-start | bytes 491524
  3.6 10.9 %copy-start = (bf16[2,512,1536]{2,1,0:T(8,128)(2,1)S(1)}, bf16[2,512,1536]{2,1,0:T(8,128)(2,1)}, u32[]{:S(2)}) copy-start(bf16[2,512,1536]{2,1,0:T(8,128)(2,1)} %t_qkv.7) | copy-start | bytes 9437188
  3.6 10.9 %copy-start.4 = (bf16[2,256,768]{2,1,0:T(8,128)(2,1)S(1)}, bf16[2,256,768]{2,1,0:T(8,128)(2,1)}, u32[]{:S(2)}) copy-start(bf16[2,256,768]{2,1,0:T(8,128)(2,1)} %s_qkv.3) | copy-start | bytes 2359300
  3.6 10.9 %copy-start.5 = (bf16[2,256,256]{2,1,0:T(8,128)(2,1)S(1)}, bf16[2,256,256]{2,1,0:T(8,128)(2,1)}, u32[]{:S(2)}) copy-start(bf16[2,256,256]{2,1,0:T(8,128)(2,1)} %s_out.3) | copy-start | bytes 786436
  3.6 10.9 %copy-start.6 = (bf16[256,512]{1,0:T(8,128)(2,1)S(1)}, bf16[256,512]{1,0:T(8,128)(2,1)}, u32[]{:S(2)}) copy-start(bf16[256,512]{1,0:T(8,128)(2,1)} %proj.3) | copy-start | bytes 786436
  3.6 10.9 %copy-start.7 = (bf16[1,24,12,256]{3,1,2,0:T(8,128)(2,1)S(1)}, bf16[1,24,12,256]{3,1,2,0:T(8,128)(2,1)}, u32[]{:S(2)}) copy-start(bf16[1,24,12,256]{3,1,2,0:T(8,128)(2,1)} %param.21) | copy-start | bytes 442372
  3.6 10.9 %copy-start.9 = (bf16[400,320]{1,0:T(8,128)(2,1)S(1)}, bf16[400,320]{1,0:T(8,128)(2,1)}, u32[]{:S(2)}) copy-start(bf16[400,320]{1,0:T(8,128)(2,1)} %constant.28.clone.a_to_g) | copy-start | bytes 768004
  3.6 10.9 %copy-start.13 = (bf16[128,112]{1,0:T(8,128)(2,1)S(1)}, bf16[128,112]{1,0:T(8,128)(2,1)}, u32[]{:S(2)}) copy-start(bf16[128,112]{1,0:T(8,128)(2,1)} %constant.29.clone.pack) | copy-start | bytes 86020
  7.3 11.3 %collective-permute-start.1 = (bf16[80,512]{1,0:T(8,128)(2,1)S(1)}, bf16[80,512]{1,0:T(8,128)(2,1)S(1)}, u32[]{:S(2)}, u32[]{:S(2)}) collective-permute-start(bf16[80,512]{1,0:T(8,128)(2,1)S(1)} %get-tuple-element.42), channel_id=1, source_target_pairs={{0,2},{2,0},{4,6},{6,4},{8,10},{10,8},{12,14},{14,12},{16,18},{18,... | collective-permute-start | bytes 245768 | tf_op jit(solution)/shard_map/ppermute | solution.py:648
  14.5 4.6 %collective-permute-start.2 = (bf16[80,512]{1,0:T(8,128)(2,1)S(1)}, bf16[80,512]{1,0:T(8,128)(2,1)S(1)}, u32[]{:S(2)}, u32[]{:S(2)}) collective-permute-start(bf16[80,512]{1,0:T(8,128)(2,1)S(1)} %get-tuple-element.40.after_ref), channel_id=1, source_target_pairs={{0,32},{32,0},{64,96},{96,64},{128,160},{160,128},{192,224},{224,1... | collective-permute-start | bytes 245768 | tf_op jit(solution)/shard_map/ppermute | solution.py:647
  14.6 4.5 %copy-start.1 = (bf16[256,80]{1,0:T(8,128)(2,1)S(1)}, bf16[256,80]{1,0:T(8,128)(2,1)}, u32[]{:S(2)}) copy-start(bf16[256,80]{1,0:T(8,128)(2,1)} %constant.31.clone.from_south) | copy-start | bytes 122884
  14.6 4.5 %copy-start.2 = (bf16[256,80]{1,0:T(8,128)(2,1)S(1)}, bf16[256,80]{1,0:T(8,128)(2,1)}, u32[]{:S(2)}) copy-start(bf16[256,80]{1,0:T(8,128)(2,1)} %constant.30.clone.from_north) | copy-start | bytes 122884
  14.6 11.2 %copy-start.14 = (bf16[112,80]{1,0:T(8,128)(2,1)S(1)}, bf16[112,80]{1,0:T(8,128)(2,1)}, u32[]{:S(2)}) copy-start(bf16[112,80]{1,0:T(8,128)(2,1)} %constant.32.clone.open_rows) | copy-start | bytes 53764
  19.4 9.4 %collective-permute-start.3 = (bf16[112,512]{1,0:T(8,128)(2,1)S(1)}, bf16[112,512]{1,0:T(8,128)(2,1)S(1)}, u32[]{:S(2)}, u32[]{:S(2)}) collective-permute-start(bf16[112,512]{1,0:T(8,128)(2,1)S(1)} %get-tuple-element.46), channel_id=1, source_target_pairs={{0,30},{2,4},{4,2},{6,8},{8,6},{10,12},{12,10},{14,16},{16,14},{18... | collective-permute-start | bytes 344072 | tf_op jit(solution)/shard_map/ppermute | solution.py:666
  25.7 4.8 %collective-permute-start.4 = (bf16[112,512]{1,0:T(8,128)(2,1)S(1)}, bf16[112,512]{1,0:T(8,128)(2,1)S(1)}, u32[]{:S(2)}, u32[]{:S(2)}) collective-permute-start(bf16[112,512]{1,0:T(8,128)(2,1)S(1)} %get-tuple-element.47.after_ref), channel_id=1, source_target_pairs={{0,2},{2,0},{4,6},{6,4},{8,10},{10,8},{12,14},{14,12},{16,18},{18,... | collective-permute-start | bytes 344072 | tf_op jit(solution)/shard_map/ppermute | solution.py:665
  25.7 4.8 %copy-start.3 = (bf16[2,512,512]{2,1,0:T(8,128)(2,1)S(1)}, bf16[2,512,512]{2,1,0:T(8,128)(2,1)}, u32[]{:S(2)}) copy-start(bf16[2,512,512]{2,1,0:T(8,128)(2,1)} %t_out.3) | copy-start | bytes 3145732
  25.8 4.8 %copy-start.8 = (bf16[320,400]{1,0:T(8,128)(2,1)S(1)}, bf16[320,400]{1,0:T(8,128)(2,1)}, u32[]{:S(2)}) copy-start(bf16[320,400]{1,0:T(8,128)(2,1)} %constant.35.clone.g_to_a) | copy-start | bytes 768004
  25.8 4.8 %copy-start.10 = (bf16[384,320]{1,0:T(8,128)(2,1)S(1)}, bf16[384,320]{1,0:T(8,128)(2,1)}, u32[]{:S(2)}) copy-start(bf16[384,320]{1,0:T(8,128)(2,1)} %constant.34.clone.from_a) | copy-start | bytes 737284
  25.8 4.8 %copy-start.12 = (bf16[176,112]{1,0:T(8,128)(2,1)S(1)}, bf16[176,112]{1,0:T(8,128)(2,1)}, u32[]{:S(2)}) copy-start(bf16[176,112]{1,0:T(8,128)(2,1)} %constant.33.clone.open_cols) | copy-start | bytes 118276

commit v12 on v11

--- a/solution.py
+++ b/solution.py
@@ -360,9 +360,13 @@
 
 def opened(sent, table, tokens):
     values = dot(table, sent).astype(BF)
+    return jnp.concatenate([values, opened_ids(sent, table, tokens)], axis=1)
+
+
+def opened_ids(sent, table, tokens):
     row = sent.astype(F32)[tokens : tokens + 1, : table.shape[1]]
-    ids = dot((table.astype(F32) * row).astype(BF), jnp.ones((table.shape[1], 128), BF))
-    return jnp.concatenate([values, ids.astype(BF)], axis=1)
+    picked = (table.astype(F32) * row).astype(BF)
+    return dot(picked, jnp.ones((table.shape[1], 128), BF)).astype(BF)
 
 
 def part(x, name):
@@ -526,17 +530,21 @@
     width = h_ref.shape[1]
     blocks = head_blocks()
     west, east = swapped("lon", first_ref[...], second_ref[...])
-    came = [opened(sent, open_cols[...], COL_TOKENS) for sent in (east, west)]
-    came = jnp.concatenate(came, axis=0)
-    rows = came[:, :width]
+    table = open_cols[...]
+    ids_came = jnp.concatenate([opened_ids(x, table, COL_TOKENS) for x in (east, west)], axis=0)
+    rows = jnp.concatenate([east, west], axis=0)
     k = unit(dot(rows, t_qkv[1, :, width : 2 * width]), blocks)[0].astype(BF)
     v = dot(rows, t_qkv[1, :, 2 * width :]).astype(BF)
+    k, v = [
+        jnp.concatenate([dot(table, x[:COL_SENT]), dot(table, x[COL_SENT:])], axis=0).astype(BF)
+        for x in (k, v)
+    ]
     atts = {"c": c_ref[...], "n": n_ref[...], "s": s_ref[...]}
     windows = []
     for name in LATE:
         items = [item for item in EXTRA[name] if item in COME]
         keys = [gather([(new, COME)], items) for new in (k, v)]
-        ids = (part(g_ref, name)[:, width:], gather([(came, COME)], items)[:, width:])
+        ids = (part(g_ref, name)[:, width:], gather([(ids_came, COME)], items))
         windows.append((part(q_ref, name), keys, ids))
     start = 0
     for name, (num, den) in zip(LATE, window_sums(windows)):

time: 36.9 us -> 36.8 us (level)
  no operation moved by 1% of the time
where the time goes in v12:
time: 36.8 us; the launch traced here: 36.7 us
  Pallas kernels  18.5 us (50%)
  starting transfers between devices  13.6 us (37%)
  waiting for transfers between devices  3.46 us (9%)
  between operations  1.03 us (3%)
    pallas_call x6, Pallas kernels, call(): pl.pallas_call(kernel, name=name, out_shape=shapes, in_specs=specs, out_s...  18.5 us
    ppermute x1, starting transfers between devices, shards(): lax.ppermute(rows_1, ('lat', 'lon'), inner_swaps(lat_size, lon_size))  7.18 us
    ppermute x1, starting transfers between devices, shards(): cols_1 = lax.ppermute(cols_1, 'lon', swaps(lon_size, 1))  6.36 us
    ppermute x1, waiting for transfers between devices, shards(): cols_2 = lax.ppermute(cols_2, 'lon', swaps(lon_size, 0))  1.79 us
    ppermute x1, waiting for transfers between devices, shards(): cols_1 = lax.ppermute(cols_1, 'lon', swaps(lon_size, 1))  1.19 us
  transfers between devices with their start and end apart: 5, of which 3 were waited for; matrix products, arithmetic and copies ran while one was open for 0% of the time, Pallas kernels for 23%

profile of v12, /device:TPU:6, one launch (start us, length us, event | category | flops | bytes accessed | tf_op | source)
XLA Modules:
  0.0 36.7 jit_solution(9820372389521363380)
XLA Ops:
  0.6 0.1 collective-permute-start
  0.7 0.0 copy-start.11
  0.7 2.8 %teacher_own.1 = (bf16[320,512]{1,0:T(8,128)(2,1)S(1)}, bf16[320,128]{1,0:T(8,128)(2,1)S(1)}, bf16[320,128]{1,0:T(8,128)(2,1)S(1)}, bf16[320,512]{1,0:T(8,128)(2...) custom-call(bf16[1,12,24,512]{3,2,1,0:T(8,128)(2,1)} %bitcast.7, ...), custom_call_target="tpu_custom_call" | custom-call | flops 1000000000 | bytes 3711744 | tf_op jit(solution)/shard_map/teacher_own/pallas_call | solution.py:585
  3.6 0.0 copy-start
  3.6 0.0 copy-start.6
  3.6 0.0 copy-start.7
  3.6 0.0 copy-start.9
  3.6 0.0 copy-start.13
  3.7 3.7 %teacher_first.1 = (bf16[320,512]{1,0:T(8,128)(2,1)S(1)}, bf16[80,512]{1,0:T(8,128)(2,1)S(1)}, bf16[80,512]{1,0:T(8,128)(2,1)S(1)}) custom-call(bf16[1,12,24,512]{3,2,1,0:T(8,128)(2,1)S(1)} %collective-permute-done.far_ref, bf16[320,512]{1,0:T(8,128)(2,1)S(1)} %get-tuple-element.31.x_ref, bf16[320,128]{1,0:T(8,128)(2,1)S(1)} %get-tuple-element.32.id_ref, ...), custom_call_target="tpu_custom_call" | custom-call | flops 3000000000 | bytes 4800512 | tf_op jit(solution)/shard_map/teacher_first/pallas_call | solution.py:585
  7.3 7.2 %collective-permute-start.1 = (bf16[80,512]{1,0:T(8,128)(2,1)S(1)}, bf16[80,512]{1,0:T(8,128)(2,1)S(1)}, u32[]{:S(2)}, u32[]{:S(2)}) collective-permute-start(bf16[80,512]{1,0:T(8,128)(2,1)S(1)} %get-tuple-element.42), channel_id=1, source_target_pairs={{0,2},{2,0},{4,6},{6,4},{8,10},{10,8},{12,14},{14,12},{16,18},{18,... | collective-permute-start | bytes 245768 | tf_op jit(solution)/shard_map/ppermute | solution.py:656
  14.6 0.0 copy-start.1
  14.6 0.0 copy-start.2
  14.6 0.0 copy-start.14
  14.6 4.0 %beside_rows.1 = (bf16[400,640]{1,0:T(8,128)(2,1)S(1)}, f32[320,256]{1,0:T(8,128)S(1)}, bf16[320,2816]{1,0:T(8,128)(2,1)S(1)}, bf16[320,2816]{1,0:T(8,128)(2,1)S...) custom-call(bf16[1,12,24,256]{3,2,1,0:T(8,128)(2,1)S(1)} %bitcast.5,, ...), custom_call_target="tpu_custom_call" | custom-call | flops 5000000000 | bytes 5625856 | tf_op jit(solution)/shard_map/beside_rows/pallas_call | solution.py:585
  18.6 0.5 %collective-permute-done.2.second_ref = bf16[80,512]{1,0:T(8,128)(2,1)S(1)} collective-permute-done((bf16[80,512]{1,0:T(8,128)(2,1)S(1)}, bf16[80,512]{1,0:T(8,128)(2,1)S(1)}, u32[]{:S(2)}, u32[]{:S(2)}) %collective-permute-start.2) | collective-permute-done | bytes 81952 | tf_op jit(solution)/shard_map/ppermute | solution.py:655
  19.1 0.3 send_columns.1
  19.4 6.4 %collective-permute-start.3 = (bf16[112,512]{1,0:T(8,128)(2,1)S(1)}, bf16[112,512]{1,0:T(8,128)(2,1)S(1)}, u32[]{:S(2)}, u32[]{:S(2)}) collective-permute-start(bf16[112,512]{1,0:T(8,128)(2,1)S(1)} %get-tuple-element.46), channel_id=1, source_target_pairs={{0,30},{2,4},{4,2},{6,8},{8,6},{10,12},{12,10},{14,16},{16,14},{18... | collective-permute-start | bytes 344072 | tf_op jit(solution)/shard_map/ppermute | solution.py:674
  25.8 0.0 copy-start.8
  25.8 0.0 copy-start.10
  25.8 0.0 copy-start.12
  25.8 1.8 %beside_columns.1 = (bf16[48,512]{1,0:T(8,128)(2,1)S(1)}, bf16[48,512]{1,0:T(8,128)(2,1)S(1)}, f32[224,512]{1,0:T(8,128)S(1)}, f32[224,512]{1,0:T(8,128)S(1)}) custom-call(bf16[400,640]{1,0:T(8,128)(2,1)S(1)} %get-tuple-element.41.g_ref, bf16[80,512]{1,0:T(8,128)(2,1)S(1)} %collective-permute-done.1.first_ref, ...), custom_call_target="tpu_custom_call" | custom-call | flops 2000000000 | bytes 5182976 | tf_op jit(solution)/shard_map/beside_columns/pallas_call | solution.py:585
  27.6 1.2 %collective-permute-done.3.first_ref = bf16[112,512]{1,0:T(8,128)(2,1)S(1)} collective-permute-done((bf16[112,512]{1,0:T(8,128)(2,1)S(1)}, bf16[112,512]{1,0:T(8,128)(2,1)S(1)}, u32[]{:S(2)}, u32[]{:S(2)}) %collective-permute-start.3) | collective-permute-done | bytes 114720 | tf_op jit(solution)/shard_map/ppermute | solution.py:674
  28.7 1.8 %collective-permute-done.4.second_ref = bf16[112,512]{1,0:T(8,128)(2,1)S(1)} collective-permute-done((bf16[112,512]{1,0:T(8,128)(2,1)S(1)}, bf16[112,512]{1,0:T(8,128)(2,1)S(1)}, u32[]{:S(2)}, u32[]{:S(2)}) %collective-permute-start.4) | collective-permute-done | bytes 114720 | tf_op jit(solution)/shard_map/ppermute | solution.py:673
  30.6 6.0 %teacher_second.1 = (bf16[1,12,24,512]{3,2,1,0:T(8,128)(2,1)}, f32[1,12,24,256]{3,2,1,0:T(8,128)}) custom-call(bf16[320,512]{1,0:T(8,128)(2,1)S(1)} %get-tuple-element.39.hidden_ref.h_ref, bf16[400,640]{1,0:T(8,128)(2,1)S(1)} %get-tuple-element.41.g_ref, bf16[112,512]{1,0:T(8,128)(2,1)S(1)} %collective-permute-done.3.first_ref, ...), custom_call_target="tpu_custom_call" | custom-call | flops 6000000000 | bytes 12554752 | tf_op jit(solution)/shard_map/teacher_second/pallas_call | solution.py:585
  (22 shorter events, 0.1 us)
Async XLA Ops:
  0.6 2.9 %collective-permute-start = (bf16[1,12,24,512]{3,2,1,0:T(8,128)(2,1)}, bf16[1,12,24,512]{3,2,1,0:T(8,128)(2,1)S(1)}, u32[]{:S(2)}, u32[]{:S(2)}) collective-permute-start(bf16[1,12,24,512]{3,2,1,0:T(8,128)(2,1)} %bitcast.6), channel_id=1, source_target_pairs={{0,1},{1,0},{2,3},{3,2},{4,5},{5,4},{6,7},{7,6},{8,9},{9,8},{10,11... | collective-permute-start | bytes 884744 | tf_op jit(solution)/shard_map/ppermute | solution.py:630
  0.7 2.8 %copy-start.11 = (bf16[256,320]{1,0:T(8,128)(2,1)S(1)}, bf16[256,320]{1,0:T(8,128)(2,1)}, u32[]{:S(2)}) copy-start(bf16[256,320]{1,0:T(8,128)(2,1)} %constant.27.clone.rows_from_a) | copy-start | bytes 491524
  3.6 10.9 %copy-start = (bf16[2,512,1536]{2,1,0:T(8,128)(2,1)S(1)}, bf16[2,512,1536]{2,1,0:T(8,128)(2,1)}, u32[]{:S(2)}) copy-start(bf16[2,512,1536]{2,1,0:T(8,128)(2,1)} %t_qkv.7) | copy-start | bytes 9437188
  3.6 10.9 %copy-start.4 = (bf16[2,256,768]{2,1,0:T(8,128)(2,1)S(1)}, bf16[2,256,768]{2,1,0:T(8,128)(2,1)}, u32[]{:S(2)}) copy-start(bf16[2,256,768]{2,1,0:T(8,128)(2,1)} %s_qkv.3) | copy-start | bytes 2359300
  3.6 10.9 %copy-start.5 = (bf16[2,256,256]{2,1,0:T(8,128)(2,1)S(1)}, bf16[2,256,256]{2,1,0:T(8,128)(2,1)}, u32[]{:S(2)}) copy-start(bf16[2,256,256]{2,1,0:T(8,128)(2,1)} %s_out.3) | copy-start | bytes 786436
  3.6 10.9 %copy-start.6 = (bf16[256,512]{1,0:T(8,128)(2,1)S(1)}, bf16[256,512]{1,0:T(8,128)(2,1)}, u32[]{:S(2)}) copy-start(bf16[256,512]{1,0:T(8,128)(2,1)} %proj.3) | copy-start | bytes 786436
  3.6 10.9 %copy-start.7 = (bf16[1,24,12,256]{3,1,2,0:T(8,128)(2,1)S(1)}, bf16[1,24,12,256]{3,1,2,0:T(8,128)(2,1)}, u32[]{:S(2)}) copy-start(bf16[1,24,12,256]{3,1,2,0:T(8,128)(2,1)} %param.21) | copy-start | bytes 442372
  3.6 10.9 %copy-start.9 = (bf16[400,320]{1,0:T(8,128)(2,1)S(1)}, bf16[400,320]{1,0:T(8,128)(2,1)}, u32[]{:S(2)}) copy-start(bf16[400,320]{1,0:T(8,128)(2,1)} %constant.28.clone.a_to_g) | copy-start | bytes 768004
  3.6 10.9 %copy-start.13 = (bf16[128,112]{1,0:T(8,128)(2,1)S(1)}, bf16[128,112]{1,0:T(8,128)(2,1)}, u32[]{:S(2)}) copy-start(bf16[128,112]{1,0:T(8,128)(2,1)} %constant.29.clone.pack) | copy-start | bytes 86020
  7.3 11.3 %collective-permute-start.1 = (bf16[80,512]{1,0:T(8,128)(2,1)S(1)}, bf16[80,512]{1,0:T(8,128)(2,1)S(1)}, u32[]{:S(2)}, u32[]{:S(2)}) collective-permute-start(bf16[80,512]{1,0:T(8,128)(2,1)S(1)} %get-tuple-element.42), channel_id=1, source_target_pairs={{0,2},{2,0},{4,6},{6,4},{8,10},{10,8},{12,14},{14,12},{16,18},{18,... | collective-permute-start | bytes 245768 | tf_op jit(solution)/shard_map/ppermute | solution.py:656
  14.5 4.6 %collective-permute-start.2 = (bf16[80,512]{1,0:T(8,128)(2,1)S(1)}, bf16[80,512]{1,0:T(8,128)(2,1)S(1)}, u32[]{:S(2)}, u32[]{:S(2)}) collective-permute-start(bf16[80,512]{1,0:T(8,128)(2,1)S(1)} %get-tuple-element.40.after_ref), channel_id=1, source_target_pairs={{0,32},{32,0},{64,96},{96,64},{128,160},{160,128},{192,224},{224,1... | collective-permute-start | bytes 245768 | tf_op jit(solution)/shard_map/ppermute | solution.py:655
  14.6 4.5 %copy-start.1 = (bf16[256,80]{1,0:T(8,128)(2,1)S(1)}, bf16[256,80]{1,0:T(8,128)(2,1)}, u32[]{:S(2)}) copy-start(bf16[256,80]{1,0:T(8,128)(2,1)} %constant.31.clone.from_south) | copy-start | bytes 122884
  14.6 4.5 %copy-start.2 = (bf16[256,80]{1,0:T(8,128)(2,1)S(1)}, bf16[256,80]{1,0:T(8,128)(2,1)}, u32[]{:S(2)}) copy-start(bf16[256,80]{1,0:T(8,128)(2,1)} %constant.30.clone.from_north) | copy-start | bytes 122884
  14.6 11.2 %copy-start.14 = (bf16[112,80]{1,0:T(8,128)(2,1)S(1)}, bf16[112,80]{1,0:T(8,128)(2,1)}, u32[]{:S(2)}) copy-start(bf16[112,80]{1,0:T(8,128)(2,1)} %constant.32.clone.open_rows) | copy-start | bytes 53764
  19.4 9.4 %collective-permute-start.3 = (bf16[112,512]{1,0:T(8,128)(2,1)S(1)}, bf16[112,512]{1,0:T(8,128)(2,1)S(1)}, u32[]{:S(2)}, u32[]{:S(2)}) collective-permute-start(bf16[112,512]{1,0:T(8,128)(2,1)S(1)} %get-tuple-element.46), channel_id=1, source_target_pairs={{0,30},{2,4},{4,2},{6,8},{8,6},{10,12},{12,10},{14,16},{16,14},{18... | collective-permute-start | bytes 344072 | tf_op jit(solution)/shard_map/ppermute | solution.py:674
  25.7 4.8 %collective-permute-start.4 = (bf16[112,512]{1,0:T(8,128)(2,1)S(1)}, bf16[112,512]{1,0:T(8,128)(2,1)S(1)}, u32[]{:S(2)}, u32[]{:S(2)}) collective-permute-start(bf16[112,512]{1,0:T(8,128)(2,1)S(1)} %get-tuple-element.47.after_ref), channel_id=1, source_target_pairs={{0,2},{2,0},{4,6},{6,4},{8,10},{10,8},{12,14},{14,12},{16,18},{18,... | collective-permute-start | bytes 344072 | tf_op jit(solution)/shard_map/ppermute | solution.py:673
  25.7 4.8 %copy-start.3 = (bf16[2,512,512]{2,1,0:T(8,128)(2,1)S(1)}, bf16[2,512,512]{2,1,0:T(8,128)(2,1)}, u32[]{:S(2)}) copy-start(bf16[2,512,512]{2,1,0:T(8,128)(2,1)} %t_out.3) | copy-start | bytes 3145732
  25.8 4.8 %copy-start.8 = (bf16[320,400]{1,0:T(8,128)(2,1)S(1)}, bf16[320,400]{1,0:T(8,128)(2,1)}, u32[]{:S(2)}) copy-start(bf16[320,400]{1,0:T(8,128)(2,1)} %constant.35.clone.g_to_a) | copy-start | bytes 768004
  25.8 4.8 %copy-start.10 = (bf16[384,320]{1,0:T(8,128)(2,1)S(1)}, bf16[384,320]{1,0:T(8,128)(2,1)}, u32[]{:S(2)}) copy-start(bf16[384,320]{1,0:T(8,128)(2,1)} %constant.34.clone.from_a) | copy-start | bytes 737284
  25.8 4.8 %copy-start.12 = (bf16[176,112]{1,0:T(8,128)(2,1)S(1)}, bf16[176,112]{1,0:T(8,128)(2,1)}, u32[]{:S(2)}) copy-start(bf16[176,112]{1,0:T(8,128)(2,1)} %constant.33.clone.open_cols) | copy-start | bytes 118276

commit v13 on v12

--- a/solution.py
+++ b/solution.py
@@ -556,10 +556,10 @@
     teacher = residual(h_ref[...], att, t_out[1])[0]
     natural = dot(from_a[...], teacher).astype(BF)
     out_ref[0] = natural.reshape(COLS, TALL, width)[:, :ROWS, :]
-    copies = fetch((out_ref, out_hbm, sems.at[0]))
 
     g = g0_ref[...] - dot_nt(teacher, proj[...])
     g = student_back(g, save1, s_qkv[1], s_out[1])
+    copies = fetch((out_ref, out_hbm, sems.at[0]))
     g = student_back(g, save0, s_qkv[0], s_out[0])
     high = g.astype(BF)
     low = (g - high.astype(F32)).astype(BF)

time: 36.8 us -> 36.8 us (level)
  no operation moved by 1% of the time
where the time goes in v13:
time: 36.8 us; the launch traced here: 36.7 us
  Pallas kernels  18.5 us (50%)
  starting transfers between devices  13.6 us (37%)
  waiting for transfers between devices  3.46 us (9%)
  between operations  1.03 us (3%)
    pallas_call x6, Pallas kernels, call(): pl.pallas_call(kernel, name=name, out_shape=shapes, in_specs=specs, out_s...  18.5 us
    ppermute x1, starting transfers between devices, shards(): lax.ppermute(rows_1, ('lat', 'lon'), inner_swaps(lat_size, lon_size))  7.18 us
    ppermute x1, starting transfers between devices, shards(): cols_1 = lax.ppermute(cols_1, 'lon', swaps(lon_size, 1))  6.36 us
    ppermute x1, waiting for transfers between devices, shards(): cols_2 = lax.ppermute(cols_2, 'lon', swaps(lon_size, 0))  1.79 us
    ppermute x1, waiting for transfers between devices, shards(): cols_1 = lax.ppermute(cols_1, 'lon', swaps(lon_size, 1))  1.19 us
  transfers between devices with their start and end apart: 5, of which 3 were waited for; matrix products, arithmetic and copies ran while one was open for 0% of the time, Pallas kernels for 23%

profile of v13, /device:TPU:6, one launch (start us, length us, event | category | flops | bytes accessed | tf_op | source)
XLA Modules:
  0.0 36.7 jit_solution(9820372389521363380)
XLA Ops:
  0.6 0.1 collective-permute-start
  0.7 0.0 copy-start.11
  0.7 2.8 %teacher_own.1 = (bf16[320,512]{1,0:T(8,128)(2,1)S(1)}, bf16[320,128]{1,0:T(8,128)(2,1)S(1)}, bf16[320,128]{1,0:T(8,128)(2,1)S(1)}, bf16[320,512]{1,0:T(8,128)(2...) custom-call(bf16[1,12,24,512]{3,2,1,0:T(8,128)(2,1)} %bitcast.7, ...), custom_call_target="tpu_custom_call" | custom-call | flops 1000000000 | bytes 3711744 | tf_op jit(solution)/shard_map/teacher_own/pallas_call | solution.py:585
  3.6 0.0 copy-start
  3.6 0.0 copy-start.6
  3.6 0.0 copy-start.7
  3.6 0.0 copy-start.9
  3.6 0.0 copy-start.13
  3.7 3.7 %teacher_first.1 = (bf16[320,512]{1,0:T(8,128)(2,1)S(1)}, bf16[80,512]{1,0:T(8,128)(2,1)S(1)}, bf16[80,512]{1,0:T(8,128)(2,1)S(1)}) custom-call(bf16[1,12,24,512]{3,2,1,0:T(8,128)(2,1)S(1)} %collective-permute-done.far_ref, bf16[320,512]{1,0:T(8,128)(2,1)S(1)} %get-tuple-element.31.x_ref, bf16[320,128]{1,0:T(8,128)(2,1)S(1)} %get-tuple-element.32.id_ref, ...), custom_call_target="tpu_custom_call" | custom-call | flops 3000000000 | bytes 4800512 | tf_op jit(solution)/shard_map/teacher_first/pallas_call | solution.py:585
  7.3 7.2 %collective-permute-start.1 = (bf16[80,512]{1,0:T(8,128)(2,1)S(1)}, bf16[80,512]{1,0:T(8,128)(2,1)S(1)}, u32[]{:S(2)}, u32[]{:S(2)}) collective-permute-start(bf16[80,512]{1,0:T(8,128)(2,1)S(1)} %get-tuple-element.42), channel_id=1, source_target_pairs={{0,2},{2,0},{4,6},{6,4},{8,10},{10,8},{12,14},{14,12},{16,18},{18,... | collective-permute-start | bytes 245768 | tf_op jit(solution)/shard_map/ppermute | solution.py:656
  14.6 0.0 copy-start.1
  14.6 0.0 copy-start.2
  14.6 0.0 copy-start.14
  14.6 4.0 %beside_rows.1 = (bf16[400,640]{1,0:T(8,128)(2,1)S(1)}, f32[320,256]{1,0:T(8,128)S(1)}, bf16[320,2816]{1,0:T(8,128)(2,1)S(1)}, bf16[320,2816]{1,0:T(8,128)(2,1)S...) custom-call(bf16[1,12,24,256]{3,2,1,0:T(8,128)(2,1)S(1)} %bitcast.5,, ...), custom_call_target="tpu_custom_call" | custom-call | flops 5000000000 | bytes 5625856 | tf_op jit(solution)/shard_map/beside_rows/pallas_call | solution.py:585
  18.6 0.5 %collective-permute-done.2.second_ref = bf16[80,512]{1,0:T(8,128)(2,1)S(1)} collective-permute-done((bf16[80,512]{1,0:T(8,128)(2,1)S(1)}, bf16[80,512]{1,0:T(8,128)(2,1)S(1)}, u32[]{:S(2)}, u32[]{:S(2)}) %collective-permute-start.2) | collective-permute-done | bytes 81952 | tf_op jit(solution)/shard_map/ppermute | solution.py:655
  19.1 0.3 send_columns.1
  19.4 6.4 %collective-permute-start.3 = (bf16[112,512]{1,0:T(8,128)(2,1)S(1)}, bf16[112,512]{1,0:T(8,128)(2,1)S(1)}, u32[]{:S(2)}, u32[]{:S(2)}) collective-permute-start(bf16[112,512]{1,0:T(8,128)(2,1)S(1)} %get-tuple-element.46), channel_id=1, source_target_pairs={{0,30},{2,4},{4,2},{6,8},{8,6},{10,12},{12,10},{14,16},{16,14},{18... | collective-permute-start | bytes 344072 | tf_op jit(solution)/shard_map/ppermute | solution.py:674
  25.8 0.0 copy-start.8
  25.8 0.0 copy-start.10
  25.8 0.0 copy-start.12
  25.8 1.8 %beside_columns.1 = (bf16[48,512]{1,0:T(8,128)(2,1)S(1)}, bf16[48,512]{1,0:T(8,128)(2,1)S(1)}, f32[224,512]{1,0:T(8,128)S(1)}, f32[224,512]{1,0:T(8,128)S(1)}) custom-call(bf16[400,640]{1,0:T(8,128)(2,1)S(1)} %get-tuple-element.41.g_ref, bf16[80,512]{1,0:T(8,128)(2,1)S(1)} %collective-permute-done.1.first_ref, ...), custom_call_target="tpu_custom_call" | custom-call | flops 2000000000 | bytes 5182976 | tf_op jit(solution)/shard_map/beside_columns/pallas_call | solution.py:585
  27.6 1.2 %collective-permute-done.3.first_ref = bf16[112,512]{1,0:T(8,128)(2,1)S(1)} collective-permute-done((bf16[112,512]{1,0:T(8,128)(2,1)S(1)}, bf16[112,512]{1,0:T(8,128)(2,1)S(1)}, u32[]{:S(2)}, u32[]{:S(2)}) %collective-permute-start.3) | collective-permute-done | bytes 114720 | tf_op jit(solution)/shard_map/ppermute | solution.py:674
  28.7 1.8 %collective-permute-done.4.second_ref = bf16[112,512]{1,0:T(8,128)(2,1)S(1)} collective-permute-done((bf16[112,512]{1,0:T(8,128)(2,1)S(1)}, bf16[112,512]{1,0:T(8,128)(2,1)S(1)}, u32[]{:S(2)}, u32[]{:S(2)}) %collective-permute-start.4) | collective-permute-done | bytes 114720 | tf_op jit(solution)/shard_map/ppermute | solution.py:673
  30.6 6.0 %teacher_second.1 = (bf16[1,12,24,512]{3,2,1,0:T(8,128)(2,1)}, f32[1,12,24,256]{3,2,1,0:T(8,128)}) custom-call(bf16[320,512]{1,0:T(8,128)(2,1)S(1)} %get-tuple-element.39.hidden_ref.h_ref, bf16[400,640]{1,0:T(8,128)(2,1)S(1)} %get-tuple-element.41.g_ref, bf16[112,512]{1,0:T(8,128)(2,1)S(1)} %collective-permute-done.3.first_ref, ...), custom_call_target="tpu_custom_call" | custom-call | flops 6000000000 | bytes 12554752 | tf_op jit(solution)/shard_map/teacher_second/pallas_call | solution.py:585
  (22 shorter events, 0.1 us)
Async XLA Ops:
  0.6 2.9 %collective-permute-start = (bf16[1,12,24,512]{3,2,1,0:T(8,128)(2,1)}, bf16[1,12,24,512]{3,2,1,0:T(8,128)(2,1)S(1)}, u32[]{:S(2)}, u32[]{:S(2)}) collective-permute-start(bf16[1,12,24,512]{3,2,1,0:T(8,128)(2,1)} %bitcast.6), channel_id=1, source_target_pairs={{0,1},{1,0},{2,3},{3,2},{4,5},{5,4},{6,7},{7,6},{8,9},{9,8},{10,11... | collective-permute-start | bytes 884744 | tf_op jit(solution)/shard_map/ppermute | solution.py:630
  0.7 2.8 %copy-start.11 = (bf16[256,320]{1,0:T(8,128)(2,1)S(1)}, bf16[256,320]{1,0:T(8,128)(2,1)}, u32[]{:S(2)}) copy-start(bf16[256,320]{1,0:T(8,128)(2,1)} %constant.27.clone.rows_from_a) | copy-start | bytes 491524
  3.6 10.9 %copy-start = (bf16[2,512,1536]{2,1,0:T(8,128)(2,1)S(1)}, bf16[2,512,1536]{2,1,0:T(8,128)(2,1)}, u32[]{:S(2)}) copy-start(bf16[2,512,1536]{2,1,0:T(8,128)(2,1)} %t_qkv.7) | copy-start | bytes 9437188
  3.6 10.9 %copy-start.4 = (bf16[2,256,768]{2,1,0:T(8,128)(2,1)S(1)}, bf16[2,256,768]{2,1,0:T(8,128)(2,1)}, u32[]{:S(2)}) copy-start(bf16[2,256,768]{2,1,0:T(8,128)(2,1)} %s_qkv.3) | copy-start | bytes 2359300
  3.6 10.9 %copy-start.5 = (bf16[2,256,256]{2,1,0:T(8,128)(2,1)S(1)}, bf16[2,256,256]{2,1,0:T(8,128)(2,1)}, u32[]{:S(2)}) copy-start(bf16[2,256,256]{2,1,0:T(8,128)(2,1)} %s_out.3) | copy-start | bytes 786436
  3.6 10.9 %copy-start.6 = (bf16[256,512]{1,0:T(8,128)(2,1)S(1)}, bf16[256,512]{1,0:T(8,128)(2,1)}, u32[]{:S(2)}) copy-start(bf16[256,512]{1,0:T(8,128)(2,1)} %proj.3) | copy-start | bytes 786436
  3.6 10.9 %copy-start.7 = (bf16[1,24,12,256]{3,1,2,0:T(8,128)(2,1)S(1)}, bf16[1,24,12,256]{3,1,2,0:T(8,128)(2,1)}, u32[]{:S(2)}) copy-start(bf16[1,24,12,256]{3,1,2,0:T(8,128)(2,1)} %param.21) | copy-start | bytes 442372
  3.6 10.9 %copy-start.9 = (bf16[400,320]{1,0:T(8,128)(2,1)S(1)}, bf16[400,320]{1,0:T(8,128)(2,1)}, u32[]{:S(2)}) copy-start(bf16[400,320]{1,0:T(8,128)(2,1)} %constant.28.clone.a_to_g) | copy-start | bytes 768004
  3.6 10.9 %copy-start.13 = (bf16[128,112]{1,0:T(8,128)(2,1)S(1)}, bf16[128,112]{1,0:T(8,128)(2,1)}, u32[]{:S(2)}) copy-start(bf16[128,112]{1,0:T(8,128)(2,1)} %constant.29.clone.pack) | copy-start | bytes 86020
  7.3 11.3 %collective-permute-start.1 = (bf16[80,512]{1,0:T(8,128)(2,1)S(1)}, bf16[80,512]{1,0:T(8,128)(2,1)S(1)}, u32[]{:S(2)}, u32[]{:S(2)}) collective-permute-start(bf16[80,512]{1,0:T(8,128)(2,1)S(1)} %get-tuple-element.42), channel_id=1, source_target_pairs={{0,2},{2,0},{4,6},{6,4},{8,10},{10,8},{12,14},{14,12},{16,18},{18,... | collective-permute-start | bytes 245768 | tf_op jit(solution)/shard_map/ppermute | solution.py:656
  14.5 4.6 %collective-permute-start.2 = (bf16[80,512]{1,0:T(8,128)(2,1)S(1)}, bf16[80,512]{1,0:T(8,128)(2,1)S(1)}, u32[]{:S(2)}, u32[]{:S(2)}) collective-permute-start(bf16[80,512]{1,0:T(8,128)(2,1)S(1)} %get-tuple-element.40.after_ref), channel_id=1, source_target_pairs={{0,32},{32,0},{64,96},{96,64},{128,160},{160,128},{192,224},{224,1... | collective-permute-start | bytes 245768 | tf_op jit(solution)/shard_map/ppermute | solution.py:655
  14.6 4.5 %copy-start.1 = (bf16[256,80]{1,0:T(8,128)(2,1)S(1)}, bf16[256,80]{1,0:T(8,128)(2,1)}, u32[]{:S(2)}) copy-start(bf16[256,80]{1,0:T(8,128)(2,1)} %constant.31.clone.from_south) | copy-start | bytes 122884
  14.6 4.5 %copy-start.2 = (bf16[256,80]{1,0:T(8,128)(2,1)S(1)}, bf16[256,80]{1,0:T(8,128)(2,1)}, u32[]{:S(2)}) copy-start(bf16[256,80]{1,0:T(8,128)(2,1)} %constant.30.clone.from_north) | copy-start | bytes 122884
  14.6 11.2 %copy-start.14 = (bf16[112,80]{1,0:T(8,128)(2,1)S(1)}, bf16[112,80]{1,0:T(8,128)(2,1)}, u32[]{:S(2)}) copy-start(bf16[112,80]{1,0:T(8,128)(2,1)} %constant.32.clone.open_rows) | copy-start | bytes 53764
  19.4 9.4 %collective-permute-start.3 = (bf16[112,512]{1,0:T(8,128)(2,1)S(1)}, bf16[112,512]{1,0:T(8,128)(2,1)S(1)}, u32[]{:S(2)}, u32[]{:S(2)}) collective-permute-start(bf16[112,512]{1,0:T(8,128)(2,1)S(1)} %get-tuple-element.46), channel_id=1, source_target_pairs={{0,30},{2,4},{4,2},{6,8},{8,6},{10,12},{12,10},{14,16},{16,14},{18... | collective-permute-start | bytes 344072 | tf_op jit(solution)/shard_map/ppermute | solution.py:674
  25.7 4.8 %collective-permute-start.4 = (bf16[112,512]{1,0:T(8,128)(2,1)S(1)}, bf16[112,512]{1,0:T(8,128)(2,1)S(1)}, u32[]{:S(2)}, u32[]{:S(2)}) collective-permute-start(bf16[112,512]{1,0:T(8,128)(2,1)S(1)} %get-tuple-element.47.after_ref), channel_id=1, source_target_pairs={{0,2},{2,0},{4,6},{6,4},{8,10},{10,8},{12,14},{14,12},{16,18},{18,... | collective-permute-start | bytes 344072 | tf_op jit(solution)/shard_map/ppermute | solution.py:673
  25.7 4.8 %copy-start.3 = (bf16[2,512,512]{2,1,0:T(8,128)(2,1)S(1)}, bf16[2,512,512]{2,1,0:T(8,128)(2,1)}, u32[]{:S(2)}) copy-start(bf16[2,512,512]{2,1,0:T(8,128)(2,1)} %t_out.3) | copy-start | bytes 3145732
  25.8 4.8 %copy-start.8 = (bf16[320,400]{1,0:T(8,128)(2,1)S(1)}, bf16[320,400]{1,0:T(8,128)(2,1)}, u32[]{:S(2)}) copy-start(bf16[320,400]{1,0:T(8,128)(2,1)} %constant.35.clone.g_to_a) | copy-start | bytes 768004
  25.8 4.8 %copy-start.10 = (bf16[384,320]{1,0:T(8,128)(2,1)S(1)}, bf16[384,320]{1,0:T(8,128)(2,1)}, u32[]{:S(2)}) copy-start(bf16[384,320]{1,0:T(8,128)(2,1)} %constant.34.clone.from_a) | copy-start | bytes 737284
  25.8 4.8 %copy-start.12 = (bf16[176,112]{1,0:T(8,128)(2,1)S(1)}, bf16[176,112]{1,0:T(8,128)(2,1)}, u32[]{:S(2)}) copy-start(bf16[176,112]{1,0:T(8,128)(2,1)} %constant.33.clone.open_cols) | copy-start | bytes 118276
